TPU v7x, 256 devices: a whole 4x4x8 slice. The times are simulated.
256 devices in a mesh: own: 16 (over z, core), rep: 16 (over x, y).
Axes of the slice: x: 4, y: 4, z: 8, core: 2. Of those that a mesh axis runs over, the one named last changes fastest.
Arguments:
- histories: bfloat16 [8192, 64, 1024], P(('own', 'rep')), may hold values from -6 to 6
- lengths: int32 [8192], P(('own', 'rep')), may hold values from 1 to 64, as said below
- counts: int32 [4096], P(('own', 'rep')), may hold values from 0 to 2, as said below
- imp_user: int32 [65536], P(('own', 'rep')), may hold values from 0 to 511, as said below
- items: bfloat16 [65536, 1024], P(('own', 'rep')), may hold values from -0.8984375 to 0.8984375
- labels: int32 [65536], P(('own', 'rep')), may hold values 0 or 1
- w_uvqk: bfloat16 [1024, 2048], replicated, may hold values from -0.1875 to 0.1875
- w_out: bfloat16 [512, 1024], replicated, may hold values from -0.25 to 0.25
Outputs:
- logits: float32 [65536], P(('own', 'rep'))
- grad_out: bfloat16 [512, 1024], replicated
- grad_gate: bfloat16 [1024, 512], replicated
Inputs may be any that keep to these rules, and one draw needn't show every extreme that they name: `counts`: on every data replica one owner receives 2 live slots from every shard; on every replica the first shard along own sends the first owner at least one live slot, and the last shard along own sends the last owner exactly 2 live slots. `lengths`: every shard has a live slot of length 64. `imp_user`: each impression names a live slot held by a shard of its own data replica; on every replica the smallest and the largest index are named.
All inputs are finite; a program needn't handle non-finite values. No bound on the sum of `labels` on one device may be relied on, other than what follows from the above.
Results may differ from a plain program's by a relative error of at most 0.017.
Values may be sent and summed in bfloat16 or wider, within the bound.
A program may use at most 128 MiB of HBM per device.

v0:
```python
import jax
import jax.numpy as jnp
from jax import lax
from jax.sharding import PartitionSpec as P

D = 1024
HEADS = 4
HEAD = 128
HIST = 64


EPS_NORM = 1e-06
EPS_LAYER = 1e-05


def user_forward(block, spans, w_uvqk):
    width = HEADS * HEAD
    users = block.shape[0]
    feats = block.astype(jnp.float32)
    square = jnp.mean(feats * feats, -1, keepdims=True)
    normed = (feats * lax.rsqrt(square + EPS_NORM)).astype(jnp.bfloat16)
    linear = jnp.dot(normed.reshape(-1, D), w_uvqk, preferred_element_type=jnp.float32).reshape(
        users, HIST, 4 * width
    )
    active = jax.nn.silu(linear)
    gate_act = active[..., :width]
    values = active[..., width : 2 * width].astype(jnp.bfloat16).reshape(users, HIST, HEADS, HEAD)
    queries = (
        active[..., 2 * width : 3 * width].astype(jnp.bfloat16).reshape(users, HIST, HEADS, HEAD)
    )
    keyset = active[..., 3 * width :].astype(jnp.bfloat16).reshape(users, HIST, HEADS, HEAD)
    scores = jnp.einsum(
        "bqne,bkne->bnqk", queries, keyset, preferred_element_type=jnp.float32
    ) * HEAD ** (-0.5)
    places = jnp.arange(HIST, dtype=jnp.int32)
    allowed = (places[None, :] <= places[:, None])[None, :, :] & (
        places[None, None, :] < spans[:, None, None]
    )
    attn = (jax.nn.silu(scores) * allowed[:, None].astype(jnp.float32)).astype(jnp.bfloat16)
    attended = jnp.einsum(
        "bnqk,bkne->bqne", attn, values, preferred_element_type=jnp.float32
    ).reshape(users, HIST, width)
    center = jnp.mean(attended, -1, keepdims=True)
    spread = jnp.mean((attended - center) ** 2, -1, keepdims=True)
    normal_out = (attended - center) * lax.rsqrt(spread + EPS_LAYER)
    mixed = normal_out * gate_act
    validity = (places[None, :] < spans[:, None]).astype(jnp.float32)
    share = validity / jnp.maximum(spans, 1).astype(jnp.float32)[:, None]
    pooled_y = jnp.sum(mixed * share[..., None], 1).astype(jnp.bfloat16)
    pooled_x = jnp.sum(feats * share[..., None], 1)
    gate_in = linear[..., :width]
    sigmoid_gate = jax.nn.sigmoid(gate_in)
    slope = normal_out * (sigmoid_gate + gate_in * sigmoid_gate * (1.0 - sigmoid_gate))
    return (pooled_y, pooled_x, normed, slope, share)


def body(histories, lengths, counts, imp_user, items, labels, w_uvqk, w_out):
    width = HEADS * HEAD
    owners = lax.axis_size("own")
    slots = histories.shape[0]
    capacity = slots // owners
    ranks = jnp.arange(slots, dtype=jnp.int32)
    limits = jnp.repeat(counts, capacity)
    alive = ranks % capacity < limits
    effective = jnp.where(alive, lengths, 0)
    outgoing = histories.reshape(owners, capacity, HIST, D)
    out_spans = effective.reshape(owners, capacity).astype(jnp.bfloat16)
    blocks = lax.all_to_all(outgoing, "own", split_axis=0, concat_axis=0, tiled=True)
    span_grid = lax.all_to_all(out_spans, "own", split_axis=0, concat_axis=0, tiled=True)
    senders, taken = span_grid.shape
    results = user_forward(
        blocks.reshape(-1, HIST, D), span_grid.reshape(-1).astype(jnp.int32), w_uvqk
    )
    pooled_y, pooled_x, normed, slope, share = tuple(
        (entry.reshape((senders, taken) + entry.shape[1:]) for entry in results)
    )
    pooled_y = pooled_y.reshape(slots, width)
    pooled_x = pooled_x.reshape(slots, D)
    normed = normed.reshape(-1, D)
    slope = slope.reshape(slots, HIST, width)
    share = share.reshape(slots, HIST)
    embeds = (pooled_x + jnp.dot(pooled_y, w_out, preferred_element_type=jnp.float32)).astype(
        jnp.bfloat16
    )
    piece = lax.all_gather(embeds, "own", axis=0, tiled=True)
    columns = jnp.arange(piece.shape[0], dtype=jnp.int32)
    select = (imp_user[:, None] == columns[None, :]).astype(jnp.bfloat16)
    user_rows = jnp.dot(select, piece, preferred_element_type=jnp.float32)
    logits = jnp.sum(user_rows * items.astype(jnp.float32), -1)
    weighted = (jax.nn.sigmoid(logits) - labels.astype(jnp.float32))[:, None] * items.astype(
        jnp.float32
    )
    rows = jnp.arange(lax.axis_size("own") * slots, dtype=jnp.int32)
    select = (rows[:, None] == imp_user[None, :]).astype(jnp.float32)
    grad_embed = lax.psum_scatter(
        jnp.dot(select, weighted, precision=lax.Precision.HIGHEST),
        "own",
        scatter_dimension=0,
        tiled=True,
    ).astype(jnp.bfloat16)
    out_term = lax.dot_general(
        pooled_y, grad_embed, (((0,), (0,)), ((), ())), preferred_element_type=jnp.float32
    )
    grad_pool = lax.dot_general(
        grad_embed, w_out, (((1,), (1,)), ((), ())), preferred_element_type=jnp.float32
    ).astype(jnp.bfloat16)
    grad_pre = (share[..., None] * grad_pool[:, None, :].astype(jnp.float32) * slope).astype(
        jnp.bfloat16
    )
    gate_term = lax.dot_general(
        normed,
        grad_pre.reshape(-1, width),
        (((0,), (0,)), ((), ())),
        preferred_element_type=jnp.float32,
    )
    out_sum, gate_sum = lax.psum((out_term, gate_term), ("own", "rep"))
    return (logits, out_sum.astype(jnp.bfloat16), gate_sum.astype(jnp.bfloat16))


def solution(mesh):
    return jax.shard_map(
        body,
        mesh=mesh,
        in_specs=(
            P(("own", "rep"), None, None),
            P(("own", "rep")),
            P(("own", "rep")),
            P(("own", "rep")),
            P(("own", "rep"), None),
            P(("own", "rep")),
            P(),
            P(),
        ),
        out_specs=(P(("own", "rep")), P(), P()),
        check_vma=False,
    )
```

profile of v0, /device:TPU:1, one launch (start us, length us, event | category | flops | bytes accessed | tf_op | source)
XLA Modules:
  0.0 422.6 jit_solution(10973036580861680031)
XLA Ops:
  7.2 0.8 broadcast_in_dim.4
  8.1 0.7 fusion.34
  8.8 16.8 %all_to_all.11 = bf16[16,1,2]{2,1,0:T(2,128)(2,1)S(1)} all-to-all(bf16[16,1,2]{2,1,0:T(2,128)(2,1)S(1)} %convert_element_type.151), channel_id=1, replica_groups=mesh['own'=16,'rep'=16] {'own'}, dimensions={0} | all-to-all | bytes 128 | tf_op jit(solution)/shard_map/all_to_all | solution.py:69
  25.6 4.9 %all-to-all-start = ((bf16[16,2,64,1024]{3,2,1,0:T(8,128)(2,1)}), bf16[16,2,64,1024]{3,2,1,0:T(8,128)(2,1)}, u32[]{:S(2)}, u32[]{:S(2)}) async-start(bf16[16,2,64,1024]{3,2,1,0:T(8,128)(2,1)} %bitcast.71), calls=%async_computation | async-start | bytes 8388608 | tf_op jit(solution)/shard_map/all_to_all | solution.py:68
  31.2 0.1 fusion.31
  31.3 1.1 and_convert_fusion
  32.4 91.9 %all-to-all-done = bf16[16,2,64,1024]{3,2,1,0:T(8,128)(2,1)} async-done(((bf16[16,2,64,1024]{3,2,1,0:T(8,128)(2,1)}), bf16[16,2,64,1024]{3,2,1,0:T(8,128)(2,1)}, u32[]{:S(2)}, u32[]{:S(2)}) %all-to-all-start) | async-done | bytes 4194336 | tf_op jit(solution)/shard_map/all_to_all | solution.py:68
  124.2 3.5 multiply_reduce_fusion
  127.8 4.8 %fusion = bf16[32,64,1024]{2,1,0:T(8,128)(2,1)} fusion(f32[32,64]{1,0:T(8,128)S(1)} %bitcast.72, bf16[16,2,64,1024]{3,2,1,0:T(8,128)(2,1)} %all-to-all-done), kind=kLoop, calls=%fused_computation.2 | loop fusion | flops 6291456 | bytes 8396800 | tf_op jit(solution)/shard_map/convert_element_type | solution.py:21
  132.6 21.6 %fusion.38 = (bf16[32,64,2048]{2,1,0:T(8,128)(2,1)}, f32[32,64,2048]{2,1,0:T(8,128)}, f32[32,64,2048]{2,1,0:T(8,128)}) fusion(bf16[32,64,1024]{2,1,0:T(8,128)(2,1)} %fusion, bf16[1024,2048]{1,0:T(8,128)(2,1)} %param.14), kind=kOutput, calls=%fused_computation.67 | convolution fusion | flops 8610906112 | bytes 50331648 | tf_op jit(solution)/shard_map/dot_general | solution.py:22
  154.2 6.6 %slice_bitcast_fusion.2 = (bf16[32,8,4,8,128]{4,3,2,1,0:T(8,128)(2,1)S(1)}, bf16[32,8,4,8,128]{4,3,2,1,0:T(8,128)(2,1)}, bf16[32,8,4,8,128]{4,3,2,1,0:T(8,128)(2,1)}) fusion(bf16[32,64,2048]{2,1,0:T(8,128)(2,1)} %get-tuple-element.7), kind=kLoop, calls=%fused_computation.27 | loop fusion | bytes 12582912
  160.8 6.6 %bitcast_reduce_fusion = (f32[32,64]{1,0:T(8,128)S(1)}, f32[32,4,128,64]{2,3,1,0:T(8,128)}) fusion(bf16[32,8,4,8,128]{4,3,2,1,0:T(8,128)(2,1)} %get-tuple-element.11, bf16[32,8,4,8,128]{4,3,2,1,0:T(8,128)(2,1)} %get-tuple-element.10, bf16[32,8,4,8,128]{4,3,2,1,0:T(8,128)(2,1)S(1)} %get-tuple-element.9, f32[32,64,64]{2,1,0:T(8,128)} %and_convert_fusion), kind=kOutput, calls=%fused_computation.10 | convolution fusion | flops 273152000 | bytes 11018240 | tf_op jit(solution)/shard_map/bnqk,bkne->bqne/dot_general | solution.py:40
  167.4 2.9 fusion.5
  170.5 4.1 fusion.3
  174.7 0.9 fusion.22
  175.6 0.2 reduce-scatter.2.cloned.1.call-start
  175.8 38.2 %all-gather.2.cloned.1.call-done = bf16[512,1024]{1,0:T(8,128)(2,1)} async-done(((bf16[32,1024]{1,0:T(8,128)(2,1)}), bf16[512,1024]{1,0:T(8,128)(2,1)}) %all-gather.2.cloned.1.call-update) | async-done | bytes 1048592 | tf_op jit(solution)/shard_map/all_gather | solution.py:85
  214.1 1.8 fusion.21
  215.9 2.6 fusion.24
  218.5 54.8 %reduce-scatter.2.cloned.1.call-done = f32[32,1024]{1,0:T(8,128)} async-done(((f32[512,1024]{1,0:T(8,128)}), f32[32,1024]{1,0:T(8,128)}) %reduce-scatter.2.cloned.1.call-update) | async-done | bytes 131088 | tf_op jit(solution)/shard_map/reduce_scatter | solution.py:95
  273.3 1.3 fusion.23
  274.6 9.3 %fusion.16 = f32[1024,512]{1,0:T(8,128)} fusion(bf16[32,64,1024]{2,1,0:T(8,128)(2,1)} %fusion, f32[32,64,2048]{2,1,0:T(8,128)} %get-tuple-element.12, f32[32,512]{1,0:T(8,128)S(1)} %fusion.23, f32[32,64]{1,0:T(8,128)S(1)} %convert_divide_fusion, f32[32,64]{1,0:T(8,128)S(1)} %add_rsqrt_fusion, f32[32,64]{1,0:T(8,128)S(1)} %broadcast_multiply_fusion, ...), kind=kOutput, calls=%fused_computation.29 | convolution fusion | flops 2161115136 | bytes 14770176 | tf_op jit(solution)/shard_map/dot_general | solution.py:110
  283.9 0.4 fusion.29
  284.3 131.5 %all-reduce.2 = (bf16[512,1024]{1,0:T(8,128)(2,1)}, bf16[1024,512]{1,0:T(8,128)(2,1)}) all-reduce(f32[512,1024]{1,0:T(8,128)S(1)} %fusion.29, f32[1024,512]{1,0:T(8,128)} %fusion.16), channel_id=1, replica_groups=mesh['own'=16,'rep'=16] {'own','rep'}, use_global_device_ids=true, to_apply=%region_7.8 | all-reduce | flops 1048576 | bytes 6291456 | tf_op jit(solution)/shard_map/psum | solution.py:116
  (33 shorter events, 1.0 us)
Async XLA Ops:
  7.2 167.5 %copy-start = (bf16[512,1024]{1,0:T(8,128)(2,1)S(1)}, bf16[512,1024]{1,0:T(8,128)(2,1)}, u32[]{:S(2)}) copy-start(bf16[512,1024]{1,0:T(8,128)(2,1)} %param.15) | copy-start | bytes 3145732
  25.6 98.6 %all-to-all-start = ((bf16[16,2,64,1024]{3,2,1,0:T(8,128)(2,1)}), bf16[16,2,64,1024]{3,2,1,0:T(8,128)(2,1)}, u32[]{:S(2)}, u32[]{:S(2)}) async-start(bf16[16,2,64,1024]{3,2,1,0:T(8,128)(2,1)} %bitcast.71), calls=%async_computation | async-start | bytes 8388608 | tf_op jit(solution)/shard_map/all_to_all | solution.py:68
  30.6 183.5 %all-gather.2.cloned.1.call-start = ((), (), s32[]{:S(2)}) async-start(), calls=%async_computation.3 | async-start | bytes 1114112 | tf_op jit(solution)/shard_map/all_gather | solution.py:85
  170.5 43.6 %copy-start.2 = (bf16[256,1024]{1,0:T(8,128)(2,1)S(1)}, bf16[256,1024]{1,0:T(8,128)(2,1)}, u32[]{:S(2)}) copy-start(bf16[256,1024]{1,0:T(8,128)(2,1)} %param.12) | copy-start | bytes 1572868
  170.5 43.6 %copy-start.3 = (s32[256]{0:T(256)S(1)}, s32[256]{0:T(256)}, u32[]{:S(2)}) copy-start(s32[256]{0:T(256)} %param.11) | copy-start | bytes 3076
  170.5 45.3 %copy-start.4 = (s32[256]{0:T(256)S(1)}, s32[256]{0:T(256)}, u32[]{:S(2)}) copy-start(s32[256]{0:T(256)} %param.13) | copy-start | bytes 3076
  175.6 97.6 %reduce-scatter.2.cloned.1.call-start = ((), (), s32[]{:S(2)}) async-start(), calls=%async_computation.4 | async-start | bytes 2228224 | tf_op jit(solution)/shard_map/reduce_scatter | solution.py:95
  215.8 68.0 %copy-start.5 = (f32[256]{0:T(256)}, f32[256]{0:T(256)S(1)}, u32[]{:S(2)}) copy-start(f32[256]{0:T(256)S(1)} %fusion.21) | copy-start | bytes 3076
  274.6 9.3 %copy-start.1 = (f32[32,1024]{1,0:T(8,128)S(1)}, f32[32,1024]{1,0:T(8,128)}, u32[]{:S(2)}) copy-start(f32[32,1024]{1,0:T(8,128)} %reduce-scatter.2.cloned.1.call-done) | copy-start | bytes 393220
Sparse Core Ops, SparseCore 0:
  175.7 38.2 all-gather.1
  218.6 54.6 reduce-scatter.1
where the time goes:
time: 424 us; the launch traced here: 423 us
  waiting for transfers between devices  185 us (44%)
  blocking collectives  148 us (35%)
  matrix products  44.5 us (10%)
  other arithmetic  17.5 us (4%)
  between operations  14.2 us (3%)
  local copies, waits for them, and re-layouts  8.06 us (2%)
  starting transfers between devices  5.18 us (1%)
    psum x1, blocking collectives, body(): out_sum, gate_sum = lax.psum((out_term, gate_term), ('own', 'rep'))  131 us
    all_to_all x1, waiting for transfers between devices, body(): lax.all_to_all(outgoing, 'own', split_axis=0, concat_axis=0, tiled=True)  91.9 us
    reduce_scatter x1, waiting for transfers between devices, body(): lax.psum_scatter(jnp.dot(select, weighted, precision=lax.Precision.HIGHES...  54.8 us
    all_gather x1, waiting for transfers between devices, body(): piece = lax.all_gather(embeds, 'own', axis=0, tiled=True)  38.2 us
    dot_general x1, matrix products, user_forward(): jnp.dot(normed.reshape(-1, D), w_uvqk, preferred_element_type=jnp.float32)  21.6 us
    all_to_all x1, blocking collectives, body(): lax.all_to_all(out_spans, 'own', split_axis=0, concat_axis=0, tiled=True)  16.8 us
    dot_general x1, matrix products, body(): lax.dot_general(normed, grad_pre.reshape(-1, width), (((0,), (0,)), ((),...  9.26 us
  transfers between devices with their start and end apart: 3, of which 3 were waited for; matrix products, arithmetic and copies ran while one was open for 0% of the time, Pallas kernels for 0%

commit v1 on v0

v1 whole, which is shorter than its diff:
```python
import jax
import jax.numpy as jnp
from jax import lax
from jax.experimental import pallas as pl
from jax.experimental.pallas import tpu as pltpu
from jax.sharding import PartitionSpec as P

D = 1024
HEADS = 4
HEAD = 128
HIST = 64
WIDTH = HEADS * HEAD
GROUP = 8
PAIR = 2 * HIST

EPS_NORM = 1e-06
EPS_LAYER = 1e-05


def sigmoid(v):
    return 0.5 * jnp.tanh(0.5 * v) + 0.5


def forward_kernel(spans, col_ref, h_ref, w_ref, px_ref, py_ref, slope_ref, lin):
    group = pl.program_id(0)
    tokens = GROUP * HIST
    x = h_ref[...].reshape(tokens, D)
    lin[...] = jnp.dot(x, w_ref[...], preferred_element_type=jnp.float32)
    span_col = col_ref[...]
    slot = lax.broadcasted_iota(jnp.int32, (GROUP, tokens), 0)
    place = lax.broadcasted_iota(jnp.int32, (GROUP, tokens), 1) - slot * HIST
    live = (place >= 0) & (place < span_col)
    inverse = 1.0 / jnp.maximum(span_col, 1).astype(jnp.float32)
    px_ref[...] = jnp.dot(live.astype(jnp.bfloat16), x, preferred_element_type=jnp.float32) * inverse

    def pair_step(p):
        rows = slice(p * PAIR, (p + 1) * PAIR)
        first = spans[group * GROUP + 2 * p]
        second = spans[group * GROUP + 2 * p + 1]
        feats = h_ref[2 * p : 2 * p + 2].reshape(PAIR, D).astype(jnp.float32)
        scale = lax.rsqrt(jnp.mean(feats * feats, -1, keepdims=True) + EPS_NORM)
        row = lax.broadcasted_iota(jnp.int32, (PAIR, PAIR), 0)
        col = lax.broadcasted_iota(jnp.int32, (PAIR, PAIR), 1)
        allowed = (
            (col <= row)
            & ((row < HIST) | (col >= HIST))
            & (col < jnp.where(col < HIST, first, HIST + second))
        )
        attended = []
        for h in range(HEADS):
            cols = [slice(k * WIDTH + h * HEAD, k * WIDTH + (h + 1) * HEAD) for k in (1, 2, 3)]
            raw = [lin[rows, c] * scale for c in cols]
            value, query, key = [(v * sigmoid(v)).astype(jnp.bfloat16) for v in raw]
            scores = lax.dot_general(
                query, key, (((1,), (1,)), ((), ())), preferred_element_type=jnp.float32
            ) * HEAD ** (-0.5)
            attn = jnp.where(allowed, scores * sigmoid(scores), 0.0).astype(jnp.bfloat16)
            attended.append(jnp.dot(attn, value, preferred_element_type=jnp.float32))
        center = sum(jnp.sum(a, -1, keepdims=True) for a in attended) / WIDTH
        moved = [a - center for a in attended]
        spread = sum(jnp.sum(a * a, -1, keepdims=True) for a in moved) / WIDTH
        norm = lax.rsqrt(spread + EPS_LAYER)
        spot = lax.broadcasted_iota(jnp.int32, (PAIR, 1), 0)
        valid = spot < jnp.where(spot < HIST, first, HIST + second)
        both = jnp.where(spot < HIST, first, second)
        share = jnp.where(valid, 1.0 / jnp.maximum(both, 1).astype(jnp.float32), 0.0)
        back = share * scale
        for h in range(HEADS):
            gate = lin[rows, h * HEAD : (h + 1) * HEAD] * scale
            sig = sigmoid(gate)
            act = gate * sig
            normal = moved[h] * norm
            mixed = normal * act * share
            for k in range(2):
                pooled = jnp.sum(mixed[k * HIST : (k + 1) * HIST], 0, keepdims=True)
                py_ref[2 * p + k : 2 * p + k + 1, h * HEAD : (h + 1) * HEAD] = pooled
            slope = back * normal * (sig + act * (1.0 - sig))
            slope_ref[h * HEAD : (h + 1) * HEAD, rows] = slope.T.astype(jnp.bfloat16)

    for p in range(GROUP // 2):
        pair_step(p)


def forward(histories, spans, w_uvqk):
    slots = histories.shape[0]
    steps = slots // GROUP
    return pl.pallas_call(
        forward_kernel,
        grid_spec=pltpu.PrefetchScalarGridSpec(
            num_scalar_prefetch=1,
            grid=(steps,),
            in_specs=[
                pl.BlockSpec((GROUP, 1), lambda i, s: (i, 0)),
                pl.BlockSpec((GROUP, HIST, D), lambda i, s: (i, 0, 0)),
                pl.BlockSpec((D, 4 * WIDTH), lambda i, s: (0, 0)),
            ],
            out_specs=[
                pl.BlockSpec((GROUP, D), lambda i, s: (i, 0)),
                pl.BlockSpec((GROUP, WIDTH), lambda i, s: (i, 0)),
                pl.BlockSpec((WIDTH, GROUP * HIST), lambda i, s: (0, i)),
            ],
            scratch_shapes=[pltpu.VMEM((GROUP * HIST, 4 * WIDTH), jnp.float32)],
        ),
        out_shape=[
            jax.ShapeDtypeStruct((slots, D), jnp.float32),
            jax.ShapeDtypeStruct((slots, WIDTH), jnp.float32),
            jax.ShapeDtypeStruct((WIDTH, slots * HIST), jnp.bfloat16),
        ],
        compiler_params=pltpu.CompilerParams(vmem_limit_bytes=48 * 1024 * 1024),
        name="forward",
    )(spans, spans[:, None], histories, w_uvqk)


def body(histories, lengths, counts, imp_user, items, labels, w_uvqk, w_out):
    slots = histories.shape[0]
    owners = lax.axis_size("own")
    capacity = slots // owners
    ranks = jnp.arange(slots, dtype=jnp.int32)
    alive = ranks % capacity < jnp.repeat(counts, capacity)
    spans = jnp.where(alive, lengths, 0)
    px, py, slope = forward(histories, spans, w_uvqk)
    px_all = lax.all_gather(px.astype(jnp.bfloat16), "own", axis=0, tiled=True)
    py_all = lax.all_gather(py.astype(jnp.bfloat16), "own", axis=0, tiled=True)
    place = (imp_user % slots) // capacity * slots + imp_user // slots * capacity + imp_user % capacity
    columns = jnp.arange(owners * slots, dtype=jnp.int32)
    select = place[:, None] == columns[None, :]
    item_w = lax.dot_general(items, w_out, (((1,), (1,)), ((), ())), preferred_element_type=jnp.float32)
    table = lax.dot_general(
        items, px_all, (((1,), (1,)), ((), ())), preferred_element_type=jnp.float32
    ) + lax.dot_general(
        item_w.astype(jnp.bfloat16), py_all, (((1,), (1,)), ((), ())), preferred_element_type=jnp.float32
    )
    logits = jnp.sum(jnp.where(select, table, 0.0), -1)
    error = (jax.nn.sigmoid(logits) - labels.astype(jnp.float32))[:, None]
    pick = select.astype(jnp.bfloat16)
    pool_part = lax.dot_general(
        pick, (error * item_w).astype(jnp.bfloat16), (((0,), (0,)), ((), ())), preferred_element_type=jnp.float32
    )
    pool = lax.psum_scatter(pool_part.astype(jnp.bfloat16), "own", scatter_dimension=0, tiled=True)
    rows = jnp.dot(pick, py_all, preferred_element_type=jnp.float32).astype(jnp.bfloat16)
    out_term = lax.dot_general(
        rows, (error * items.astype(jnp.float32)).astype(jnp.bfloat16), (((0,), (0,)), ((), ())),
        preferred_element_type=jnp.float32,
    )
    spread = jnp.repeat(pool.T.astype(jnp.float32), HIST, axis=1)
    grad_pre = (spread * slope.astype(jnp.float32)).astype(jnp.bfloat16)
    gate_term = jnp.dot(grad_pre, histories.reshape(-1, D), preferred_element_type=jnp.float32)
    out_sum, gate_sum = lax.psum(
        (out_term.astype(jnp.bfloat16), gate_term.astype(jnp.bfloat16)), ("own", "rep")
    )
    return (logits, out_sum, gate_sum.T)


def solution(mesh):
    return jax.shard_map(
        body,
        mesh=mesh,
        in_specs=(
            P(("own", "rep"), None, None),
            P(("own", "rep")),
            P(("own", "rep")),
            P(("own", "rep")),
            P(("own", "rep"), None),
            P(("own", "rep")),
            P(),
            P(),
        ),
        out_specs=(P(("own", "rep")), P(), P()),
        check_vma=False,
    )
```

time: 424 us -> 424 us (level)
  waiting for transfers between devices: 185 us -> 327 us
  blocking collectives: 148 us -> 23.3 us
  matrix products: 44.5 us -> 16.8 us
  Pallas kernels: 0 us -> 25.8 us
  other arithmetic: 17.5 us -> 2.09 us
  local copies, waits for them, and re-layouts: 8.06 us -> 14.2 us
  starting transfers between devices: 5.18 us -> 0.12 us
    psum x0 -> x1, waiting for transfers between devices: none -> 262 us  [body(): lax.psum((out_term.astype(jnp.bfloat16), gate_term.astype(jnp.bfloat16)),...]
    psum x1 -> x0, blocking collectives: 131 us -> none  [body(): out_sum, gate_sum = lax.psum((out_term, gate_term), ('own', 'rep'))]
    all_to_all x1 -> x0, waiting for transfers between devices: 91.9 us -> none  [body(): lax.all_to_all(outgoing, 'own', split_axis=0, concat_axis=0, tiled=True)]
    dot_general x8 -> x6, matrix products: 44.5 us -> 16.8 us  [the longest x1 6.77 us: body(): jnp.dot(grad_pre, histories.reshape(-1, D), preferred_element_type=jnp.fl...]
    pallas_call x0 -> x1, Pallas kernels: none -> 25.8 us  [forward(): pl.pallas_call(forward_kernel, grid_spec=pltpu.PrefetchScalarGridSpec(num...]
    all_gather x0 -> x1, blocking collectives: none -> 23.3 us  [body(): py_all = lax.all_gather(py.astype(jnp.bfloat16), 'own', axis=0, tiled=True)]
    all_gather x1, waiting for transfers between devices: 38.2 us -> 15.9 us  [body(): px_all = lax.all_gather(px.astype(jnp.bfloat16), 'own', axis=0, tiled=True)]
    all_to_all x1 -> x0, blocking collectives: 16.8 us -> none  [body(): lax.all_to_all(out_spans, 'own', split_axis=0, concat_axis=0, tiled=True)]
  transfers between devices with their start and end apart: 3 -> 3, of which waited for: 3 -> 3; matrix products, arithmetic and copies ran while one was open for 0% -> 1% of each run, Pallas kernels for 0% -> 0%
where the time goes in v1:
time: 424 us; the launch traced here: 423 us
  waiting for transfers between devices  327 us (77%)
  Pallas kernels  25.8 us (6%)
  blocking collectives  23.3 us (5%)
  matrix products  16.8 us (4%)
  local copies, waits for them, and re-layouts  14.2 us (3%)
  between operations  13.9 us (3%)
    psum x1, waiting for transfers between devices, body(): lax.psum((out_term.astype(jnp.bfloat16), gate_term.astype(jnp.bfloat16)),...  262 us
    reduce_scatter x1, waiting for transfers between devices, body(): lax.psum_scatter(pool_part.astype(jnp.bfloat16), 'own', scatter_dimension...  49 us
    pallas_call x1, Pallas kernels, forward(): pl.pallas_call(forward_kernel, grid_spec=pltpu.PrefetchScalarGridSpec(num...  25.8 us
    all_gather x1, blocking collectives, body(): py_all = lax.all_gather(py.astype(jnp.bfloat16), 'own', axis=0, tiled=True)  23.3 us
    all_gather x1, waiting for transfers between devices, body(): px_all = lax.all_gather(px.astype(jnp.bfloat16), 'own', axis=0, tiled=True)  15.9 us
  transfers between devices with their start and end apart: 3, of which 3 were waited for; matrix products, arithmetic and copies ran while one was open for 1% of the time, Pallas kernels for 0%

profile of v1, /device:TPU:1, one launch (start us, length us, event | category | flops | bytes accessed | tf_op | source)
XLA Modules:
  0.0 422.9 jit_solution(13646857276939953123)
XLA Ops:
  7.2 0.8 broadcast_in_dim.18
  8.0 0.1 reshape.17
  8.1 0.7 compare_select_fusion.spans
  8.8 0.1 copy.15.col_ref
  8.9 25.8 %forward.1 = (f32[32,1024]{1,0:T(8,128)S(1)}, f32[32,512]{1,0:T(8,128)S(1)}, bf16[512,2048]{1,0:T(8,128)(2,1)S(1)}) custom-call(s32[32]{0:T(128)S(1)} %compare_select_fusion.spans, s32[32,1]{1,0:T(8,128)S(1)} %copy.15.col_ref, bf16[32,64,1024]{2,1,0:T(8,128)(2,1)} %h_ref.1, bf16[1024,2048]{1,0:T(8,128)(2,1)} %w_ref.1), custom_call_target="tpu_custom_call" | custom-call | tf_op jit(solution)/shard_map/forward/pallas_call | solution.py:87
  34.7 0.6 convert_element_type.46
  35.4 0.0 reduce-scatter.2.cloned.1.call-start
  35.5 23.3 %all_gather.7 = bf16[512,512]{1,0:T(8,128)(2,1)S(1)} all-gather(bf16[32,512]{1,0:T(8,128)(2,1)S(1)} %convert_element_type.48), channel_id=1, replica_groups=mesh['own'=16,'rep'=16] {'own'}, dimensions={0}, use_global_device_ids=true | all-gather | bytes 557056 | tf_op jit(solution)/shard_map/all_gather | solution.py:123
  58.8 1.7 fusion.14
  60.5 0.8 copy-done.1
  61.3 1.1 fusion.8
  62.4 15.9 %all-gather.2.cloned.1.call-done = bf16[512,1024]{1,0:T(8,128)(2,1)} async-done(((bf16[32,1024]{1,0:T(8,128)(2,1)}), bf16[512,1024]{1,0:T(8,128)(2,1)}) %all-gather.2.cloned.1.call-update) | async-done | bytes 1048592 | tf_op jit(solution)/shard_map/all_gather | solution.py:122
  78.4 2.0 fusion.5
  80.4 2.2 convolution_convert_fusion.1
  82.7 0.0 all-reduce.3.cloned.1.call-start
  82.7 3.0 convolution_convert_fusion
  85.8 49.0 %reduce-scatter.2.cloned.1.call-done = bf16[32,512]{1,0:T(8,128)(2,1)} async-done(((bf16[512,512]{1,0:T(8,128)(2,1)}), bf16[32,512]{1,0:T(8,128)(2,1)}) %reduce-scatter.2.cloned.1.call-update) | async-done | bytes 32784 | tf_op jit(solution)/shard_map/reduce_scatter | solution.py:139
  134.7 0.8 convert_bitcast_fusion
  135.5 2.5 broadcast_in_dim.21
  138.0 5.4 %copy.17 = f32[512,2048]{1,0:T(8,128)} copy(f32[512,2048]{0,1:T(8,128)} %bitcast.23) | data formatting | bytes 8388608 | tf_op jit(solution)/shard_map/reshape | solution.py:145
  143.4 6.8 %fusion.2 = bf16[1024,512]{0,1:T(8,128)(2,1)} fusion(bf16[2048,1024]{1,0:T(8,128)(2,1)} %bitcast.24, f32[512,2048]{1,0:T(8,128)} %copy.17, bf16[512,2048]{1,0:T(8,128)(2,1)S(1)} %get-tuple-element.8), kind=kOutput, calls=%fused_computation.4 | convolution fusion | flops 2151153664 | bytes 11534336 | tf_op jit(solution)/shard_map/dot_general | solution.py:147
  150.2 261.6 %all-reduce.3.cloned.1.call-done = (bf16[512,1024]{1,0:T(8,128)(2,1)}, bf16[1024,512]{0,1:T(8,128)(2,1)}) async-done(((bf16[512,1024]{1,0:T(8,128)(2,1)}, bf16[1024,512]{0,1:T(8,128)(2,1)}), (bf16[512,1024]{1,0:T(8,128)(2,1)}, bf16[1024,512]{0,1:T(8,128)(2,1)})) %all-reduce.3.cloned.1.call-update) | async-done | bytes 2097168 | tf_op jit(solution)/shard_map/psum | solution.py:148
  411.8 2.3 copy.18
  414.1 2.3 copy.22
  (18 shorter events, 0.2 us)
Async XLA Ops:
  7.2 51.6 %copy-start = (bf16[512,1024]{1,0:T(8,128)(2,1)S(1)}, bf16[512,1024]{1,0:T(8,128)(2,1)}, u32[]{:S(2)}) copy-start(bf16[512,1024]{1,0:T(8,128)(2,1)} %param.15) | copy-start | bytes 3145732
  7.2 71.2 %all-gather.2.cloned.1.call-start = ((), (), s32[]{:S(2)}) async-start(), calls=%async_computation.1 | async-start | bytes 1114112 | tf_op jit(solution)/shard_map/all_gather | solution.py:122
  8.9 26.6 %copy-start.5 = (s32[256]{0:T(256)S(1)}, s32[256]{0:T(256)}, u32[]{:S(2)}) copy-start(s32[256]{0:T(256)} %param.11) | copy-start | bytes 3076
  34.7 45.7 %copy-start.3 = (s32[256]{0:T(256)S(1)}, s32[256]{0:T(256)}, u32[]{:S(2)}) copy-start(s32[256]{0:T(256)} %param.13) | copy-start | bytes 3076
  35.4 99.3 %reduce-scatter.2.cloned.1.call-start = ((), (), s32[]{:S(2)}) async-start(), calls=%async_computation.2 | async-start | bytes 557056 | tf_op jit(solution)/shard_map/reduce_scatter | solution.py:139
  58.8 1.7 copy-start.2
  60.5 0.8 copy-start.1
  80.4 63.0 %copy-start.4 = (f32[256]{0:T(256)}, f32[256]{0:T(256)S(1)}, u32[]{:S(2)}) copy-start(f32[256]{0:T(256)S(1)} %fusion.5) | copy-start | bytes 3076
  82.7 329.1 %all-reduce.3.cloned.1.call-start = ((), (), s32[]{:S(2)}) async-start(), calls=%async_computation.3 | async-start | bytes 4194304 | tf_op jit(solution)/shard_map/psum | solution.py:148
Sparse Core Ops, SparseCore 0:
  35.5 42.8 all-gather.1
  82.8 51.8 reduce-scatter.1
  150.3 261.4 all-reduce.2

commit v2 on v1

--- a/solution.py
+++ b/solution.py
@@ -1,3 +1,5 @@
+import functools
+
 import jax
 import jax.numpy as jnp
 from jax import lax
@@ -12,6 +14,10 @@
 WIDTH = HEADS * HEAD
 GROUP = 8
 PAIR = 2 * HIST
+CORES = 2
+TILE = 16
+LANES = 128
+MESH = pl.DeviceIdType.MESH
 
 EPS_NORM = 1e-06
 EPS_LAYER = 1e-05
@@ -111,44 +117,367 @@
     )(spans, spans[:, None], histories, w_uvqk)
 
 
+def dot(a, b):
+    return jnp.dot(a, b, preferred_element_type=jnp.float32)
+
+
+def dot_t(a, b):
+    return lax.dot_general(a, b, (((1,), (1,)), ((), ())), preferred_element_type=jnp.float32)
+
+
+def exchange_kernel(
+    nz, nr, user_ref, label_ref, px_ref, py_ref, items_hbm, w_hbm, slope_hbm, hist_hbm,
+    logit_ref, out_ref, gate_ref,
+    items, w_out, slope, hist, users, pool_send, pool_core, pool_mine, pool_z, pool_got,
+    pre, mine, core_send, core_got, half, plane_got, row_sum, piece_got,
+    load_sem, user_send, user_recv, relay_send, relay_recv, pcore_sem, pz_send, pz_recv,
+    core_sem, plane_send, plane_recv, piece_send, piece_recv, back_send, back_recv,
+    wide_send, wide_recv, last_send, last_recv,
+):
+    own = lax.axis_index("own")
+    rep = lax.axis_index("rep")
+    z, c = own // CORES, own % CORES
+    other = 1 - c
+    slots = px_ref.shape[0]
+    side = nz * slots
+    block = WIDTH // nr
+    half_w = D // CORES
+    grads = (out_ref, gate_ref)
+
+    loads = [
+        pltpu.make_async_copy(source, target, load_sem.at[k])
+        for k, (source, target) in enumerate(
+            ((items_hbm, items), (w_hbm, w_out), (slope_hbm, slope), (hist_hbm, hist))
+        )
+    ]
+    for load in loads:
+        load.start()
+
+    def z_id(k):
+        return ((z + k) % nz * CORES + c, rep)
+
+    def plane_id(k):
+        return (own, (rep + k) % nr)
+
+    sibling = (z * CORES + other, rep)
+
+    def copy(source, target, send, recv, device):
+        return pltpu.make_async_remote_copy(
+            src_ref=source, dst_ref=target, send_sem=send, recv_sem=recv,
+            device_id=device, device_id_type=MESH,
+        )
+
+    def each(count, step):
+        def run(k, carry):
+            step(k)
+            return carry
+        lax.fori_loop(1, count, run, 0)
+
+    barrier = pltpu.get_barrier_semaphore()
+    each(nz, lambda k: pl.semaphore_signal(barrier, inc=1, device_id=z_id(k), device_id_type=MESH))
+    each(nr, lambda k: pl.semaphore_signal(barrier, inc=1, device_id=plane_id(k), device_id_type=MESH))
+    pl.semaphore_signal(barrier, inc=1, device_id=sibling, device_id_type=MESH)
+    pl.semaphore_wait(barrier, nz - 1 + nr - 1 + 1)
+
+    at = c * nz + z
+    users[at, :, 0:D] = px_ref[...].astype(jnp.bfloat16)
+    users[at, :, D : D + WIDTH] = py_ref[...].astype(jnp.bfloat16)
+
+    def user_copy(k):
+        return copy(users.at[at], users.at[at], user_send.at[k], user_recv.at[z], z_id(k))
+
+    def user_relay(zz):
+        spot = users.at[c * nz + zz]
+        return copy(spot, spot, relay_send.at[zz], relay_recv.at[zz], sibling)
+
+    def user_wait(zz):
+        spot = users.at[c * nz + zz]
+        copy(spot, spot, user_send.at[0], user_recv.at[zz], sibling).wait_recv()
+
+    def relay_wait(zz):
+        spot = users.at[other * nz + zz]
+        copy(spot, spot, relay_send.at[zz], relay_recv.at[zz], sibling).wait_recv()
+
+    each(nz, lambda k: user_copy(k).start())
+    user_relay(z).start()
+
+    loads[0].wait()
+    loads[1].wait()
+    item_w = dot_t(items[...], w_out[...]).astype(jnp.bfloat16)
+
+    def pass_on(k):
+        zz = (z + k) % nz
+        user_wait(zz)
+        user_relay(zz).start()
+
+    each(nz, pass_on)
+    relay_wait(z)
+    each(nz, lambda k: relay_wait((z + k) % nz))
+
+    index = user_ref[...]
+    source = (index % slots) // 2
+    place = (source % CORES) * side + (source // CORES) * slots + index // slots * 2 + index % 2
+    table = dot_t(users[:, :, 0:D].reshape(2 * side, D), items[...]) + dot_t(
+        users[:, :, D : D + WIDTH].reshape(2 * side, WIDTH), item_w
+    )
+    imps = index.shape[1]
+    picked = lax.broadcasted_iota(jnp.int32, (2 * side, imps), 0) == place
+    logits = jnp.sum(jnp.where(picked, table, 0.0), 0, keepdims=True)
+    logit_ref[...] = logits
+    error = sigmoid(logits) - label_ref[...].astype(jnp.float32)
+
+    line = lax.broadcasted_iota(jnp.int32, (side, imps), 0)
+
+    def pool_side(core):
+        weight = jnp.where(line + core * side == place, error, 0.0).astype(jnp.bfloat16)
+        return dot(weight, item_w)
+
+    pool_send[...] = pool_side(other).astype(jnp.bfloat16).reshape(nz, slots, WIDTH)
+    pool_copy = copy(pool_send, pool_core, pcore_sem.at[0], pcore_sem.at[1], sibling)
+    pool_copy.start()
+    pool_mine[...] = pool_side(c).reshape(nz, slots, WIDTH)
+
+    turned = users[:, :, D : D + WIDTH].reshape(2 * side, WIDTH).astype(jnp.float32).T.astype(jnp.bfloat16)
+    chosen = dot(turned, picked.astype(jnp.bfloat16))
+    chosen = (chosen * error).astype(jnp.bfloat16)
+
+    def columns(core, k=0, size=half_w):
+        return pl.ds(pl.multiple_of(core * half_w + k * size, size), size)
+
+    def core_copy(a):
+        return copy(core_send.at[a], core_got.at[a], core_sem.at[a, 0], core_sem.at[a, 1], sibling)
+
+    core_send[0] = dot(chosen, items[:, columns(other)]).astype(jnp.bfloat16)
+    core_copy(0).start()
+    pool_copy.wait()
+    pool_z[...] = (pool_mine[...] + pool_core[...].astype(jnp.float32)).astype(jnp.bfloat16)
+
+    def pool_out(k):
+        zz = (z + k) % nz
+        return copy(pool_z.at[zz], pool_got.at[z], pz_send.at[k], pz_recv.at[z], z_id(k))
+
+    each(nz, lambda k: pool_out(k).start())
+    mine[0] = dot(chosen, items[:, columns(c)])
+
+    def plane_rows(k):
+        return pl.ds(pl.multiple_of((rep + k) % nr * block, block), block)
+
+    def plane_copy(a, k):
+        return copy(
+            half.at[a, plane_rows(k)], plane_got.at[a, rep], plane_send.at[a, k], plane_recv.at[a, rep], plane_id(k)
+        )
+
+    def core_end(a):
+        core_copy(a).wait()
+        half[a] = (mine[a] + core_got[a].astype(jnp.float32)).astype(jnp.bfloat16)
+        each(nr, lambda k: plane_copy(a, k).start())
+
+    def piece_spot(zz):
+        return (
+            pl.multiple_of(zz // 4 * TILE, TILE),
+            pl.multiple_of(zz % 4 * LANES, LANES),
+        )
+
+    def piece_copy(a, k):
+        down, across = piece_spot((z + k) % nz)
+        return copy(
+            row_sum.at[a, pl.ds(down, TILE), pl.ds(across, LANES)], piece_got.at[a, z],
+            piece_send.at[a, k], piece_recv.at[a, z], z_id(k),
+        )
+
+    def plane_end(a):
+        def add(k, total):
+            rr = (rep + k) % nr
+            spot = plane_got.at[a, rr]
+            copy(spot, spot, plane_send.at[a, 0], plane_recv.at[a, rr], sibling).wait_recv()
+            return total + spot[...].astype(jnp.float32)
+        total = half[a, plane_rows(0)].astype(jnp.float32)
+        row_sum[a] = lax.fori_loop(1, nr, add, total).astype(jnp.bfloat16)
+        each(nz, lambda k: piece_copy(a, k).start())
+
+    def final_spot(a, zz):
+        down, across = piece_spot(zz)
+        rows = pl.ds(pl.multiple_of(rep * block + down, TILE), TILE)
+        return grads[a].at[rows, pl.ds(pl.multiple_of(c * half_w + across, LANES), LANES)]
+
+    def back_copy(a, k):
+        spot = final_spot(a, z)
+        return copy(spot, spot, back_send.at[a, k], back_recv.at[a, z], z_id(k))
+
+    def piece_end(a):
+        down, across = piece_spot(z)
+        def add(k, total):
+            zz = (z + k) % nz
+            spot = piece_got.at[a, zz]
+            copy(spot, spot, piece_send.at[a, 0], piece_recv.at[a, zz], sibling).wait_recv()
+            return total + spot[...].astype(jnp.float32)
+        total = row_sum[a, pl.ds(down, TILE), pl.ds(across, LANES)].astype(jnp.float32)
+        final_spot(a, z)[...] = lax.fori_loop(1, nz, add, total).astype(jnp.bfloat16)
+        each(nz, lambda k: back_copy(a, k).start())
+
+    def wide_spot(a, core, k):
+        return grads[a].at[plane_rows(k), columns(core)]
+
+    def wide_copy(a, k):
+        spot = wide_spot(a, c, 0)
+        return copy(spot, spot, wide_send.at[a, k], wide_recv.at[a, rep], plane_id(k))
+
+    def last_copy(a, k):
+        spot = wide_spot(a, c, k)
+        rr = (rep + k) % nr
+        return copy(spot, spot, last_send.at[a, rr], last_recv.at[a, rr], sibling)
+
+    def back_end(a):
+        def wait(k):
+            zz = (z + k) % nz
+            spot = final_spot(a, zz)
+            copy(spot, spot, back_send.at[a, 0], back_recv.at[a, zz], sibling).wait_recv()
+        each(nz, wait)
+        each(nr, lambda k: wide_copy(a, k).start())
+        last_copy(a, 0).start()
+
+    def wide_end(a):
+        def step(k):
+            rr = (rep + k) % nr
+            spot = wide_spot(a, c, k)
+            copy(spot, spot, wide_send.at[a, 0], wide_recv.at[a, rr], sibling).wait_recv()
+            last_copy(a, k).start()
+        each(nr, step)
+
+    def last_end(a):
+        def step(k):
+            rr = (rep + k) % nr
+            spot = wide_spot(a, other, k)
+            copy(spot, spot, last_send.at[a, 0], last_recv.at[a, rr], sibling).wait_recv()
+        step(0)
+        each(nr, step)
+
+    core_end(0)
+
+    def pool_add(k, total):
+        zz = (z + k) % nz
+        spot = pool_got.at[zz]
+        copy(spot, spot, pz_send.at[0], pz_recv.at[zz], sibling).wait_recv()
+        return total + spot[...].astype(jnp.float32)
+
+    loads[2].wait()
+    loads[3].wait()
+    pool = lax.fori_loop(1, nz, pool_add, pool_z[z].astype(jnp.float32))
+    pool_t = pool.astype(jnp.bfloat16).astype(jnp.float32).T.astype(jnp.bfloat16)
+    tokens = slots * HIST
+    slot = lax.broadcasted_iota(jnp.int32, (slots, tokens), 0)
+    event = lax.broadcasted_iota(jnp.int32, (slots, tokens), 1)
+    holds = (event // HIST == slot).astype(jnp.bfloat16)
+    pre[...] = (dot(pool_t, holds) * slope[...].astype(jnp.float32)).astype(jnp.bfloat16)
+
+    quarter = half_w // 2
+
+    def gate_part(core, k):
+        return dot(pre[...], hist[:, columns(core, k, quarter)])
+
+    core_send[1, :, 0:quarter] = gate_part(other, 0).astype(jnp.bfloat16)
+    core_send[1, :, quarter:half_w] = gate_part(other, 1).astype(jnp.bfloat16)
+    core_copy(1).start()
+    plane_end(0)
+    mine[1, :, 0:quarter] = gate_part(c, 0)
+    mine[1, :, quarter:half_w] = gate_part(c, 1)
+    piece_end(0)
+    core_end(1)
+    back_end(0)
+    plane_end(1)
+    piece_end(1)
+    wide_end(0)
+    back_end(1)
+    wide_end(1)
+    last_end(0)
+    last_end(1)
+
+    def sent(k):
+        user_copy(k).wait_send()
+        pool_out(k).wait_send()
+        user_relay((z + k) % nz).wait_send()
+        for a in range(2):
+            piece_copy(a, k).wait_send()
+            back_copy(a, k).wait_send()
+
+    def sent_plane(k):
+        for a in range(2):
+            plane_copy(a, k).wait_send()
+            wide_copy(a, k).wait_send()
+            last_copy(a, k).wait_send()
+
+    each(nz, sent)
+    each(nr, sent_plane)
+    user_relay(z).wait_send()
+    for a in range(2):
+        last_copy(a, 0).wait_send()
+
+
+def exchange(imp_user, labels, px, py, items, w_out, slope, hist):
+    nz = lax.axis_size("own") // CORES
+    nr = lax.axis_size("rep")
+    slots = px.shape[0]
+    imps = imp_user.shape[0]
+    half_w = D // CORES
+    bf16, f32 = jnp.bfloat16, jnp.float32
+    vmem = pl.BlockSpec(memory_space=pltpu.VMEM)
+    hbm = pl.BlockSpec(memory_space=pl.ANY)
+    dma = pltpu.SemaphoreType.DMA
+    return pl.pallas_call(
+        functools.partial(exchange_kernel, nz, nr),
+        in_specs=[vmem] * 4 + [hbm] * 4,
+        out_specs=[vmem] * 3,
+        out_shape=[
+            jax.ShapeDtypeStruct((1, imps), f32),
+            jax.ShapeDtypeStruct((WIDTH, D), bf16),
+            jax.ShapeDtypeStruct((WIDTH, D), bf16),
+        ],
+        scratch_shapes=[
+            pltpu.VMEM(items.shape, bf16),
+            pltpu.VMEM(w_out.shape, bf16),
+            pltpu.VMEM(slope.shape, bf16),
+            pltpu.VMEM(hist.shape, bf16),
+            pltpu.VMEM((CORES * nz, slots, D + WIDTH), bf16),
+            pltpu.VMEM((nz, slots, WIDTH), bf16),
+            pltpu.VMEM((nz, slots, WIDTH), bf16),
+            pltpu.VMEM((nz, slots, WIDTH), f32),
+            pltpu.VMEM((nz, slots, WIDTH), bf16),
+            pltpu.VMEM((nz, slots, WIDTH), bf16),
+            pltpu.VMEM(slope.shape, bf16),
+            pltpu.VMEM((2, WIDTH, half_w), f32),
+            pltpu.VMEM((2, WIDTH, half_w), bf16),
+            pltpu.VMEM((2, WIDTH, half_w), bf16),
+            pltpu.VMEM((2, WIDTH, half_w), bf16),
+            pltpu.VMEM((2, nr, WIDTH // nr, half_w), bf16),
+            pltpu.VMEM((2, WIDTH // nr, half_w), bf16),
+            pltpu.VMEM((2, nz, TILE, LANES), bf16),
+            dma((4,)),
+            dma((nz,)), dma((nz,)), dma((nz,)), dma((nz,)),
+            dma((2,)),
+            dma((nz,)), dma((nz,)),
+            dma((2, 2)),
+            dma((2, nr)), dma((2, nr)),
+            dma((2, nz)), dma((2, nz)), dma((2, nz)), dma((2, nz)),
+            dma((2, nr)), dma((2, nr)), dma((2, nr)), dma((2, nr)),
+        ],
+        compiler_params=pltpu.CompilerParams(
+            collective_id=0, has_side_effects=True, vmem_limit_bytes=48 * 1024 * 1024
+        ),
+        name="exchange",
+    )(imp_user[None], labels[None], px, py, items, w_out, slope, hist)
+
+
 def body(histories, lengths, counts, imp_user, items, labels, w_uvqk, w_out):
     slots = histories.shape[0]
-    owners = lax.axis_size("own")
-    capacity = slots // owners
+    capacity = slots // lax.axis_size("own")
     ranks = jnp.arange(slots, dtype=jnp.int32)
     alive = ranks % capacity < jnp.repeat(counts, capacity)
     spans = jnp.where(alive, lengths, 0)
     px, py, slope = forward(histories, spans, w_uvqk)
-    px_all = lax.all_gather(px.astype(jnp.bfloat16), "own", axis=0, tiled=True)
-    py_all = lax.all_gather(py.astype(jnp.bfloat16), "own", axis=0, tiled=True)
-    place = (imp_user % slots) // capacity * slots + imp_user // slots * capacity + imp_user % capacity
-    columns = jnp.arange(owners * slots, dtype=jnp.int32)
-    select = place[:, None] == columns[None, :]
-    item_w = lax.dot_general(items, w_out, (((1,), (1,)), ((), ())), preferred_element_type=jnp.float32)
-    table = lax.dot_general(
-        items, px_all, (((1,), (1,)), ((), ())), preferred_element_type=jnp.float32
-    ) + lax.dot_general(
-        item_w.astype(jnp.bfloat16), py_all, (((1,), (1,)), ((), ())), preferred_element_type=jnp.float32
+    logits, grad_out, grad_gate = exchange(
+        imp_user, labels, px, py, items, w_out, slope, histories.reshape(-1, D)
     )
-    logits = jnp.sum(jnp.where(select, table, 0.0), -1)
-    error = (jax.nn.sigmoid(logits) - labels.astype(jnp.float32))[:, None]
-    pick = select.astype(jnp.bfloat16)
-    pool_part = lax.dot_general(
-        pick, (error * item_w).astype(jnp.bfloat16), (((0,), (0,)), ((), ())), preferred_element_type=jnp.float32
-    )
-    pool = lax.psum_scatter(pool_part.astype(jnp.bfloat16), "own", scatter_dimension=0, tiled=True)
-    rows = jnp.dot(pick, py_all, preferred_element_type=jnp.float32).astype(jnp.bfloat16)
-    out_term = lax.dot_general(
-        rows, (error * items.astype(jnp.float32)).astype(jnp.bfloat16), (((0,), (0,)), ((), ())),
-        preferred_element_type=jnp.float32,
-    )
-    spread = jnp.repeat(pool.T.astype(jnp.float32), HIST, axis=1)
-    grad_pre = (spread * slope.astype(jnp.float32)).astype(jnp.bfloat16)
-    gate_term = jnp.dot(grad_pre, histories.reshape(-1, D), preferred_element_type=jnp.float32)
-    out_sum, gate_sum = lax.psum(
-        (out_term.astype(jnp.bfloat16), gate_term.astype(jnp.bfloat16)), ("own", "rep")
-    )
-    return (logits, out_sum, gate_sum.T)
+    return (logits[0], grad_out, grad_gate.T)
 
 
 def solution(mesh):

time: 424 us -> 113 us (0.27)
  waiting for transfers between devices: 327 us -> 0 us
  Pallas kernels: 25.8 us -> 107 us
  blocking collectives: 23.3 us -> 0 us
  matrix products: 16.8 us -> 0 us
  between operations: 13.9 us -> 0.69 us
  local copies, waits for them, and re-layouts: 14.2 us -> 3.78 us
    psum x1 -> x0, waiting for transfers between devices: 262 us -> none  [body(): lax.psum((out_term.astype(jnp.bfloat16), gate_term.astype(jnp.bfloat16)),...]
    pallas_call x0 -> x1, Pallas kernels: none -> 81.5 us  [exchange(): pl.pallas_call(functools.partial(exchange_kernel, nz, nr), in_specs=[vmem...]
    reduce_scatter x1 -> x0, waiting for transfers between devices: 49 us -> none  [body(): lax.psum_scatter(pool_part.astype(jnp.bfloat16), 'own', scatter_dimension...]
    all_gather x1 -> x0, blocking collectives: 23.3 us -> none  [body(): py_all = lax.all_gather(py.astype(jnp.bfloat16), 'own', axis=0, tiled=True)]
    dot_general x6 -> x0, matrix products: 16.8 us -> none  [the longest x1 6.77 us: body(): jnp.dot(grad_pre, histories.reshape(-1, D), preferred_element_type=jnp.fl...]
    all_gather x1 -> x0, waiting for transfers between devices: 15.9 us -> none  [body(): px_all = lax.all_gather(px.astype(jnp.bfloat16), 'own', axis=0, tiled=True)]
    reshape x1 -> x0, local copies, waits for them, and re-layouts: 5.41 us -> none  [body(): spread = jnp.repeat(pool.T.astype(jnp.float32), HIST, axis=1)]
  transfers between devices with their start and end apart: 3 -> 0, of which waited for: 3 -> 0; matrix products, arithmetic and copies ran while one was open for 1% -> 0% of each run, Pallas kernels for 0% -> 0%
where the time goes in v2:
time: 113 us; the launch traced here: 112 us
  Pallas kernels  107 us (95%)
  local copies, waits for them, and re-layouts  3.78 us (3%)
    pallas_call x1, Pallas kernels, exchange(): pl.pallas_call(functools.partial(exchange_kernel, nz, nr), in_specs=[vmem...  81.5 us
    pallas_call x1, Pallas kernels, forward(): pl.pallas_call(forward_kernel, grid_spec=pltpu.PrefetchScalarGridSpec(num...  25.8 us
    unnamed x11, local copies, waits for them, and re-layouts  2.87 us

profile of v2, /device:TPU:1, one launch (start us, length us, event | category | flops | bytes accessed | tf_op | source)
XLA Modules:
  0.0 112.5 jit_solution(11502531006345129885)
XLA Ops:
  0.6 0.7 broadcast_in_dim.16
  1.4 0.1 reshape.12
  1.4 0.7 compare_select_fusion.spans
  2.1 0.1 copy.13.col_ref
  2.2 0.0 copy-start
  2.2 0.0 copy-start.1
  2.2 0.0 copy-start.2
  2.2 0.0 copy-start.3
  2.2 25.8 %forward.1 = (f32[32,1024]{1,0:T(8,128)S(1)}, f32[32,512]{1,0:T(8,128)S(1)}, bf16[512,2048]{1,0:T(8,128)(2,1)S(1)}) custom-call(s32[32]{0:T(128)S(1)} %compare_select_fusion.spans, s32[32,1]{1,0:T(8,128)S(1)} %copy.13.col_ref, bf16[32,64,1024]{2,1,0:T(8,128)(2,1)} %h_ref.1, bf16[1024,2048]{1,0:T(8,128)(2,1)} %w_ref.1), custom_call_target="tpu_custom_call" | custom-call | tf_op jit(solution)/shard_map/forward/pallas_call | solution.py:93
  28.1 0.0 copy-done
  28.1 0.0 copy-done.1
  28.1 0.0 copy-done.2
  28.1 0.0 copy-done.3
  28.1 81.5 %exchange.1 = (f32[1,256]{1,0:T(1,128)S(1)}, bf16[512,1024]{1,0:T(8,128)(2,1)S(1)}, bf16[512,1024]{1,0:T(8,128)(2,1)S(1)}) custom-call(s32[1,256]{1,0:T(1,128)S(1)} %bitcast.8, s32[1,256]{1,0:T(1,128)S(1)} %bitcast.9, f32[32,1024]{1,0:T(8,128)S(1)} %get-tuple-element.9.px_ref, f32[32,512]{1,0:T(8,128)S(1)} %get-tuple-element.10.py_ref, ...), custom_call_target="tpu_custom_call" | custom-call | tf_op jit(solution)/shard_map/exchange/pallas_call | solution.py:426
  109.6 1.3 %copy.14 = bf16[1024,512]{1,0:T(8,128)(2,1)} copy(bf16[1024,512]{0,1:T(8,128)(2,1)S(1)} %bitcast.6) | data formatting | bytes 2097152
  110.9 0.6 copy.17
  111.5 1.0 copy.18
Async XLA Ops:
  2.2 25.9 %copy-start = (bf16[512,1024]{1,0:T(8,128)(2,1)S(1)}, bf16[512,1024]{1,0:T(8,128)(2,1)}, u32[]{:S(2)}) copy-start(bf16[512,1024]{1,0:T(8,128)(2,1)} %w_hbm.1) | copy-start | bytes 3145732
  2.2 25.9 %copy-start.1 = (bf16[256,1024]{1,0:T(8,128)(2,1)S(1)}, bf16[256,1024]{1,0:T(8,128)(2,1)}, u32[]{:S(2)}) copy-start(bf16[256,1024]{1,0:T(8,128)(2,1)} %items_hbm.1) | copy-start | bytes 1572868
  2.2 25.9 %copy-start.2 = (s32[256]{0:T(256)S(1)}, s32[256]{0:T(256)}, u32[]{:S(2)}) copy-start(s32[256]{0:T(256)} %param.11) | copy-start | bytes 3076
  2.2 25.9 %copy-start.3 = (s32[256]{0:T(256)S(1)}, s32[256]{0:T(256)}, u32[]{:S(2)}) copy-start(s32[256]{0:T(256)} %param.13) | copy-start | bytes 3076

commit v3 on v2

v3 whole, which is shorter than its diff:
```python
import functools

import jax
import jax.numpy as jnp
from jax import lax
from jax.experimental import pallas as pl
from jax.experimental.pallas import tpu as pltpu
from jax.sharding import PartitionSpec as P

D = 1024
HEADS = 4
HEAD = 128
HIST = 64
WIDTH = HEADS * HEAD
BIN = 128
CHUNK = 256
CORES = 2
TILE = 16
LANES = 128
PARTS = 4
MESH = pl.DeviceIdType.MESH

EPS_NORM = 1e-06
EPS_LAYER = 1e-05


def sigmoid(v):
    return 0.5 * jnp.tanh(0.5 * v) + 0.5


def dot(a, b):
    return jnp.dot(a, b, preferred_element_type=jnp.float32)


def dot_t(a, b):
    return lax.dot_general(a, b, (((1,), (1,)), ((), ())), preferred_element_type=jnp.float32)


def forward_kernel(
    lengths, counts, h_hbm, w_hbm, user_ref, slope_ref, packed_ref, holds_ref,
    hist, w, heads_in, gate_act, gate_slope, sum_x, sum_y,
    spans, free, unit_source, unit_start, unit_span, unit_slot, load_sem,
):
    slots = user_ref.shape[0]
    bins = slots * HIST // BIN
    per_bin = BIN // TILE
    loads = [
        pltpu.make_async_copy(h_hbm, hist, load_sem.at[0]),
        pltpu.make_async_copy(w_hbm, w, load_sem.at[1]),
    ]
    for load in loads:
        load.start()
    sum_x[...] = jnp.zeros_like(sum_x)
    sum_y[...] = jnp.zeros_like(sum_y)

    def clear(u, carry):
        unit_source[u] = 0
        unit_start[u] = 0
        unit_span[u] = 0
        unit_slot[u] = 0
        return carry

    def clear_bin(b, carry):
        free[b] = per_bin
        return carry

    lax.fori_loop(0, bins * per_bin, clear, 0)
    lax.fori_loop(0, bins, clear_bin, 0)

    def size_of(s):
        return (spans[s] + TILE - 1) // TILE

    def put(s, b):
        size = size_of(s)
        used = per_bin - free[b]
        for j in range(HIST // TILE):
            @pl.when(j < size)
            def _():
                u = b * per_bin + used + j
                unit_source[u] = s * (HIST // TILE) + j
                unit_start[u] = used * TILE
                unit_span[u] = spans[s]
                unit_slot[u] = s
        free[b] = free[b] - size

    def large(s, count):
        live = s % 2 < counts[s // 2]
        spans[s] = jnp.where(live, lengths[s], 0)
        fits = size_of(s) > 2

        @pl.when(fits)
        def _():
            put(s, count // 2)
        return count + fits.astype(jnp.int32)

    used_bins = (lax.fori_loop(0, slots, large, jnp.int32(0)) + 1) // 2

    def small(size):
        def step(s, carry):
            def place(carry):
                at, top = carry
                at = lax.while_loop(lambda b: (b < bins - 1) & (free[b] < size), lambda b: b + 1, at)
                put(s, at)
                return at, jnp.maximum(top, at + 1)
            return lax.cond(size_of(s) == size, place, lambda carry: carry, carry)
        return step

    for size in (2, 1):
        used_bins = lax.fori_loop(0, slots, small(size), (jnp.int32(0), used_bins))[1]
    steps = (used_bins + 1) // 2

    for load in loads:
        load.wait()

    def block(i, carry):
        base = pl.multiple_of(i * 2 * BIN, 2 * BIN)
        for j in range(2 * per_bin):
            packed_ref[pl.ds(base + j * TILE, TILE), :] = hist[unit_source[i * 2 * per_bin + j]]
        x = packed_ref[pl.ds(base, 2 * BIN), :]
        feats = x.astype(jnp.float32)
        scale = lax.rsqrt(jnp.mean(feats * feats, -1, keepdims=True) + EPS_NORM)
        for j in range(4 * WIDTH // CHUNK):
            linear = dot(x, w[:, j * CHUNK : (j + 1) * CHUNK]) * scale
            sig = sigmoid(linear)
            act = linear * sig
            if j < WIDTH // CHUNK:
                gate_act[:, j * CHUNK : (j + 1) * CHUNK] = act
                gate_slope[:, j * CHUNK : (j + 1) * CHUNK] = sig + act * (1.0 - sig)
            else:
                heads_in[:, j * CHUNK - WIDTH : (j + 1) * CHUNK - WIDTH] = act.astype(jnp.bfloat16)
        row = lax.broadcasted_iota(jnp.int32, (BIN, BIN), 0)
        col = lax.broadcasted_iota(jnp.int32, (BIN, BIN), 1)
        spot = lax.broadcasted_iota(jnp.int32, (BIN, 1), 0)
        lane = lax.broadcasted_iota(jnp.int32, (1, BIN), 1)
        slot = lax.broadcasted_iota(jnp.int32, (slots, BIN), 0)
        for k in range(2):
            rows = slice(k * BIN, (k + 1) * BIN)
            units = [(i * 2 + k) * per_bin + j for j in range(per_bin)]

            def down(table):
                return jnp.concatenate([jnp.full((TILE, 1), table[u], jnp.int32) for u in units], 0)

            start = down(unit_start)
            span = down(unit_span)
            end = start + span
            allowed = (col >= start) & (col <= row) & (col < end)
            share = jnp.where(spot < end, 1.0 / jnp.maximum(span, 1).astype(jnp.float32), 0.0)
            back = share * scale[rows]
            name = jnp.full((1, BIN), -1, jnp.int32)
            stop = jnp.zeros((1, BIN), jnp.int32)
            for j, u in enumerate(units):
                here = lane // TILE == j
                name = jnp.where(here, unit_slot[u], name)
                stop = jnp.where(here, unit_start[u] + unit_span[u], stop)
            member = ((slot == name) & (lane < stop)).astype(jnp.bfloat16)
            place = pl.ds(pl.multiple_of(base + k * BIN, BIN), BIN)
            holds_ref[:, place] = member
            sum_x[...] += dot(member, x[rows])
            attended = []
            for h in range(HEADS):
                value, query, key = [
                    heads_in[rows, m * WIDTH + h * HEAD : m * WIDTH + (h + 1) * HEAD] for m in range(3)
                ]
                scores = dot_t(query, key) * HEAD ** (-0.5)
                attn = jnp.where(allowed, scores * sigmoid(scores), 0.0).astype(jnp.bfloat16)
                attended.append(dot(attn, value))
            center = sum(jnp.sum(a, -1, keepdims=True) for a in attended) / WIDTH
            moved = [a - center for a in attended]
            spread = sum(jnp.sum(a * a, -1, keepdims=True) for a in moved) / WIDTH
            norm = lax.rsqrt(spread + EPS_LAYER)
            for h in range(HEADS):
                cols = slice(h * HEAD, (h + 1) * HEAD)
                normal = moved[h] * norm
                mixed = normal * gate_act[rows, cols]
                high = mixed.astype(jnp.bfloat16)
                low = (mixed - high.astype(jnp.float32)).astype(jnp.bfloat16)
                sum_y[:, cols] += dot(member, high) + dot(member, low)
                slope = back * normal * gate_slope[rows, cols]
                slope_ref[cols, place] = slope.T.astype(jnp.bfloat16)
        return carry

    def blank(i, carry):
        place = pl.ds(pl.multiple_of(i * 2 * BIN, 2 * BIN), 2 * BIN)
        packed_ref[place, :] = jnp.zeros((2 * BIN, D), jnp.bfloat16)
        slope_ref[:, place] = jnp.zeros((WIDTH, 2 * BIN), jnp.bfloat16)
        holds_ref[:, place] = jnp.zeros((slots, 2 * BIN), jnp.bfloat16)
        return carry

    lax.fori_loop(0, steps, block, 0)
    lax.fori_loop(steps, bins // 2, blank, 0)
    which = lax.broadcasted_iota(jnp.int32, (slots, 1), 0)
    span = jnp.ones((slots, 1), jnp.int32)
    for s in range(slots):
        span = jnp.where(which == s, jnp.maximum(spans[s], 1), span)
    inverse = 1.0 / span.astype(jnp.float32)
    user_ref[:, 0:D] = (sum_x[...] * inverse).astype(jnp.bfloat16)
    user_ref[:, D : D + WIDTH] = (sum_y[...] * inverse).astype(jnp.bfloat16)


def forward(histories, lengths, counts, w_uvqk):
    slots = histories.shape[0]
    tokens = slots * HIST
    units = tokens // TILE
    bf16, f32 = jnp.bfloat16, jnp.float32
    vmem = pl.BlockSpec(memory_space=pltpu.VMEM)
    smem = pl.BlockSpec(memory_space=pltpu.SMEM)
    hbm = pl.BlockSpec(memory_space=pl.ANY)
    return pl.pallas_call(
        forward_kernel,
        in_specs=[smem, smem, hbm, hbm],
        out_specs=[vmem] * 4,
        out_shape=[
            jax.ShapeDtypeStruct((slots, D + WIDTH), bf16),
            jax.ShapeDtypeStruct((WIDTH, tokens), bf16),
            jax.ShapeDtypeStruct((tokens, D), bf16),
            jax.ShapeDtypeStruct((slots, tokens), bf16),
        ],
        scratch_shapes=[
            pltpu.VMEM((units, TILE, D), bf16),
            pltpu.VMEM(w_uvqk.shape, bf16),
            pltpu.VMEM((2 * BIN, 3 * WIDTH), bf16),
            pltpu.VMEM((2 * BIN, WIDTH), f32),
            pltpu.VMEM((2 * BIN, WIDTH), f32),
            pltpu.VMEM((slots, D), f32),
            pltpu.VMEM((slots, WIDTH), f32),
            pltpu.SMEM((slots,), jnp.int32),
            pltpu.SMEM((tokens // BIN,), jnp.int32),
            pltpu.SMEM((units,), jnp.int32),
            pltpu.SMEM((units,), jnp.int32),
            pltpu.SMEM((units,), jnp.int32),
            pltpu.SMEM((units,), jnp.int32),
            pltpu.SemaphoreType.DMA((2,)),
        ],
        compiler_params=pltpu.CompilerParams(vmem_limit_bytes=40 * 1024 * 1024),
        name="forward",
    )(lengths, counts, histories.reshape(units, TILE, D), w_uvqk)


def exchange_kernel(
    nz, nr, user_ref, label_ref, mine_ref, items, w_out, slope, packed, holds,
    logit_ref, out_ref, gate_ref,
    users, pool_send, pool_core, pool_mine, pool_z, pool_got,
    pre, mine, core_send, core_got, half, plane_got, row_sum, piece_got,
    user_send, user_recv, relay_send, relay_recv, pcore_sem, pz_send, pz_recv,
    core_sem, plane_send, plane_recv, piece_send, piece_recv, back_send, back_recv,
    wide_send, wide_recv, last_send, last_recv,
):
    own = lax.axis_index("own")
    rep = lax.axis_index("rep")
    z, c = own // CORES, own % CORES
    other = 1 - c
    slots = mine_ref.shape[0]
    side = nz * slots
    block = WIDTH // nr
    half_w = D // CORES
    grads = (out_ref, gate_ref)

    def z_id(k):
        return ((z + k) % nz * CORES + c, rep)

    def plane_id(k):
        return (own, (rep + k) % nr)

    sibling = (z * CORES + other, rep)

    def copy(source, target, send, recv, device):
        return pltpu.make_async_remote_copy(
            src_ref=source, dst_ref=target, send_sem=send, recv_sem=recv,
            device_id=device, device_id_type=MESH,
        )

    def each(count, step):
        def run(k, carry):
            step(k)
            return carry
        lax.fori_loop(1, count, run, 0)

    barrier = pltpu.get_barrier_semaphore()
    each(nz, lambda k: pl.semaphore_signal(barrier, inc=1, device_id=z_id(k), device_id_type=MESH))
    each(nr, lambda k: pl.semaphore_signal(barrier, inc=1, device_id=plane_id(k), device_id_type=MESH))
    pl.semaphore_signal(barrier, inc=1, device_id=sibling, device_id_type=MESH)
    pl.semaphore_wait(barrier, nz - 1 + nr - 1 + 1)

    at = c * nz + z
    users[at] = mine_ref[...]

    reach = nz // 2
    width = (D + WIDTH) // PARTS
    ends = (z_id(1), z_id(nz - 1))

    def origin(way, step):
        return (z + nz - step if way == 0 else z + step) % nz

    def hop(way, step, part):
        spot = users.at[c * nz + origin(way, step), :, part * width : (part + 1) * width]
        flag = (way * reach + step) * PARTS + part
        return copy(spot, spot, user_send.at[flag], user_recv.at[flag], ends[way])

    def landed(way, step, part):
        spot = users.at[c * nz + origin(way, step + 1), :, part * width : (part + 1) * width]
        flag = (way * reach + step) * PARTS + part
        copy(spot, spot, user_send.at[flag], user_recv.at[flag], ends[way]).wait_recv()

    def goes(way, step, part):
        return step < reach - 1 or part % 2 == way

    hops = [
        (way, step, part)
        for step in range(reach) for part in range(PARTS) for way in range(2) if goes(way, step, part)
    ]

    def user_relay(zz):
        spot = users.at[c * nz + zz]
        return copy(spot, spot, relay_send.at[zz], relay_recv.at[zz], sibling)

    def relay_wait(zz):
        spot = users.at[other * nz + zz]
        copy(spot, spot, relay_send.at[zz], relay_recv.at[zz], sibling).wait_recv()

    for part in range(PARTS):
        for way in range(2):
            hop(way, 0, part).start()
    user_relay(z).start()

    item_w = dot_t(items[...], w_out[...]).astype(jnp.bfloat16)

    for step in range(reach):
        for part in range(PARTS):
            for way in range(2):
                if goes(way, step, part):
                    landed(way, step, part)
                if step + 1 < reach and goes(way, step + 1, part):
                    hop(way, step + 1, part).start()
        user_relay(origin(0, step + 1)).start()
        if step + 1 < reach:
            user_relay(origin(1, step + 1)).start()
    relay_wait(z)
    each(nz, lambda k: relay_wait((z + k) % nz))

    index = user_ref[...]
    source = (index % slots) // 2
    place = (source % CORES) * side + (source // CORES) * slots + index // slots * 2 + index % 2
    table = dot_t(users[:, :, 0:D].reshape(2 * side, D), items[...]) + dot_t(
        users[:, :, D : D + WIDTH].reshape(2 * side, WIDTH), item_w
    )
    imps = index.shape[1]
    picked = lax.broadcasted_iota(jnp.int32, (2 * side, imps), 0) == place
    logits = jnp.sum(jnp.where(picked, table, 0.0), 0, keepdims=True)
    logit_ref[...] = logits
    error = sigmoid(logits) - label_ref[...].astype(jnp.float32)

    line = lax.broadcasted_iota(jnp.int32, (side, imps), 0)

    def pool_side(core):
        weight = jnp.where(line + core * side == place, error, 0.0).astype(jnp.bfloat16)
        return dot(weight, item_w)

    pool_send[...] = pool_side(other).astype(jnp.bfloat16).reshape(nz, slots, WIDTH)
    pool_copy = copy(pool_send, pool_core, pcore_sem.at[0], pcore_sem.at[1], sibling)
    pool_copy.start()
    pool_mine[...] = pool_side(c).reshape(nz, slots, WIDTH)

    turned = users[:, :, D : D + WIDTH].reshape(2 * side, WIDTH).astype(jnp.float32).T.astype(jnp.bfloat16)

    pool_copy.wait()
    pool_z[...] = (pool_mine[...] + pool_core[...].astype(jnp.float32)).astype(jnp.bfloat16)

    def pool_out(k):
        zz = (z + k) % nz
        return copy(pool_z.at[zz], pool_got.at[z], pz_send.at[k], pz_recv.at[z], z_id(k))

    each(nz, lambda k: pool_out(k).start())

    chosen = dot(turned, picked.astype(jnp.bfloat16))
    chosen = (chosen * error).astype(jnp.bfloat16)

    def columns(core, k=0, size=half_w):
        return pl.ds(pl.multiple_of(core * half_w + k * size, size), size)

    def core_copy(a):
        return copy(core_send.at[a], core_got.at[a], core_sem.at[a, 0], core_sem.at[a, 1], sibling)

    core_send[0] = dot(chosen, items[:, columns(other)]).astype(jnp.bfloat16)
    core_copy(0).start()
    mine[0] = dot(chosen, items[:, columns(c)])

    def plane_rows(k):
        return pl.ds(pl.multiple_of((rep + k) % nr * block, block), block)

    def plane_copy(a, k):
        return copy(
            half.at[a, plane_rows(k)], plane_got.at[a, rep], plane_send.at[a, k], plane_recv.at[a, rep], plane_id(k)
        )

    def core_end(a):
        core_copy(a).wait()
        half[a] = (mine[a] + core_got[a].astype(jnp.float32)).astype(jnp.bfloat16)
        each(nr, lambda k: plane_copy(a, k).start())

    def piece_spot(zz):
        return (
            pl.multiple_of(zz // 4 * TILE, TILE),
            pl.multiple_of(zz % 4 * LANES, LANES),
        )

    def piece_copy(a, k):
        down, across = piece_spot((z + k) % nz)
        return copy(
            row_sum.at[a, pl.ds(down, TILE), pl.ds(across, LANES)], piece_got.at[a, z],
            piece_send.at[a, k], piece_recv.at[a, z], z_id(k),
        )

    def plane_end(a):
        def add(k, total):
            rr = (rep + k) % nr
            spot = plane_got.at[a, rr]
            copy(spot, spot, plane_send.at[a, 0], plane_recv.at[a, rr], sibling).wait_recv()
            return total + spot[...].astype(jnp.float32)
        total = half[a, plane_rows(0)].astype(jnp.float32)
        row_sum[a] = lax.fori_loop(1, nr, add, total).astype(jnp.bfloat16)
        each(nz, lambda k: piece_copy(a, k).start())

    def final_spot(a, zz):
        down, across = piece_spot(zz)
        rows = pl.ds(pl.multiple_of(rep * block + down, TILE), TILE)
        return grads[a].at[rows, pl.ds(pl.multiple_of(c * half_w + across, LANES), LANES)]

    def back_copy(a, k):
        spot = final_spot(a, z)
        return copy(spot, spot, back_send.at[a, k], back_recv.at[a, z], z_id(k))

    def piece_end(a):
        down, across = piece_spot(z)
        def add(k, total):
            zz = (z + k) % nz
            spot = piece_got.at[a, zz]
            copy(spot, spot, piece_send.at[a, 0], piece_recv.at[a, zz], sibling).wait_recv()
            return total + spot[...].astype(jnp.float32)
        total = row_sum[a, pl.ds(down, TILE), pl.ds(across, LANES)].astype(jnp.float32)
        final_spot(a, z)[...] = lax.fori_loop(1, nz, add, total).astype(jnp.bfloat16)
        each(nz, lambda k: back_copy(a, k).start())

    def wide_spot(a, core, k):
        return grads[a].at[plane_rows(k), columns(core)]

    def wide_copy(a, k):
        spot = wide_spot(a, c, 0)
        return copy(spot, spot, wide_send.at[a, k], wide_recv.at[a, rep], plane_id(k))

    def last_copy(a, k):
        spot = wide_spot(a, c, k)
        rr = (rep + k) % nr
        return copy(spot, spot, last_send.at[a, rr], last_recv.at[a, rr], sibling)

    def back_end(a):
        def wait(k):
            zz = (z + k) % nz
            spot = final_spot(a, zz)
            copy(spot, spot, back_send.at[a, 0], back_recv.at[a, zz], sibling).wait_recv()
        each(nz, wait)
        each(nr, lambda k: wide_copy(a, k).start())
        last_copy(a, 0).start()

    def wide_end(a):
        def step(k):
            rr = (rep + k) % nr
            spot = wide_spot(a, c, k)
            copy(spot, spot, wide_send.at[a, 0], wide_recv.at[a, rr], sibling).wait_recv()
            last_copy(a, k).start()
        each(nr, step)

    def last_end(a):
        def step(k):
            rr = (rep + k) % nr
            spot = wide_spot(a, other, k)
            copy(spot, spot, last_send.at[a, 0], last_recv.at[a, rr], sibling).wait_recv()
        step(0)
        each(nr, step)

    core_end(0)

    def pool_add(k, total):
        zz = (z + k) % nz
        spot = pool_got.at[zz]
        copy(spot, spot, pz_send.at[0], pz_recv.at[zz], sibling).wait_recv()
        return total + spot[...].astype(jnp.float32)

    pool = lax.fori_loop(1, nz, pool_add, pool_z[z].astype(jnp.float32))
    pool_t = pool.astype(jnp.bfloat16).astype(jnp.float32).T.astype(jnp.bfloat16)
    pre[...] = (dot(pool_t, holds[...]) * slope[...].astype(jnp.float32)).astype(jnp.bfloat16)

    quarter = half_w // 2

    def gate_part(core, k):
        return dot(pre[...], packed[:, columns(core, k, quarter)])

    core_send[1, :, 0:quarter] = gate_part(other, 0).astype(jnp.bfloat16)
    core_send[1, :, quarter:half_w] = gate_part(other, 1).astype(jnp.bfloat16)
    core_copy(1).start()
    plane_end(0)
    mine[1, :, 0:quarter] = gate_part(c, 0)
    mine[1, :, quarter:half_w] = gate_part(c, 1)
    piece_end(0)
    core_end(1)
    plane_end(1)
    back_end(0)
    piece_end(1)
    wide_end(0)
    back_end(1)
    wide_end(1)
    last_end(0)
    last_end(1)

    def sent(k):
        pool_out(k).wait_send()
        user_relay((z + k) % nz).wait_send()
        for a in range(2):
            piece_copy(a, k).wait_send()
            back_copy(a, k).wait_send()

    def sent_plane(k):
        for a in range(2):
            plane_copy(a, k).wait_send()
            wide_copy(a, k).wait_send()
            last_copy(a, k).wait_send()

    each(nz, sent)
    each(nr, sent_plane)
    user_relay(z).wait_send()
    for way, step, part in hops:
        hop(way, step, part).wait_send()
    for a in range(2):
        last_copy(a, 0).wait_send()


def exchange(imp_user, labels, users, items, w_out, slope, packed, holds):
    nz = lax.axis_size("own") // CORES
    nr = lax.axis_size("rep")
    slots = users.shape[0]
    imps = imp_user.shape[0]
    half_w = D // CORES
    bf16, f32 = jnp.bfloat16, jnp.float32
    vmem = pl.BlockSpec(memory_space=pltpu.VMEM)
    dma = pltpu.SemaphoreType.DMA
    return pl.pallas_call(
        functools.partial(exchange_kernel, nz, nr),
        in_specs=[vmem] * 8,
        out_specs=[vmem] * 3,
        out_shape=[
            jax.ShapeDtypeStruct((1, imps), f32),
            jax.ShapeDtypeStruct((WIDTH, D), bf16),
            jax.ShapeDtypeStruct((WIDTH, D), bf16),
        ],
        scratch_shapes=[
            pltpu.VMEM((CORES * nz, slots, D + WIDTH), bf16),
            pltpu.VMEM((nz, slots, WIDTH), bf16),
            pltpu.VMEM((nz, slots, WIDTH), bf16),
            pltpu.VMEM((nz, slots, WIDTH), f32),
            pltpu.VMEM((nz, slots, WIDTH), bf16),
            pltpu.VMEM((nz, slots, WIDTH), bf16),
            pltpu.VMEM(slope.shape, bf16),
            pltpu.VMEM((2, WIDTH, half_w), f32),
            pltpu.VMEM((2, WIDTH, half_w), bf16),
            pltpu.VMEM((2, WIDTH, half_w), bf16),
            pltpu.VMEM((2, WIDTH, half_w), bf16),
            pltpu.VMEM((2, nr, WIDTH // nr, half_w), bf16),
            pltpu.VMEM((2, WIDTH // nr, half_w), bf16),
            pltpu.VMEM((2, nz, TILE, LANES), bf16),
            dma((nz * PARTS,)), dma((nz * PARTS,)), dma((nz,)), dma((nz,)),
            dma((2,)),
            dma((nz,)), dma((nz,)),
            dma((2, 2)),
            dma((2, nr)), dma((2, nr)),
            dma((2, nz)), dma((2, nz)), dma((2, nz)), dma((2, nz)),
            dma((2, nr)), dma((2, nr)), dma((2, nr)), dma((2, nr)),
        ],
        compiler_params=pltpu.CompilerParams(
            collective_id=0, has_side_effects=True, vmem_limit_bytes=48 * 1024 * 1024
        ),
        name="exchange",
    )(imp_user[None], labels[None], users, items, w_out, slope, packed, holds)


def body(histories, lengths, counts, imp_user, items, labels, w_uvqk, w_out):
    users, slope, packed, holds = forward(histories, lengths, counts, w_uvqk)
    logits, grad_out, grad_gate = exchange(
        imp_user, labels, users, items, w_out, slope, packed, holds
    )
    return (logits[0], grad_out, grad_gate.T)


def solution(mesh):
    return jax.shard_map(
        body,
        mesh=mesh,
        in_specs=(
            P(("own", "rep"), None, None),
            P(("own", "rep")),
            P(("own", "rep")),
            P(("own", "rep")),
            P(("own", "rep"), None),
            P(("own", "rep")),
            P(),
            P(),
        ),
        out_specs=(P(("own", "rep")), P(), P()),
        check_vma=False,
    )
```

time: 113 us -> 107 us (0.947)
  Pallas kernels: 107 us -> 97.7 us
  local copies, waits for them, and re-layouts: 3.78 us -> 8.3 us
    pallas_call x1, Pallas kernels: 25.8 us -> 19.9 us  [forward(): pl.pallas_call(forward_kernel, in_specs=[smem, smem, hbm, hbm], out_specs...]
    unnamed x11 -> x19, local copies, waits for them, and re-layouts: 2.87 us -> 8.3 us
    pallas_call x1, Pallas kernels: 81.5 us -> 77.8 us  [exchange(): pl.pallas_call(functools.partial(exchange_kernel, nz, nr), in_specs=[vmem...]
where the time goes in v3:
time: 107 us
  Pallas kernels  97.7 us (91%)
  local copies, waits for them, and re-layouts  8.3 us (8%)
    pallas_call x1, Pallas kernels, exchange(): pl.pallas_call(functools.partial(exchange_kernel, nz, nr), in_specs=[vmem...  77.8 us
    pallas_call x1, Pallas kernels, forward(): pl.pallas_call(forward_kernel, in_specs=[smem, smem, hbm, hbm], out_specs...  19.9 us
    unnamed x19, local copies, waits for them, and re-layouts  8.3 us

profile of v3, /device:TPU:1, one launch (start us, length us, event | category | flops | bytes accessed | tf_op | source)
XLA Modules:
  0.0 106.7 jit_solution(119083849758393411)
XLA Ops:
  0.6 0.0 copy-start
  0.6 2.2 %copy-done = bf16[32,64,1024]{2,1,0:T(8,128)(2,1)S(1)} copy-done((bf16[32,64,1024]{2,1,0:T(8,128)(2,1)S(1)}, bf16[32,64,1024]{2,1,0:T(8,128)(2,1)}, u32[]{:S(2)}) %copy-start) | copy-done | bytes 4194328
  2.8 0.0 copy-start.6
  2.8 0.7 copy-done.6
  3.5 0.0 copy-start.7
  3.5 0.7 copy-done.7
  4.1 0.0 copy-start.2
  4.1 0.0 copy-start.3
  4.1 0.0 copy-start.4
  4.1 0.0 copy-start.5
  4.1 19.9 %forward.1 = (bf16[32,1536]{1,0:T(8,128)(2,1)S(1)}, bf16[512,2048]{1,0:T(8,128)(2,1)S(1)}, bf16[2048,1024]{1,0:T(8,128)(2,1)S(1)}, bf16[32,2048]{1,0:T(8,128)(2,1)S(1)}) custom-call(s32[32]{0:T(128)S(1)} %copy-done.6, s32[16]{0:T(128)S(1)} %copy-done.7, bf16[128,16,1024]{2,1,0:T(8,128)(2,1)S(1)} %bitcast.5, bf16[1024,2048]{1,0:T(8,128)(2,1)} %w_hbm.1), custom_call_target="tpu_custom_call" | custom-call | tf_op jit(solution)/shard_map/forward/pallas_call | solution.py:208
  24.1 0.0 copy-start.1
  24.1 1.9 %copy-done.1 = bf16[2048,1024]{1,0:T(8,128)(2,1)} copy-done((bf16[2048,1024]{1,0:T(8,128)(2,1)}, bf16[2048,1024]{1,0:T(8,128)(2,1)S(1)}, u32[]{:S(2)}) %copy-start.1) | copy-done | bytes 4194328
  26.0 0.0 copy-done.2
  26.0 0.0 copy-done.3
  26.0 0.0 copy-done.4
  26.0 0.0 copy-done.5
  26.1 77.8 %exchange.1 = (f32[1,256]{1,0:T(1,128)S(1)}, bf16[512,1024]{1,0:T(8,128)(2,1)S(1)}, bf16[512,1024]{1,0:T(8,128)(2,1)S(1)}) custom-call(s32[1,256]{1,0:T(1,128)S(1)} %bitcast.7, s32[1,256]{1,0:T(1,128)S(1)} %bitcast.8, bf16[32,1536]{1,0:T(8,128)(2,1)S(1)} %get-tuple-element.10.mine_ref, bf16[256,1024]{1,0:T(8,128)(2,1)S(1)} %copy-done.3, ...), custom_call_target="tpu_custom_call" | custom-call | tf_op jit(solution)/shard_map/exchange/pallas_call | solution.py:545
  103.8 1.3 %copy.11 = bf16[1024,512]{1,0:T(8,128)(2,1)} copy(bf16[1024,512]{0,1:T(8,128)(2,1)S(1)} %bitcast.6) | data formatting | bytes 2097152
  105.2 0.6 copy.14
  105.7 1.0 copy.15
Async XLA Ops:
  0.6 2.2 %copy-start = (bf16[32,64,1024]{2,1,0:T(8,128)(2,1)S(1)}, bf16[32,64,1024]{2,1,0:T(8,128)(2,1)}, u32[]{:S(2)}) copy-start(bf16[32,64,1024]{2,1,0:T(8,128)(2,1)} %param.8) | copy-start | bytes 12582916
  2.8 0.7 copy-start.6
  3.5 0.7 copy-start.7
  4.1 21.9 %copy-start.2 = (bf16[512,1024]{1,0:T(8,128)(2,1)S(1)}, bf16[512,1024]{1,0:T(8,128)(2,1)}, u32[]{:S(2)}) copy-start(bf16[512,1024]{1,0:T(8,128)(2,1)} %w_out.1) | copy-start | bytes 3145732
  4.1 21.9 %copy-start.3 = (bf16[256,1024]{1,0:T(8,128)(2,1)S(1)}, bf16[256,1024]{1,0:T(8,128)(2,1)}, u32[]{:S(2)}) copy-start(bf16[256,1024]{1,0:T(8,128)(2,1)} %items.1) | copy-start | bytes 1572868
  4.1 21.9 %copy-start.4 = (s32[256]{0:T(256)S(1)}, s32[256]{0:T(256)}, u32[]{:S(2)}) copy-start(s32[256]{0:T(256)} %param.11) | copy-start | bytes 3076
  4.1 21.9 %copy-start.5 = (s32[256]{0:T(256)S(1)}, s32[256]{0:T(256)}, u32[]{:S(2)}) copy-start(s32[256]{0:T(256)} %param.13) | copy-start | bytes 3076
  24.1 1.9 %copy-start.1 = (bf16[2048,1024]{1,0:T(8,128)(2,1)}, bf16[2048,1024]{1,0:T(8,128)(2,1)S(1)}, u32[]{:S(2)}) copy-start(bf16[2048,1024]{1,0:T(8,128)(2,1)S(1)} %get-tuple-element.12.packed) | copy-start | bytes 12582916

commit v4 on v3

v4 whole, which is shorter than its diff:
```python
import functools

import jax
import jax.numpy as jnp
from jax import lax
from jax.experimental import pallas as pl
from jax.experimental.pallas import tpu as pltpu
from jax.sharding import PartitionSpec as P

D = 1024
HEADS = 4
HEAD = 128
HIST = 64
WIDTH = HEADS * HEAD
BIN = 128
CHUNK = 256
CORES = 2
TILE = 16
LANES = 128
PARTS = 4
MESH = pl.DeviceIdType.MESH

EPS_NORM = 1e-06
EPS_LAYER = 1e-05


def sigmoid(v):
    return 0.5 * jnp.tanh(0.5 * v) + 0.5


def dot(a, b):
    return jnp.dot(a, b, preferred_element_type=jnp.float32)


def dot_t(a, b):
    return lax.dot_general(a, b, (((1,), (1,)), ((), ())), preferred_element_type=jnp.float32)


def forward_kernel(
    lengths_hbm, counts_hbm, h_hbm, w_hbm, user_ref, slope_hbm, packed_hbm, holds_hbm,
    slope_ref, packed_ref, holds_ref, w, heads_in, gate_act, gate_slope, sum_x, sum_y,
    lengths, counts, spans, free, unit_source, unit_start, unit_stop, unit_slot, load_sem, unit_sem, out_sem,
):
    slots = user_ref.shape[0]
    bins = slots * HIST // BIN
    per_bin = BIN // TILE
    per_step = 2 * per_bin
    loads = [
        pltpu.make_async_copy(source, target, load_sem.at[k])
        for k, (source, target) in enumerate(((lengths_hbm, lengths), (counts_hbm, counts), (w_hbm, w)))
    ]
    for load in loads:
        load.start()
    sum_x[...] = jnp.zeros_like(sum_x)
    sum_y[...] = jnp.zeros_like(sum_y)

    def clear_bin(b, carry):
        free[b] = per_bin
        return carry

    lax.fori_loop(0, bins, clear_bin, 0)
    loads[0].wait()
    loads[1].wait()

    def size_of(s):
        return (spans[s] + TILE - 1) // TILE

    def put(s, b):
        size = size_of(s)
        used = per_bin - free[b]
        first = b * per_bin + used

        def fill(j, carry):
            unit_source[first + j] = s * (HIST // TILE) + j
            unit_start[first + j] = used * TILE
            unit_stop[first + j] = used * TILE + spans[s]
            unit_slot[first + j] = s
            return carry

        lax.fori_loop(0, size, fill, 0)
        free[b] = free[b] - size

    def large(s, count):
        live = s % 2 < counts[s // 2]
        spans[s] = jnp.where(live, lengths[s], 0)
        fits = size_of(s) > 2

        @pl.when(fits)
        def _():
            put(s, count // 2)
        return count + fits.astype(jnp.int32)

    used_bins = (lax.fori_loop(0, slots, large, jnp.int32(0)) + 1) // 2

    def small(size):
        def step(s, carry):
            def place(carry):
                at, top = carry
                at = lax.while_loop(lambda b: (b < bins - 1) & (free[b] < size), lambda b: b + 1, at)
                put(s, at)
                return at, jnp.maximum(top, at + 1)
            return lax.cond(size_of(s) == size, place, lambda carry: carry, carry)
        return step

    for size in (2, 1):
        used_bins = lax.fori_loop(0, slots, small(size), (jnp.int32(0), used_bins))[1]
    steps = (used_bins + 1) // 2

    def pad(b, carry):
        def fill(u, carry):
            unit_source[u] = 0
            unit_start[u] = 0
            unit_stop[u] = 0
            unit_slot[u] = 0
            return carry
        lax.fori_loop((b + 1) * per_bin - free[b], (b + 1) * per_bin, fill, 0)
        return carry

    lax.fori_loop(0, 2 * steps, pad, 0)

    def tile_copy(u):
        row = pl.ds(pl.multiple_of(u * TILE, TILE), TILE)
        return pltpu.make_async_copy(h_hbm.at[unit_source[u]], packed_ref.at[row], unit_sem.at[u])

    def fetch(u, carry):
        tile_copy(u).start()
        return carry

    lax.fori_loop(0, steps * per_step, fetch, 0)

    def packed_out(i):
        place = pl.ds(pl.multiple_of(i * 2 * BIN, 2 * BIN), 2 * BIN)
        return pltpu.make_async_copy(packed_ref.at[place], packed_hbm.at[place], out_sem.at[0, i])

    def rest_out(i):
        place = pl.ds(pl.multiple_of(i * 2 * BIN, 2 * BIN), 2 * BIN)
        return [
            pltpu.make_async_copy(slope_ref.at[:, place], slope_hbm.at[:, place], out_sem.at[1, i]),
            pltpu.make_async_copy(holds_ref.at[:, place], holds_hbm.at[:, place], out_sem.at[2, i]),
        ]

    def blank(i, carry):
        place = pl.ds(pl.multiple_of(i * 2 * BIN, 2 * BIN), 2 * BIN)
        packed_ref[place, :] = jnp.zeros((2 * BIN, D), jnp.bfloat16)
        slope_ref[:, place] = jnp.zeros((WIDTH, 2 * BIN), jnp.bfloat16)
        holds_ref[:, place] = jnp.zeros((slots, 2 * BIN), jnp.bfloat16)
        packed_out(i).start()
        for done in rest_out(i):
            done.start()
        return carry

    lax.fori_loop(steps, bins // 2, blank, 0)
    loads[2].wait()

    def block(i, carry):
        base = pl.multiple_of(i * 2 * BIN, 2 * BIN)
        for j in range(per_step):
            tile_copy(i * per_step + j).wait()
        packed_out(i).start()
        x = packed_ref[pl.ds(base, 2 * BIN), :]
        feats = x.astype(jnp.float32)
        scale = lax.rsqrt(jnp.mean(feats * feats, -1, keepdims=True) + EPS_NORM)
        half_scale = 0.5 * scale
        for j in range(4 * WIDTH // CHUNK):
            half = dot(x, w[:, j * CHUNK : (j + 1) * CHUNK]) * half_scale
            t = jnp.tanh(half)
            act = half * t + half
            if j < WIDTH // CHUNK:
                gate_act[:, j * CHUNK : (j + 1) * CHUNK] = act
                gate_slope[:, j * CHUNK : (j + 1) * CHUNK] = (1.0 + t) * (1.0 + half * (1.0 - t))
            else:
                heads_in[:, j * CHUNK - WIDTH : (j + 1) * CHUNK - WIDTH] = act.astype(jnp.bfloat16)
        row = lax.broadcasted_iota(jnp.int32, (BIN, BIN), 0)
        col = lax.broadcasted_iota(jnp.int32, (BIN, BIN), 1)
        lane = lax.broadcasted_iota(jnp.int32, (1, BIN), 1)
        slot = lax.broadcasted_iota(jnp.int32, (slots, BIN), 0)
        for k in range(2):
            rows = slice(k * BIN, (k + 1) * BIN)
            units = [(i * 2 + k) * per_bin + j for j in range(per_bin)]

            def down(values):
                return jnp.concatenate([jnp.full((TILE, BIN), v, jnp.int32) for v in values], 0)

            start = down([unit_start[u] for u in units])
            stop = down([unit_stop[u] for u in units])
            allowed = (col >= start) & (col <= row) & (col < stop)
            span = jnp.maximum(stop - start, 1).astype(jnp.float32)
            back = jnp.where(row < stop, half_scale[rows] / span, 0.0)
            name = jnp.full((1, BIN), -1, jnp.int32)
            limit = jnp.zeros((1, BIN), jnp.int32)
            for j, u in enumerate(units):
                here = lane // TILE == j
                name = jnp.where(here, unit_slot[u], name)
                limit = jnp.where(here, unit_stop[u], limit)
            member = ((slot == name) & (lane < limit)).astype(jnp.bfloat16)
            place = pl.ds(pl.multiple_of(base + k * BIN, BIN), BIN)
            holds_ref[:, place] = member
            sum_x[...] += dot(member, x[rows])
            attended = []
            for h in range(HEADS):
                value, query, key = [
                    heads_in[rows, m * WIDTH + h * HEAD : m * WIDTH + (h + 1) * HEAD] for m in range(3)
                ]
                half = dot_t(query, key) * (0.5 * HEAD ** (-0.5))
                attn = jnp.where(allowed, half * jnp.tanh(half) + half, 0.0).astype(jnp.bfloat16)
                attended.append(dot(attn, value))
            center = jnp.sum(sum(attended), -1, keepdims=True) / WIDTH
            moved = [a - center for a in attended]
            spread = jnp.sum(sum(a * a for a in moved), -1, keepdims=True) / WIDTH
            norm = lax.rsqrt(spread + EPS_LAYER)
            for h in range(HEADS):
                cols = slice(h * HEAD, (h + 1) * HEAD)
                normal = moved[h] * norm
                mixed = (normal * gate_act[rows, cols]).astype(jnp.bfloat16)
                sum_y[:, cols] += dot(member, mixed)
                slope = back * normal * gate_slope[rows, cols]
                slope_ref[cols, place] = slope.T.astype(jnp.bfloat16)
        for done in rest_out(i):
            done.start()
        return carry

    lax.fori_loop(0, steps, block, 0)
    which = lax.broadcasted_iota(jnp.int32, (slots, 1), 0)
    span = jnp.ones((slots, 1), jnp.int32)
    for s in range(slots):
        span = jnp.where(which == s, jnp.maximum(spans[s], 1), span)
    inverse = 1.0 / span.astype(jnp.float32)
    user_ref[:, 0:D] = (sum_x[...] * inverse).astype(jnp.bfloat16)
    user_ref[:, D : D + WIDTH] = (sum_y[...] * inverse).astype(jnp.bfloat16)

    def finish(i, carry):
        packed_out(i).wait()
        for done in rest_out(i):
            done.wait()
        return carry

    lax.fori_loop(0, bins // 2, finish, 0)


def forward(histories, lengths, counts, w_uvqk):
    slots = histories.shape[0]
    tokens = slots * HIST
    units = tokens // TILE
    bf16, f32 = jnp.bfloat16, jnp.float32
    vmem = pl.BlockSpec(memory_space=pltpu.VMEM)
    hbm = pl.BlockSpec(memory_space=pltpu.HBM)
    return pl.pallas_call(
        forward_kernel,
        in_specs=[hbm] * 4,
        out_specs=[vmem] + [hbm] * 3,
        out_shape=[
            jax.ShapeDtypeStruct((slots, D + WIDTH), bf16),
            jax.ShapeDtypeStruct((WIDTH, tokens), bf16),
            jax.ShapeDtypeStruct((tokens, D), bf16),
            jax.ShapeDtypeStruct((slots, tokens), bf16),
        ],
        scratch_shapes=[
            pltpu.VMEM((WIDTH, tokens), bf16),
            pltpu.VMEM((tokens, D), bf16),
            pltpu.VMEM((slots, tokens), bf16),
            pltpu.VMEM(w_uvqk.shape, bf16),
            pltpu.VMEM((2 * BIN, 3 * WIDTH), bf16),
            pltpu.VMEM((2 * BIN, WIDTH), f32),
            pltpu.VMEM((2 * BIN, WIDTH), f32),
            pltpu.VMEM((slots, D), f32),
            pltpu.VMEM((slots, WIDTH), f32),
            pltpu.SMEM(lengths.shape, jnp.int32),
            pltpu.SMEM(counts.shape, jnp.int32),
            pltpu.SMEM((slots,), jnp.int32),
            pltpu.SMEM((tokens // BIN,), jnp.int32),
            pltpu.SMEM((units,), jnp.int32),
            pltpu.SMEM((units,), jnp.int32),
            pltpu.SMEM((units,), jnp.int32),
            pltpu.SMEM((units,), jnp.int32),
            pltpu.SemaphoreType.DMA((3,)),
            pltpu.SemaphoreType.DMA((units,)),
            pltpu.SemaphoreType.DMA((3, tokens // (2 * BIN))),
        ],
        compiler_params=pltpu.CompilerParams(vmem_limit_bytes=58 * 1024 * 1024),
        name="forward",
    )(lengths, counts, histories.reshape(units, TILE, D), w_uvqk)


def exchange_kernel(
    nz, nr, *args,
):
    loaded = 8
    sources = args[:loaded]
    logit_ref, out_ref, gate_ref = args[loaded : loaded + 3]
    users = args[loaded + 3]
    user_ref, label_ref, items, w_out, slope, packed, holds = args[loaded + 4 : 2 * loaded + 3]
    exchange_steps(
        nz, nr, sources, user_ref, label_ref, items, w_out, slope, packed, holds,
        logit_ref, out_ref, gate_ref, users, *args[2 * loaded + 3 :],
    )


def exchange_steps(
    nz, nr, sources, user_ref, label_ref, items, w_out, slope, packed, holds,
    logit_ref, out_ref, gate_ref,
    users, pool_send, pool_core, pool_mine, pool_z, pool_got, *rest,
):
    per_sum = 8
    sums = [rest[n * per_sum : (n + 1) * per_sum] for n in range(3)]
    (
        load_sem, user_send, user_recv, relay_sem, pcore_send, pcore_recv, pz_send, pz_recv, sum_send, sum_recv,
    ) = rest[3 * per_sum :]
    own = lax.axis_index("own")
    rep = lax.axis_index("rep")
    z, c = own // CORES, own % CORES
    other = 1 - c
    slots = users.shape[1]
    side = nz * slots
    half_w = D // CORES
    deep = WIDTH // 2

    targets = (user_ref, label_ref, users.at[c * nz + z], items, w_out, slope, packed, holds)
    loads = [
        pltpu.make_async_copy(source, target, load_sem.at[k])
        for k, (source, target) in enumerate(zip(sources, targets))
    ]
    for k in (2, 3, 4, 0, 1, 7, 5, 6):
        loads[k].start()

    def z_id(k):
        return ((z + k) % nz * CORES + c, rep)

    def plane_id(k):
        return (own, (rep + k) % nr)

    sibling = (z * CORES + other, rep)

    def copy(source, target, send, recv, device):
        return pltpu.make_async_remote_copy(
            src_ref=source, dst_ref=target, send_sem=send, recv_sem=recv,
            device_id=device, device_id_type=MESH,
        )

    def signal(device):
        pl.semaphore_signal(barrier, inc=1, device_id=device, device_id_type=MESH)

    barrier = pltpu.get_barrier_semaphore()
    for k in range(1, nz):
        signal(z_id(k))
    for k in range(1, nr):
        signal(plane_id(k))
    signal(sibling)
    pl.semaphore_wait(barrier, nz - 1 + nr - 1 + 1)

    loads[2].wait()
    reach = nz // 2
    width = (D + WIDTH) // PARTS
    ends = (z_id(1), z_id(nz - 1))

    def origin(way, step):
        return (z + nz - step if way == 0 else z + step) % nz

    def hop(way, step, part):
        spot = users.at[c * nz + origin(way, step), :, part * width : (part + 1) * width]
        return copy(spot, spot, user_send, user_recv.at[(way * reach + step) * PARTS + part], ends[way])

    def landed(way, step, part):
        spot = users.at[c * nz + origin(way, step + 1), :, part * width : (part + 1) * width]
        copy(spot, spot, user_send, user_recv.at[(way * reach + step) * PARTS + part], ends[way]).wait_recv()

    def goes(way, step, part):
        return step < reach - 1 or part % 2 == way

    def user_relay(zz):
        spot = users.at[c * nz + zz]
        return copy(spot, spot, relay_sem.at[0], relay_sem.at[1], sibling)

    for part in range(PARTS):
        for way in range(2):
            hop(way, 0, part).start()
    user_relay(z).start()
    loads[3].wait()
    loads[4].wait()
    item_w = dot_t(items[...], w_out[...]).astype(jnp.bfloat16)
    for step in range(reach):
        for part in range(PARTS):
            for way in range(2):
                if goes(way, step, part):
                    landed(way, step, part)
                if step + 1 < reach and goes(way, step + 1, part):
                    hop(way, step + 1, part).start()
        user_relay(origin(0, step + 1)).start()
        if step + 1 < reach:
            user_relay(origin(1, step + 1)).start()
    all_relays = copy(
        users.at[pl.ds(c * nz, nz)], users.at[pl.ds(other * nz, nz)], relay_sem.at[0], relay_sem.at[1], sibling
    )
    loads[0].wait()
    loads[1].wait()
    all_relays.wait_recv()

    index = user_ref[...]
    source = (index % slots) // 2
    place = (source % CORES) * side + (source // CORES) * slots + index // slots * 2 + index % 2
    table = dot_t(users[:, :, 0:D].reshape(2 * side, D), items[...]) + dot_t(
        users[:, :, D : D + WIDTH].reshape(2 * side, WIDTH), item_w
    )
    imps = index.shape[1]
    picked = lax.broadcasted_iota(jnp.int32, (2 * side, imps), 0) == place
    logits = jnp.sum(jnp.where(picked, table, 0.0), 0, keepdims=True)
    logit_ref[...] = logits
    error = sigmoid(logits) - label_ref[...].astype(jnp.float32)

    line = lax.broadcasted_iota(jnp.int32, (side, imps), 0)

    def pool_side(core):
        weight = jnp.where(line + core * side == place, error, 0.0).astype(jnp.bfloat16)
        return [dot(weight, item_w[:, f * deep : (f + 1) * deep]).reshape(nz, slots, deep) for f in range(2)]

    def pool_copy(f):
        return copy(pool_send.at[f], pool_core.at[f], pcore_send.at[f], pcore_recv.at[f], sibling)

    for f, part in enumerate(pool_side(other)):
        pool_send[f] = part.astype(jnp.bfloat16)
        pool_copy(f).start()
    for f, part in enumerate(pool_side(c)):
        pool_mine[f] = part

    turned = users[:, :, D : D + WIDTH].reshape(2 * side, WIDTH).astype(jnp.float32).T.astype(jnp.bfloat16)

    def pool_out(f, k):
        zz = (z + k) % nz
        return copy(pool_z.at[f, zz], pool_got.at[f, z], pz_send.at[f], pz_recv.at[f], z_id(k))

    for f in range(2):
        pool_copy(f).wait()
        pool_z[f] = (pool_mine[f] + pool_core[f].astype(jnp.float32)).astype(jnp.bfloat16)
        for k in range(1, nz):
            pool_out(f, k).start()
        pool_got[f, z] = pool_z[f, z]

    chosen = dot(turned, picked.astype(jnp.bfloat16))
    chosen = (chosen * error).astype(jnp.bfloat16)

    def columns(core):
        return pl.ds(pl.multiple_of(core * half_w, half_w), half_w)

    places = ((out_ref, 0, WIDTH), (gate_ref, 0, deep), (gate_ref, deep, deep))
    CORE, PLANE, PIECE, BACK, WIDE, LAST = range(6)

    def sems(n, stage):
        return sum_send.at[n, stage], sum_recv.at[n, stage]

    def core_copy(n):
        return copy(sums[n][1], sums[n][2], *sems(n, CORE), sibling)

    def core_start(n, part):
        sums[n][1][...] = part.astype(jnp.bfloat16)
        core_copy(n).start()

    def block_of(n):
        return places[n][2] // nr

    def plane_rows(n, k):
        size = block_of(n)
        return pl.ds(pl.multiple_of((rep + k) % nr * size, size), size)

    def core_end(n):
        mine, _, core_got, half, plane_got = sums[n][:5]
        core_copy(n).wait()
        half[...] = (mine[...] + core_got[...].astype(jnp.float32)).astype(jnp.bfloat16)
        for k in range(1, nr):
            copy(half.at[plane_rows(n, k)], plane_got.at[rep], *sems(n, PLANE), plane_id(k)).start()
        plane_got[rep] = half[plane_rows(n, 0), :]

    def plane_all(n):
        size = block_of(n) * (nr - 1)
        return copy(sums[n][3].at[pl.ds(0, size)], sums[n][4].at[pl.ds(0, nr - 1)], *sems(n, PLANE), sibling)

    def piece_spot(n, zz):
        tall = block_of(n) // 2
        return pl.ds(pl.multiple_of(zz // 4 * tall, tall), tall), pl.ds(pl.multiple_of(zz % 4 * LANES, LANES), LANES)

    def plane_end(n):
        plane_got, row_sum, piece_got = sums[n][4:7]
        plane_all(n).wait_recv()
        total = plane_got[0].astype(jnp.float32)
        for k in range(1, nr):
            total += plane_got[k].astype(jnp.float32)
        row_sum[...] = total
        for k in range(1, nz):
            copy(row_sum.at[piece_spot(n, (z + k) % nz)], piece_got.at[z], *sems(n, PIECE), z_id(k)).start()
        piece_got[z] = row_sum[piece_spot(n, z)]

    def piece_all(n):
        spot = sums[n][6].at[pl.ds(0, nz - 1)]
        return copy(spot, spot, *sems(n, PIECE), sibling)

    def piece_end(n):
        piece_got, final = sums[n][6:8]
        piece_all(n).wait_recv()
        total = piece_got[0]
        for k in range(1, nz):
            total += piece_got[k]
        spot = final.at[piece_spot(n, z)]
        spot[...] = total
        for k in range(1, nz):
            copy(spot, spot, *sems(n, BACK), z_id(k)).start()

    def back_all(n):
        spot = sums[n][6].at[pl.ds(0, nz - 1)]
        return copy(spot, spot, *sems(n, BACK), sibling)

    def wide_spot(n, core, k):
        ref, first, _ = places[n]
        size = block_of(n)
        return ref.at[pl.ds(pl.multiple_of(first + (rep + k) % nr * size, size), size), columns(core)]

    def back_end(n):
        back_all(n).wait_recv()
        spot = wide_spot(n, c, 0)
        spot[...] = sums[n][7][...].astype(jnp.bfloat16)
        for k in range(1, nr):
            copy(spot, spot, *sems(n, WIDE), plane_id(k)).start()

    def wide_all(n):
        ref, first, _ = places[n]
        spot = ref.at[pl.ds(first, block_of(n) * (nr - 1)), columns(c)]
        return copy(spot, spot, *sems(n, WIDE), sibling)

    def last_copy(n, core):
        ref, first, size = places[n]
        spot = ref.at[pl.ds(first, size), columns(core)]
        return copy(spot, spot, *sems(n, LAST), sibling)

    def wide_end(n):
        wide_all(n).wait_recv()
        last_copy(n, c).start()

    core_start(0, dot(chosen, items[:, columns(other)]))
    sums[0][0][...] = dot(chosen, items[:, columns(c)])
    core_end(0)

    def pool_all(f):
        spot = pool_got.at[f, pl.ds(0, nz - 1)]
        return copy(spot, spot, pz_send.at[f], pz_recv.at[f], sibling)

    for k in (5, 6, 7):
        loads[k].wait()
    for f in range(2):
        pool_all(f).wait_recv()
        total = pool_got[f, 0].astype(jnp.float32)
        for k in range(1, nz):
            total += pool_got[f, k].astype(jnp.float32)
        pool_t = total.astype(jnp.bfloat16).astype(jnp.float32).T.astype(jnp.bfloat16)
        rows = slice(f * deep, (f + 1) * deep)
        pre = (dot(pool_t, holds[...]) * slope[rows, :].astype(jnp.float32)).astype(jnp.bfloat16)
        core_start(1 + f, dot(pre, packed[:, columns(other)]))
        sums[1 + f][0][...] = dot(pre, packed[:, columns(c)])
        if f == 0:
            plane_end(0)
        else:
            piece_end(0)
        core_end(1 + f)

    plane_end(1)
    back_end(0)
    plane_end(2)
    piece_end(1)
    piece_end(2)
    back_end(1)
    wide_end(0)
    back_end(2)
    wide_end(1)
    wide_end(2)

    spot = users.at[pl.ds(0, nz - 1)]
    copy(spot, spot, user_send, user_recv.at[0], sibling).wait_send()
    all_relays.wait_send()
    for f in range(2):
        pool_all(f).wait_send()
    for n in range(3):
        plane_all(n).wait_send()
        piece_all(n).wait_send()
        back_all(n).wait_send()
        wide_all(n).wait_send()
    for n in range(3):
        last_copy(n, other).wait()


def exchange(imp_user, labels, users, items, w_out, slope, packed, holds):
    nz = lax.axis_size("own") // CORES
    nr = lax.axis_size("rep")
    slots = users.shape[0]
    imps = imp_user.shape[0]
    half_w = D // CORES
    deep = WIDTH // 2
    bf16, f32 = jnp.bfloat16, jnp.float32
    vmem = pl.BlockSpec(memory_space=pltpu.VMEM)
    dma = pltpu.SemaphoreType.DMA
    sums = []
    for size in (WIDTH, deep, deep):
        block = size // nr
        sums += [
            pltpu.VMEM((size, half_w), f32),
            pltpu.VMEM((size, half_w), bf16),
            pltpu.VMEM((size, half_w), bf16),
            pltpu.VMEM((size, half_w), bf16),
            pltpu.VMEM((nr, block, half_w), bf16),
            pltpu.VMEM((block, half_w), f32),
            pltpu.VMEM((nz, block // 2, LANES), f32),
            pltpu.VMEM((block, half_w), f32),
        ]
    return pl.pallas_call(
        functools.partial(exchange_kernel, nz, nr),
        in_specs=[pl.BlockSpec(memory_space=pltpu.HBM)] * 8,
        out_specs=[vmem] * 3,
        out_shape=[
            jax.ShapeDtypeStruct((1, imps), f32),
            jax.ShapeDtypeStruct((WIDTH, D), bf16),
            jax.ShapeDtypeStruct((WIDTH, D), bf16),
        ],
        scratch_shapes=[
            pltpu.VMEM((CORES * nz, slots, D + WIDTH), bf16),
            pltpu.VMEM((1, imps), jnp.int32),
            pltpu.VMEM((1, imps), jnp.int32),
            *[pltpu.VMEM(entry.shape, bf16) for entry in (items, w_out, slope, packed, holds)],
            pltpu.VMEM((2, nz, slots, deep), bf16),
            pltpu.VMEM((2, nz, slots, deep), bf16),
            pltpu.VMEM((2, nz, slots, deep), f32),
            pltpu.VMEM((2, nz, slots, deep), bf16),
            pltpu.VMEM((2, nz, slots, deep), bf16),
            *sums,
            dma((8,)), dma(()), dma((nz * PARTS,)), dma((2,)),
            dma((2,)), dma((2,)), dma((2,)), dma((2,)),
            dma((3, 6)), dma((3, 6)),
        ],
        compiler_params=pltpu.CompilerParams(
            collective_id=0, has_side_effects=True, vmem_limit_bytes=58 * 1024 * 1024
        ),
        name="exchange",
    )(imp_user[None], labels[None], users, items, w_out, slope, packed, holds)


def body(histories, lengths, counts, imp_user, items, labels, w_uvqk, w_out):
    users, slope, packed, holds = forward(histories, lengths, counts, w_uvqk)
    logits, grad_out, grad_gate = exchange(
        imp_user, labels, users, items, w_out, slope, packed, holds
    )
    return (logits[0], grad_out, grad_gate.T)


def solution(mesh):
    return jax.shard_map(
        body,
        mesh=mesh,
        in_specs=(
            P(("own", "rep"), None, None),
            P(("own", "rep")),
            P(("own", "rep")),
            P(("own", "rep")),
            P(("own", "rep"), None),
            P(("own", "rep")),
            P(),
            P(),
        ),
        out_specs=(P(("own", "rep")), P(), P()),
        check_vma=False,
    )
```

time: 107 us -> 101 us (0.944)
  Pallas kernels: 97.7 us -> 94.7 us
  local copies, waits for them, and re-layouts: 8.3 us -> 5.72 us
    pallas_call x2, Pallas kernels: 97.7 us -> 94.7 us  [the longest x1 77 us: exchange(): pl.pallas_call(functools.partial(exchange_kernel, nz, nr), in_specs=[pl.B...]
    unnamed x19 -> x3, local copies, waits for them, and re-layouts: 8.3 us -> 5.72 us
where the time goes in v4:
time: 101 us
  Pallas kernels  94.7 us (94%)
  local copies, waits for them, and re-layouts  5.72 us (6%)
    pallas_call x1, Pallas kernels, exchange(): pl.pallas_call(functools.partial(exchange_kernel, nz, nr), in_specs=[pl.B...  77 us
    pallas_call x1, Pallas kernels, forward(): pl.pallas_call(forward_kernel, in_specs=[hbm] * 4, out_specs=[vmem] + [hb...  17.7 us
    unnamed x3, local copies, waits for them, and re-layouts  5.72 us

profile of v4, /device:TPU:1, one launch (start us, length us, event | category | flops | bytes accessed | tf_op | source)
XLA Modules:
  0.0 101.1 jit_solution(3024735394290570618)
XLA Ops:
  0.6 17.7 %forward.1 = (bf16[32,1536]{1,0:T(8,128)(2,1)}, bf16[512,2048]{1,0:T(8,128)(2,1)}, bf16[2048,1024]{1,0:T(8,128)(2,1)}, bf16[32,2048]{1,0:T(8,128)(2,1)}) custom-call(s32[32]{0:T(128)} %lengths_hbm.1, s32[16]{0:T(128)} %counts_hbm.1, bf16[128,16,1024]{2,1,0:T(8,128)(2,1)} %bitcast.5, bf16[1024,2048]{1,0:T(8,128)(2,1)} %w_hbm.1), custom_call_target="tpu_custom_call" | custom-call | tf_op jit(solution)/shard_map/forward/pallas_call | solution.py:247
  18.3 77.0 %exchange.1 = (f32[1,256]{1,0:T(1,128)}, bf16[512,1024]{1,0:T(8,128)(2,1)}, bf16[512,1024]{1,0:T(8,128)(2,1)}) custom-call(s32[1,256]{1,0:T(1,128)} %bitcast.7, s32[1,256]{1,0:T(1,128)} %bitcast.8, bf16[32,1536]{1,0:T(8,128)(2,1)} %get-tuple-element.10.args_2_, bf16[256,1024]{1,0:T(8,128)(2,1)} %args_3_.4, bf16[512,1024]{1,0:T(8,128)(2,1)} %args_4_.4, ...), custom_call_target="tpu_custom_call" | custom-call | tf_op jit(solution)/shard_map/exchange/pallas_call | solution.py:609
  95.4 2.3 %copy.11 = bf16[1024,512]{1,0:T(8,128)(2,1)} copy(bf16[1024,512]{0,1:T(8,128)(2,1)} %bitcast.6) | data formatting | bytes 2097152
  97.7 1.2 %copy.14 = f32[256]{0:T(256)} copy(f32[256]{0:T(256)} %bitcast.9) | data formatting | bytes 2048
  98.8 2.3 %copy.15 = bf16[512,1024]{1,0:T(8,128)(2,1)} copy(bf16[512,1024]{1,0:T(8,128)(2,1)} %get-tuple-element.24) | data formatting | bytes 2097152

commit v5 on v4

v5 whole, which is shorter than its diff:
```python
import functools

import jax
import jax.numpy as jnp
from jax import lax
from jax.experimental import pallas as pl
from jax.experimental.pallas import tpu as pltpu
from jax.sharding import PartitionSpec as P

D = 1024
HEADS = 4
HEAD = 128
HIST = 64
WIDTH = HEADS * HEAD
BIN = 128
STEP = 512
CORES = 2
LANES = 128
PARTS = 4
MESH = pl.DeviceIdType.MESH

EPS_NORM = 1e-06
EPS_LAYER = 1e-05


def sigmoid(v):
    return 0.5 * jnp.tanh(0.5 * v) + 0.5


def dot(a, b):
    return jnp.dot(a, b, preferred_element_type=jnp.float32)


def dot_t(a, b):
    return lax.dot_general(a, b, (((1,), (1,)), ((), ())), preferred_element_type=jnp.float32)


def forward_kernel(
    lengths_hbm, counts_hbm, h_hbm, w_hbm, both_hbm,
    x, w, user_ref, slope_ref, even, odd, sum_y, lengths, counts, load_sem, h_sem, w_sem, out_sem,
):
    slots = user_ref.shape[0]
    blocks = slots * HIST // STEP
    step_bins = STEP // BIN
    step_slots = STEP // HIST
    linear = (even, odd)

    def block_rows(i):
        return slice(i * STEP, (i + 1) * STEP)

    def part(n):
        return slice(n * WIDTH, (n + 1) * WIDTH)

    h_loads = [
        pltpu.make_async_copy(h_hbm.at[block_rows(i)], x.at[block_rows(i)], h_sem.at[i]) for i in range(blocks)
    ]
    w_loads = [pltpu.make_async_copy(w_hbm.at[:, part(n)], w.at[:, part(n)], w_sem.at[n]) for n in range(4)]
    small = [
        pltpu.make_async_copy(lengths_hbm, lengths, load_sem.at[0]),
        pltpu.make_async_copy(counts_hbm, counts, load_sem.at[1]),
    ]
    h_loads[0].start()
    for load in w_loads:
        load.start()
    for load in small + h_loads[1:]:
        load.start()

    def project(i, n):
        linear[i % 2][:, part(n)] = dot(x[block_rows(i), :], w[:, part(n)])

    def span_of(s):
        return jnp.where(s % 2 < counts[s // 2], lengths[s], 0)

    def one_bin(i, k):
        b = i * step_bins + k
        source = linear[i % 2]
        rows = slice(k * BIN, (k + 1) * BIN)
        first, second = span_of(2 * b), span_of(2 * b + 1)
        feats = x[b * BIN : (b + 1) * BIN, :].astype(jnp.float32)
        half_scale = 0.5 * lax.rsqrt(jnp.mean(feats * feats, -1, keepdims=True) + EPS_NORM)
        row = lax.broadcasted_iota(jnp.int32, (BIN, BIN), 0)
        col = lax.broadcasted_iota(jnp.int32, (BIN, BIN), 1)
        allowed = (
            (col <= row) & ((row < HIST) | (col >= HIST)) & (col < jnp.where(col < HIST, first, HIST + second))
        )
        span = jnp.where(row < HIST, first, second)
        share = jnp.where(row % HIST < span, 1.0 / jnp.maximum(span, 1).astype(jnp.float32), 0.0)
        back = share * half_scale

        def half_of(m, h):
            at = m * WIDTH + h * HEAD
            return source[rows, at : at + HEAD] * half_scale

        attended = []
        for h in range(HEADS):
            value, query, key = [
                (half * jnp.tanh(half) + half).astype(jnp.bfloat16) for half in (half_of(m, h) for m in (1, 2, 3))
            ]
            half = dot_t(query, key) * (0.5 * HEAD ** (-0.5))
            attn = jnp.where(allowed, half * jnp.tanh(half) + half, 0.0).astype(jnp.bfloat16)
            attended.append(dot(attn, value))
        center = jnp.sum(sum(attended), -1, keepdims=True) / WIDTH
        moved = [a - center for a in attended]
        spread = jnp.sum(sum(a * a for a in moved), -1, keepdims=True) / WIDTH
        norm = lax.rsqrt(spread + EPS_LAYER)
        for h in range(HEADS):
            cols = slice(h * HEAD, (h + 1) * HEAD)
            half = half_of(0, h)
            t = jnp.tanh(half)
            normal = moved[h] * norm
            mixed = share * normal * (half * t + half)
            for j in range(2):
                s = 2 * b + j
                sum_y[s : s + 1, cols] = jnp.sum(mixed[j * HIST : (j + 1) * HIST], 0, keepdims=True)
            slope = back * normal * ((1.0 + t) * (1.0 + half * (1.0 - t)))
            slope_ref[cols, b * BIN : (b + 1) * BIN] = slope.T.astype(jnp.bfloat16)

    def pool_x(i):
        slot = lax.broadcasted_iota(jnp.int32, (step_slots, STEP), 0)
        event = lax.broadcasted_iota(jnp.int32, (step_slots, STEP), 1) - slot * HIST
        which = lax.broadcasted_iota(jnp.int32, (step_slots, 1), 0)
        span = jnp.zeros((step_slots, 1), jnp.int32)
        for j in range(step_slots):
            span = jnp.where(which == j, span_of(i * step_slots + j), span)
        live = ((event >= 0) & (event < span)).astype(jnp.bfloat16)
        inverse = 1.0 / jnp.maximum(span, 1).astype(jnp.float32)
        return dot(live, x[block_rows(i), :]) * inverse

    def slope_out(i):
        cols = block_rows(i)
        return pltpu.make_async_copy(slope_ref.at[:, cols], both_hbm.at[0:WIDTH, cols], out_sem.at[i])

    h_loads[0].wait()
    for n in range(4):
        w_loads[n].wait()
        project(0, n)
    for load in small:
        load.wait()
    pooled = []
    for i in range(blocks):
        if i + 1 < blocks:
            h_loads[i + 1].wait()
        for k in range(step_bins):
            if i + 1 < blocks:
                project(i + 1, k)
            one_bin(i, k)
        pooled.append(pool_x(i))
        slope_out(i).start()
    user_ref[:, 0:D] = jnp.concatenate(pooled, 0).astype(jnp.bfloat16)
    user_ref[:, D : D + WIDTH] = sum_y[...].astype(jnp.bfloat16)
    user_out = pltpu.make_async_copy(
        user_ref, both_hbm.at[WIDTH : WIDTH + slots, 0 : D + WIDTH], out_sem.at[blocks]
    )
    user_out.start()
    for i in range(blocks):
        slope_out(i).wait()
    user_out.wait()


def forward(histories, lengths, counts, w_uvqk):
    slots = histories.shape[0]
    tokens = slots * HIST
    blocks = tokens // STEP
    bf16, f32 = jnp.bfloat16, jnp.float32
    hbm = pl.BlockSpec(memory_space=pltpu.HBM)
    dma = pltpu.SemaphoreType.DMA
    return pl.pallas_call(
        forward_kernel,
        in_specs=[hbm] * 4,
        out_specs=hbm,
        out_shape=jax.ShapeDtypeStruct((WIDTH + slots, tokens), bf16),
        scratch_shapes=[
            pltpu.VMEM((tokens, D), bf16),
            pltpu.VMEM(w_uvqk.shape, bf16),
            pltpu.VMEM((slots, D + WIDTH), bf16),
            pltpu.VMEM((WIDTH, tokens), bf16),
            pltpu.VMEM((STEP, 4 * WIDTH), f32),
            pltpu.VMEM((STEP, 4 * WIDTH), f32),
            pltpu.VMEM((slots, WIDTH), f32),
            pltpu.SMEM(lengths.shape, jnp.int32),
            pltpu.SMEM(counts.shape, jnp.int32),
            dma((2,)), dma((blocks,)), dma((4,)), dma((blocks + 1,)),
        ],
        compiler_params=pltpu.CompilerParams(vmem_limit_bytes=58 * 1024 * 1024),
        name="forward",
    )(lengths, counts, histories.reshape(tokens, D), w_uvqk)


def exchange_kernel(
    nz, nr, *args,
):
    loaded = 6
    user_src, label_src, both, items_src, w_src, hist_src = args[:loaded]
    deep, wide = WIDTH, D + WIDTH
    slots = both.shape[0] - deep
    sources = (user_src, label_src, both.at[deep : deep + slots, 0:wide], items_src, w_src, both.at[0:deep], hist_src)
    logit_ref, out_ref, gate_ref = args[loaded : loaded + 3]
    users = args[loaded + 3]
    user_ref, label_ref, items, w_out, slope, hist = args[loaded + 4 : loaded + 10]
    exchange_steps(
        nz, nr, sources, user_ref, label_ref, items, w_out, slope, hist,
        logit_ref, out_ref, gate_ref, users, *args[loaded + 10 :],
    )


def exchange_steps(
    nz, nr, sources, user_ref, label_ref, items, w_out, slope, hist,
    logit_ref, out_ref, gate_ref,
    users, pool_send, pool_core, pool_mine, pool_z, pool_got, pre, *rest,
):
    per_sum = 8
    sums = [rest[n * per_sum : (n + 1) * per_sum] for n in range(3)]
    (
        load_sem, user_send, user_recv, relay_sem, pool_sem, sum_send, sum_recv,
    ) = rest[3 * per_sum :]
    own = lax.axis_index("own")
    rep = lax.axis_index("rep")
    z, c = own // CORES, own % CORES
    other = 1 - c
    slots = users.shape[1]
    side = nz * slots
    half_w = D // CORES
    part_w = half_w // 2

    targets = (user_ref, label_ref, users.at[c * nz + z], items, w_out, slope, hist)
    loads = [
        pltpu.make_async_copy(source, target, load_sem.at[k])
        for k, (source, target) in enumerate(zip(sources, targets))
    ]
    for k in (2, 3, 4, 0, 1, 5, 6):
        loads[k].start()

    def z_id(k):
        return ((z + k) % nz * CORES + c, rep)

    def plane_id(k):
        return (own, (rep + k) % nr)

    sibling = (z * CORES + other, rep)

    def copy(source, target, send, recv, device):
        return pltpu.make_async_remote_copy(
            src_ref=source, dst_ref=target, send_sem=send, recv_sem=recv,
            device_id=device, device_id_type=MESH,
        )

    def signal(device):
        pl.semaphore_signal(barrier, inc=1, device_id=device, device_id_type=MESH)

    barrier = pltpu.get_barrier_semaphore()
    for k in range(1, nz):
        signal(z_id(k))
    for k in range(1, nr):
        signal(plane_id(k))
    signal(sibling)
    pl.semaphore_wait(barrier, nz - 1 + nr - 1 + 1)

    loads[2].wait()
    reach = nz // 2
    width = (D + WIDTH) // PARTS
    ends = (z_id(1), z_id(nz - 1))

    def origin(way, step):
        return (z + nz - step if way == 0 else z + step) % nz

    def hop(way, step, part):
        spot = users.at[c * nz + origin(way, step), :, part * width : (part + 1) * width]
        return copy(spot, spot, user_send, user_recv.at[(way * reach + step) * PARTS + part], ends[way])

    def landed(way, step, part):
        spot = users.at[c * nz + origin(way, step + 1), :, part * width : (part + 1) * width]
        copy(spot, spot, user_send, user_recv.at[(way * reach + step) * PARTS + part], ends[way]).wait_recv()

    def goes(way, step, part):
        return step < reach - 1 or part % 2 == way

    def user_relay(zz):
        spot = users.at[c * nz + zz]
        return copy(spot, spot, relay_sem.at[0], relay_sem.at[1], sibling)

    for part in range(PARTS):
        for way in range(2):
            hop(way, 0, part).start()
    user_relay(z).start()
    loads[3].wait()
    loads[4].wait()
    item_w = dot_t(items[...], w_out[...]).astype(jnp.bfloat16)
    for step in range(reach):
        for part in range(PARTS):
            for way in range(2):
                if goes(way, step, part):
                    landed(way, step, part)
                if step + 1 < reach and goes(way, step + 1, part):
                    hop(way, step + 1, part).start()
        user_relay(origin(0, step + 1)).start()
        if step + 1 < reach:
            user_relay(origin(1, step + 1)).start()
    all_relays = copy(
        users.at[pl.ds(c * nz, nz)], users.at[pl.ds(other * nz, nz)], relay_sem.at[0], relay_sem.at[1], sibling
    )
    loads[0].wait()
    loads[1].wait()
    all_relays.wait_recv()

    index = user_ref[...]
    source = (index % slots) // 2
    place = (source % CORES) * side + (source // CORES) * slots + index // slots * 2 + index % 2
    table = dot_t(users[:, :, 0:D].reshape(2 * side, D), items[...]) + dot_t(
        users[:, :, D : D + WIDTH].reshape(2 * side, WIDTH), item_w
    )
    imps = index.shape[1]
    picked = lax.broadcasted_iota(jnp.int32, (2 * side, imps), 0) == place
    logits = jnp.sum(jnp.where(picked, table, 0.0), 0, keepdims=True)
    logit_ref[...] = logits
    error = sigmoid(logits) - label_ref[...].astype(jnp.float32)

    line = lax.broadcasted_iota(jnp.int32, (side, imps), 0)

    def pool_side(core):
        weight = jnp.where(line + core * side == place, error, 0.0).astype(jnp.bfloat16)
        return dot(weight, item_w).reshape(nz, slots, WIDTH)

    pool_send[...] = pool_side(other).astype(jnp.bfloat16)
    pool_copy = copy(pool_send, pool_core, pool_sem.at[0], pool_sem.at[1], sibling)
    pool_copy.start()
    pool_mine[...] = pool_side(c)
    turned = users[:, :, D : D + WIDTH].reshape(2 * side, WIDTH).astype(jnp.float32).T.astype(jnp.bfloat16)
    pool_copy.wait()
    pool_z[...] = (pool_mine[...] + pool_core[...].astype(jnp.float32)).astype(jnp.bfloat16)
    for k in range(1, nz):
        copy(pool_z.at[(z + k) % nz], pool_got.at[z], pool_sem.at[2], pool_sem.at[3], z_id(k)).start()
    pool_got[z] = pool_z[z]

    chosen = dot(turned, picked.astype(jnp.bfloat16))
    chosen = (chosen * error).astype(jnp.bfloat16)

    def columns(core, first=0, size=half_w):
        step = min(size, part_w)
        return pl.ds(pl.multiple_of(core * half_w + first, step), size)

    places = ((out_ref, 0, half_w), (gate_ref, 0, part_w), (gate_ref, part_w, part_w))
    block = WIDTH // nr
    CORE, PLANE, PIECE, BACK, WIDE, LAST = range(6)

    def sems(n, stage):
        return sum_send.at[n, stage], sum_recv.at[n, stage]

    def core_copy(n):
        return copy(sums[n][1], sums[n][2], *sems(n, CORE), sibling)

    def core_start(n, part):
        sums[n][1][...] = part.astype(jnp.bfloat16)
        core_copy(n).start()

    def plane_rows(k):
        return pl.ds(pl.multiple_of((rep + k) % nr * block, block), block)

    def core_end(n):
        mine, _, core_got, half, plane_got = sums[n][:5]
        core_copy(n).wait()
        half[...] = (mine[...] + core_got[...].astype(jnp.float32)).astype(jnp.bfloat16)
        for k in range(1, nr):
            copy(half.at[plane_rows(k)], plane_got.at[rep], *sems(n, PLANE), plane_id(k)).start()
        plane_got[rep] = half[plane_rows(0), :]

    def plane_all(n):
        return copy(sums[n][3].at[pl.ds(0, block * (nr - 1))], sums[n][4].at[pl.ds(0, nr - 1)], *sems(n, PLANE), sibling)

    def piece_spot(n, zz):
        across = places[n][2] // LANES
        tall = block * across // nz
        return (
            pl.ds(pl.multiple_of(zz // across * tall, tall), tall),
            pl.ds(pl.multiple_of(zz % across * LANES, LANES), LANES),
        )

    def plane_end(n):
        plane_got, row_sum, piece_got = sums[n][4:7]
        plane_all(n).wait_recv()
        total = plane_got[0].astype(jnp.float32)
        for k in range(1, nr):
            total += plane_got[k].astype(jnp.float32)
        row_sum[...] = total
        for k in range(1, nz):
            copy(row_sum.at[piece_spot(n, (z + k) % nz)], piece_got.at[z], *sems(n, PIECE), z_id(k)).start()
        piece_got[z] = row_sum[piece_spot(n, z)]

    def piece_all(n):
        spot = sums[n][6].at[pl.ds(0, nz - 1)]
        return copy(spot, spot, *sems(n, PIECE), sibling)

    def piece_end(n):
        piece_got, final = sums[n][6:8]
        piece_all(n).wait_recv()
        total = piece_got[0]
        for k in range(1, nz):
            total += piece_got[k]
        spot = final.at[piece_spot(n, z)]
        spot[...] = total
        for k in range(1, nz):
            copy(spot, spot, *sems(n, BACK), z_id(k)).start()

    def back_all(n):
        spot = sums[n][6].at[pl.ds(0, nz - 1)]
        return copy(spot, spot, *sems(n, BACK), sibling)

    def wide_spot(n, core, k):
        ref, first, size = places[n]
        return ref.at[plane_rows(k), columns(core, first, size)]

    def back_end(n):
        back_all(n).wait_recv()
        spot = wide_spot(n, c, 0)
        spot[...] = sums[n][7][...].astype(jnp.bfloat16)
        for k in range(1, nr):
            copy(spot, spot, *sems(n, WIDE), plane_id(k)).start()

    def wide_all(n):
        ref, first, size = places[n]
        spot = ref.at[pl.ds(0, block * (nr - 1)), columns(c, first, size)]
        return copy(spot, spot, *sems(n, WIDE), sibling)

    def last_copy(n, core):
        ref, first, size = places[n]
        spot = ref.at[:, columns(core, first, size)]
        return copy(spot, spot, *sems(n, LAST), sibling)

    def wide_end(n):
        wide_all(n).wait_recv()
        last_copy(n, c).start()

    core_start(0, dot(chosen, items[:, columns(other)]))
    sums[0][0][...] = dot(chosen, items[:, columns(c)])
    core_end(0)

    pool_spot = pool_got.at[pl.ds(0, nz - 1)]
    pool_all = copy(pool_spot, pool_spot, pool_sem.at[2], pool_sem.at[3], sibling)
    loads[5].wait()
    loads[6].wait()
    pool_all.wait_recv()
    total = pool_got[0].astype(jnp.float32)
    for k in range(1, nz):
        total += pool_got[k].astype(jnp.float32)
    pool_t = total.astype(jnp.bfloat16).astype(jnp.float32).T.astype(jnp.bfloat16)
    tokens = slots * HIST
    slot = lax.broadcasted_iota(jnp.int32, (slots, tokens), 0)
    event = lax.broadcasted_iota(jnp.int32, (slots, tokens), 1)
    holds = (event // HIST == slot).astype(jnp.bfloat16)
    pre[...] = (dot(pool_t, holds) * slope[...].astype(jnp.float32)).astype(jnp.bfloat16)
    gate_part = dot(pre[...], hist[:, columns(other)])
    core_start(1, gate_part[:, 0:part_w])
    core_start(2, gate_part[:, part_w:half_w])
    plane_end(0)
    gate_part = dot(pre[...], hist[:, columns(c)])
    sums[1][0][...] = gate_part[:, 0:part_w]
    core_end(1)
    sums[2][0][...] = gate_part[:, part_w:half_w]
    core_end(2)
    piece_end(0)
    plane_end(1)
    back_end(0)
    plane_end(2)
    piece_end(1)
    piece_end(2)
    back_end(1)
    wide_end(0)
    back_end(2)
    wide_end(1)
    wide_end(2)

    spot = users.at[pl.ds(0, nz - 1)]
    copy(spot, spot, user_send, user_recv.at[0], sibling).wait_send()
    all_relays.wait_send()
    pool_all.wait_send()
    for n in range(3):
        plane_all(n).wait_send()
        piece_all(n).wait_send()
        back_all(n).wait_send()
        wide_all(n).wait_send()
    for n in range(3):
        last_copy(n, other).wait()


def exchange(imp_user, labels, both, items, w_out, hist):
    nz = lax.axis_size("own") // CORES
    nr = lax.axis_size("rep")
    slots = both.shape[0] - WIDTH
    tokens = both.shape[1]
    imps = imp_user.shape[0]
    half_w = D // CORES
    bf16, f32 = jnp.bfloat16, jnp.float32
    vmem = pl.BlockSpec(memory_space=pltpu.VMEM)
    dma = pltpu.SemaphoreType.DMA
    sums = []
    for size in (half_w, half_w // 2, half_w // 2):
        block = WIDTH // nr
        sums += [
            pltpu.VMEM((WIDTH, size), f32),
            pltpu.VMEM((WIDTH, size), bf16),
            pltpu.VMEM((WIDTH, size), bf16),
            pltpu.VMEM((WIDTH, size), bf16),
            pltpu.VMEM((nr, block, size), bf16),
            pltpu.VMEM((block, size), f32),
            pltpu.VMEM((nz, block * size // nz // LANES, LANES), f32),
            pltpu.VMEM((block, size), f32),
        ]
    return pl.pallas_call(
        functools.partial(exchange_kernel, nz, nr),
        in_specs=[pl.BlockSpec(memory_space=pltpu.HBM)] * 6,
        out_specs=[vmem] * 3,
        out_shape=[
            jax.ShapeDtypeStruct((1, imps), f32),
            jax.ShapeDtypeStruct((WIDTH, D), bf16),
            jax.ShapeDtypeStruct((WIDTH, D), bf16),
        ],
        scratch_shapes=[
            pltpu.VMEM((CORES * nz, slots, D + WIDTH), bf16),
            pltpu.VMEM((1, imps), jnp.int32),
            pltpu.VMEM((1, imps), jnp.int32),
            *[pltpu.VMEM(shape, bf16) for shape in (items.shape, w_out.shape, (WIDTH, tokens), hist.shape)],
            pltpu.VMEM((nz, slots, WIDTH), bf16),
            pltpu.VMEM((nz, slots, WIDTH), bf16),
            pltpu.VMEM((nz, slots, WIDTH), f32),
            pltpu.VMEM((nz, slots, WIDTH), bf16),
            pltpu.VMEM((nz, slots, WIDTH), bf16),
            pltpu.VMEM((WIDTH, tokens), bf16),
            *sums,
            dma((7,)), dma(()), dma((nz * PARTS,)), dma((2,)),
            dma((4,)),
            dma((3, 6)), dma((3, 6)),
        ],
        compiler_params=pltpu.CompilerParams(
            collective_id=0, has_side_effects=True, vmem_limit_bytes=50 * 1024 * 1024
        ),
        name="exchange",
    )(imp_user[None], labels[None], both, items, w_out, hist)


def body(histories, lengths, counts, imp_user, items, labels, w_uvqk, w_out):
    both = forward(histories, lengths, counts, w_uvqk)
    logits, grad_out, grad_gate = exchange(
        imp_user, labels, both, items, w_out, histories.reshape(-1, D)
    )
    return (logits[0], grad_out, grad_gate.T)


def solution(mesh):
    return jax.shard_map(
        body,
        mesh=mesh,
        in_specs=(
            P(("own", "rep"), None, None),
            P(("own", "rep")),
            P(("own", "rep")),
            P(("own", "rep")),
            P(("own", "rep"), None),
            P(("own", "rep")),
            P(),
            P(),
        ),
        out_specs=(P(("own", "rep")), P(), P()),
        check_vma=False,
    )
```

time: 101 us -> 95.9 us (0.950)
  local copies, waits for them, and re-layouts: 5.72 us -> 2.87 us
  Pallas kernels: 94.7 us -> 92.3 us
    pallas_call x1, Pallas kernels: 77 us -> 69 us  [exchange(): pl.pallas_call(functools.partial(exchange_kernel, nz, nr), in_specs=[pl.B...]
    pallas_call x1, Pallas kernels: 17.7 us -> 23.3 us  [forward(): pl.pallas_call(forward_kernel, in_specs=[hbm] * 4, out_specs=hbm, out_sha...]
    unnamed x3 -> x11, local copies, waits for them, and re-layouts: 5.72 us -> 2.87 us
where the time goes in v5:
time: 95.9 us
  Pallas kernels  92.3 us (96%)
  local copies, waits for them, and re-layouts  2.87 us (3%)
    pallas_call x1, Pallas kernels, exchange(): pl.pallas_call(functools.partial(exchange_kernel, nz, nr), in_specs=[pl.B...  69 us
    pallas_call x1, Pallas kernels, forward(): pl.pallas_call(forward_kernel, in_specs=[hbm] * 4, out_specs=hbm, out_sha...  23.3 us
    unnamed x11, local copies, waits for them, and re-layouts  2.87 us

profile of v5, /device:TPU:1, one launch (start us, length us, event | category | flops | bytes accessed | tf_op | source)
XLA Modules:
  0.0 95.9 jit_solution(14598183819865241221)
XLA Ops:
  0.6 0.0 copy-start
  0.6 0.0 copy-start.1
  0.7 0.0 copy-start.2
  0.7 0.0 copy-start.3
  0.7 23.3 %forward.1.args_2_ = bf16[544,2048]{1,0:T(8,128)(2,1)} custom-call(s32[32]{0:T(128)} %lengths_hbm.1, s32[16]{0:T(128)} %counts_hbm.1, bf16[2048,1024]{1,0:T(8,128)(2,1)} %bitcast.9, bf16[1024,2048]{1,0:T(8,128)(2,1)} %w_hbm.1), custom_call_target="tpu_custom_call" | custom-call | tf_op jit(solution)/shard_map/forward/pallas_call | solution.py:167
  24.0 0.0 copy-done
  24.0 0.0 copy-done.1
  24.0 0.0 copy-done.2
  24.0 0.0 copy-done.3
  24.0 69.0 %exchange.1 = (f32[1,256]{1,0:T(1,128)S(1)}, bf16[512,1024]{1,0:T(8,128)(2,1)S(1)}, bf16[512,1024]{1,0:T(8,128)(2,1)S(1)}) custom-call(s32[1,256]{1,0:T(1,128)S(1)} %bitcast.6, s32[1,256]{1,0:T(1,128)S(1)} %bitcast.7, bf16[544,2048]{1,0:T(8,128)(2,1)} %forward.1.args_2_, bf16[256,1024]{1,0:T(8,128)(2,1)S(1)} %copy-done.1, bf16[512,1024]{1,0:T(8,128)(2,1)S(1)} %copy-done, ...), custom_call_target="tpu_custom_call" | custom-call | tf_op jit(solution)/shard_map/exchange/pallas_call | solution.py:507
  93.0 1.3 %copy.11 = bf16[1024,512]{1,0:T(8,128)(2,1)} copy(bf16[1024,512]{0,1:T(8,128)(2,1)S(1)} %bitcast.5) | data formatting | bytes 2097152
  94.3 0.6 copy.14
  94.9 1.0 %copy.15 = bf16[512,1024]{1,0:T(8,128)(2,1)} copy(bf16[512,1024]{1,0:T(8,128)(2,1)S(1)} %get-tuple-element.16) | data formatting | bytes 2097152
Async XLA Ops:
  0.6 23.3 %copy-start = (bf16[512,1024]{1,0:T(8,128)(2,1)S(1)}, bf16[512,1024]{1,0:T(8,128)(2,1)}, u32[]{:S(2)}) copy-start(bf16[512,1024]{1,0:T(8,128)(2,1)} %args_4_.4) | copy-start | bytes 3145732
  0.6 23.3 %copy-start.1 = (bf16[256,1024]{1,0:T(8,128)(2,1)S(1)}, bf16[256,1024]{1,0:T(8,128)(2,1)}, u32[]{:S(2)}) copy-start(bf16[256,1024]{1,0:T(8,128)(2,1)} %args_3_.4) | copy-start | bytes 1572868
  0.7 23.3 %copy-start.2 = (s32[256]{0:T(256)S(1)}, s32[256]{0:T(256)}, u32[]{:S(2)}) copy-start(s32[256]{0:T(256)} %param.11) | copy-start | bytes 3076
  0.7 23.3 %copy-start.3 = (s32[256]{0:T(256)S(1)}, s32[256]{0:T(256)}, u32[]{:S(2)}) copy-start(s32[256]{0:T(256)} %param.13) | copy-start | bytes 3076

commit v6 on v5

v6 whole, which is shorter than its diff:
```python
import functools

import jax
import jax.numpy as jnp
from jax import lax
from jax.experimental import pallas as pl
from jax.experimental.pallas import tpu as pltpu
from jax.sharding import PartitionSpec as P

D = 1024
HEADS = 4
HEAD = 128
HIST = 64
WIDTH = HEADS * HEAD
BIN = 128
STEP = 512
CORES = 2
LANES = 128
PARTS = 4
MESH = pl.DeviceIdType.MESH

EPS_NORM = 1e-06
EPS_LAYER = 1e-05


def sigmoid(v):
    return 0.5 * jnp.tanh(0.5 * v) + 0.5


def dot(a, b):
    return jnp.dot(a, b, preferred_element_type=jnp.float32)


def dot_t(a, b):
    return lax.dot_general(a, b, (((1,), (1,)), ((), ())), preferred_element_type=jnp.float32)


def step_kernel(
    nz, nr, imp_hbm, label_hbm, lengths_hbm, counts_hbm, items_hbm, w_out_hbm, w_hbm, h_hbm,
    logit_hbm, out_hbm, gate_hbm,
    user_ref, label_ref, items, w_out, w, x, slope, even, odd, sum_y, logit_ref, out_ref, gate_ref,
    users, pool_send, pool_core, pool_mine, pool_z, pool_got, pre, *rest,
):
    per_sum = 8
    sums = [rest[n * per_sum : (n + 1) * per_sum] for n in range(3)]
    (
        lengths, counts, load_sem, h_sem, w_sem, out_sem,
        user_send, user_recv, relay_sem, pool_sem, sum_send, sum_recv,
    ) = rest[3 * per_sum :]
    own = lax.axis_index("own")
    rep = lax.axis_index("rep")
    z, c = own // CORES, own % CORES
    other = 1 - c
    slots = users.shape[1]
    side = nz * slots
    half_w = D // CORES
    part_w = half_w // 2
    blocks = slots * HIST // STEP
    step_bins = STEP // BIN
    step_slots = STEP // HIST
    linear = (even, odd)

    def block_rows(i):
        return slice(i * STEP, (i + 1) * STEP)

    def part(n):
        return slice(n * WIDTH, (n + 1) * WIDTH)

    h_loads = [
        pltpu.make_async_copy(h_hbm.at[block_rows(i)], x.at[block_rows(i)], h_sem.at[i]) for i in range(blocks)
    ]
    w_loads = [pltpu.make_async_copy(w_hbm.at[:, part(n)], w.at[:, part(n)], w_sem.at[n]) for n in range(4)]
    loads = [
        pltpu.make_async_copy(source, target, load_sem.at[k])
        for k, (source, target) in enumerate(
            (
                (lengths_hbm, lengths), (counts_hbm, counts), (w_out_hbm, w_out), (items_hbm, items),
                (imp_hbm, user_ref), (label_hbm, label_ref),
            )
        )
    ]
    h_loads[0].start()
    for load in w_loads:
        load.start()
    for load in loads[:2] + h_loads[1:] + loads[2:]:
        load.start()

    def z_id(k):
        return ((z + k) % nz * CORES + c, rep)

    def plane_id(k):
        return (own, (rep + k) % nr)

    sibling = (z * CORES + other, rep)

    def copy(source, target, send, recv, device):
        return pltpu.make_async_remote_copy(
            src_ref=source, dst_ref=target, send_sem=send, recv_sem=recv,
            device_id=device, device_id_type=MESH,
        )

    def signal(device):
        pl.semaphore_signal(barrier, inc=1, device_id=device, device_id_type=MESH)

    barrier = pltpu.get_barrier_semaphore()
    for k in range(1, nz):
        signal(z_id(k))
    for k in range(1, nr):
        signal(plane_id(k))
    signal(sibling)

    at = c * nz + z
    reach = nz // 2
    some = slots // 2
    ends = (z_id(1), z_id(nz - 1))

    def origin(way, step):
        return (z + nz - step if way == 0 else z + step) % nz

    def piece_of(block, piece):
        rows = pl.ds(piece % 2 * some, some)
        return users.at[block, rows, 0:D] if piece < 2 else users.at[block, rows, D : D + WIDTH]

    def hop(way, step, piece):
        spot = piece_of(c * nz + origin(way, step), piece)
        return copy(spot, spot, user_send, user_recv.at[(way * reach + step) * PARTS + piece], ends[way])

    def landed(way, step, piece):
        spot = piece_of(c * nz + origin(way, step + 1), piece)
        copy(spot, spot, user_send, user_recv.at[(way * reach + step) * PARTS + piece], ends[way]).wait_recv()

    def goes(way, step, piece):
        return step < reach - 1 or piece % 2 == way

    def forward_hop(step, piece):
        for way in range(2):
            if goes(way, step, piece):
                landed(way, step, piece)
            if step + 1 < reach and goes(way, step + 1, piece):
                hop(way, step + 1, piece).start()

    def user_relay(zz):
        spot = users.at[c * nz + zz, :, 0:D]
        return copy(spot, spot, relay_sem.at[0], relay_sem.at[1], sibling)

    def project(i, n):
        linear[i % 2][:, part(n)] = dot(x[block_rows(i), :], w[:, part(n)])

    def span_of(s):
        return jnp.where(s % 2 < counts[s // 2], lengths[s], 0)

    def one_bin(i, k):
        b = i * step_bins + k
        source = linear[i % 2]
        rows = slice(k * BIN, (k + 1) * BIN)
        first, second = span_of(2 * b), span_of(2 * b + 1)
        feats = x[b * BIN : (b + 1) * BIN, :].astype(jnp.float32)
        half_scale = 0.5 * lax.rsqrt(jnp.mean(feats * feats, -1, keepdims=True) + EPS_NORM)
        row = lax.broadcasted_iota(jnp.int32, (BIN, BIN), 0)
        col = lax.broadcasted_iota(jnp.int32, (BIN, BIN), 1)
        allowed = (
            (col <= row) & ((row < HIST) | (col >= HIST)) & (col < jnp.where(col < HIST, first, HIST + second))
        )
        span = jnp.where(row < HIST, first, second)
        share = jnp.where(row % HIST < span, 1.0 / jnp.maximum(span, 1).astype(jnp.float32), 0.0)
        back = share * half_scale

        def half_of(m, h):
            at = m * WIDTH + h * HEAD
            return source[rows, at : at + HEAD] * half_scale

        attended = []
        for h in range(HEADS):
            value, query, key = [
                (half * jnp.tanh(half) + half).astype(jnp.bfloat16) for half in (half_of(m, h) for m in (1, 2, 3))
            ]
            half = dot_t(query, key) * (0.5 * HEAD ** (-0.5))
            attn = jnp.where(allowed, half * jnp.tanh(half) + half, 0.0).astype(jnp.bfloat16)
            attended.append(dot(attn, value))
        center = jnp.sum(sum(attended), -1, keepdims=True) / WIDTH
        moved = [a - center for a in attended]
        spread = jnp.sum(sum(a * a for a in moved), -1, keepdims=True) / WIDTH
        norm = lax.rsqrt(spread + EPS_LAYER)
        for h in range(HEADS):
            cols = slice(h * HEAD, (h + 1) * HEAD)
            half = half_of(0, h)
            t = jnp.tanh(half)
            normal = moved[h] * norm
            mixed = share * normal * (half * t + half)
            for j in range(2):
                s = 2 * b + j
                sum_y[s : s + 1, cols] = jnp.sum(mixed[j * HIST : (j + 1) * HIST], 0, keepdims=True)
            falls = back * normal * ((1.0 + t) * (1.0 + half * (1.0 - t)))
            slope[cols, b * BIN : (b + 1) * BIN] = falls.T.astype(jnp.bfloat16)

    def pool_x(i):
        slot = lax.broadcasted_iota(jnp.int32, (step_slots, STEP), 0)
        event = lax.broadcasted_iota(jnp.int32, (step_slots, STEP), 1) - slot * HIST
        which = lax.broadcasted_iota(jnp.int32, (step_slots, 1), 0)
        span = jnp.zeros((step_slots, 1), jnp.int32)
        for j in range(step_slots):
            span = jnp.where(which == j, span_of(i * step_slots + j), span)
        live = ((event >= 0) & (event < span)).astype(jnp.bfloat16)
        inverse = 1.0 / jnp.maximum(span, 1).astype(jnp.float32)
        return dot(live, x[block_rows(i), :]) * inverse

    def embed(g):
        rows = slice(g * some, (g + 1) * some)
        py = sum_y[rows, :].astype(jnp.bfloat16)
        users[at, rows, D : D + WIDTH] = py
        px = jnp.concatenate(pooled[g * blocks // 2 : (g + 1) * blocks // 2], 0)
        users[at, rows, 0:D] = (px + dot(py, w_out[...])).astype(jnp.bfloat16)
        for piece in (g, g + 2):
            for way in range(2):
                hop(way, 0, piece).start()

    h_loads[0].wait()
    for n in range(4):
        w_loads[n].wait()
        project(0, n)
    for load in loads[:3]:
        load.wait()
    pooled = []
    for i in range(blocks):
        if i + 1 < blocks:
            h_loads[i + 1].wait()
        for k in range(step_bins):
            if i + 1 < blocks:
                project(i + 1, k)
            one_bin(i, k)
            if i == blocks - 1 and k == step_bins // 2 - 1:
                for piece in (0, 2):
                    forward_hop(1, piece)
        pooled.append(pool_x(i))
        if i == blocks // 2 - 1:
            pl.semaphore_wait(barrier, nz - 1 + nr - 1 + 1)
            embed(0)
        elif i == blocks - 2:
            for piece in (0, 2):
                forward_hop(0, piece)
    embed(1)
    user_relay(z).start()
    for piece in (0, 2):
        forward_hop(2, piece)
    for load in loads[3:]:
        load.wait()
    item_w = dot_t(items[...], w_out[...]).astype(jnp.bfloat16)
    for step in range(reach):
        forward_hop(step, 1)
        if step == reach - 1:
            forward_hop(step, 0)
        user_relay(origin(0, step + 1)).start()
        if step + 1 < reach:
            user_relay(origin(1, step + 1)).start()
    forward_hop(reach - 1, 2)
    forward_hop(0, 3)

    def line_of(core, first, size):
        return users.at[pl.ds(core * nz, nz), :, first : first + size]

    all_relays = copy(line_of(c, 0, D), line_of(other, 0, D), relay_sem.at[0], relay_sem.at[1], sibling)
    all_relays.wait_recv()
    forward_hop(1, 3)

    index = user_ref[...]
    source = (index % slots) // 2
    place = (source % CORES) * side + (source // CORES) * slots + index // slots * 2 + index % 2
    table = dot_t(users[:, :, 0:D].reshape(2 * side, D), items[...])
    imps = index.shape[1]
    picked = lax.broadcasted_iota(jnp.int32, (2 * side, imps), 0) == place
    logits = jnp.sum(jnp.where(picked, table, 0.0), 0, keepdims=True)
    logit_ref[...] = logits
    logit_out = pltpu.make_async_copy(logit_ref, logit_hbm, out_sem.at[0])
    logit_out.start()
    forward_hop(2, 3)
    error = sigmoid(logits) - label_ref[...].astype(jnp.float32)

    line = lax.broadcasted_iota(jnp.int32, (side, imps), 0)

    def pool_side(core):
        weight = jnp.where(line + core * side == place, error, 0.0).astype(jnp.bfloat16)
        return dot(weight, item_w).reshape(nz, slots, WIDTH)

    pool_send[...] = pool_side(other).astype(jnp.bfloat16)
    pool_copy = copy(pool_send, pool_core, pool_sem.at[0], pool_sem.at[1], sibling)
    pool_copy.start()
    pool_mine[...] = pool_side(c)
    forward_hop(reach - 1, 3)
    py_relay = copy(
        line_of(c, D, WIDTH), line_of(c, D, WIDTH), relay_sem.at[2], relay_sem.at[3], sibling
    )
    py_relay.start()
    pool_copy.wait()
    pool_z[...] = (pool_mine[...] + pool_core[...].astype(jnp.float32)).astype(jnp.bfloat16)
    for k in range(1, nz):
        copy(pool_z.at[(z + k) % nz], pool_got.at[z], pool_sem.at[2], pool_sem.at[3], z_id(k)).start()
    pool_got[z] = pool_z[z]

    copy(line_of(c, D, WIDTH), line_of(other, D, WIDTH), relay_sem.at[2], relay_sem.at[3], sibling).wait_recv()
    turned = users[:, :, D : D + WIDTH].reshape(2 * side, WIDTH).astype(jnp.float32).T.astype(jnp.bfloat16)
    chosen = dot(turned, picked.astype(jnp.bfloat16))
    chosen = (chosen * error).astype(jnp.bfloat16)

    def columns(core, first=0, size=half_w):
        step = min(size, part_w)
        return pl.ds(pl.multiple_of(core * half_w + first, step), size)

    places = ((out_ref, 0, half_w), (gate_ref, 0, part_w), (gate_ref, part_w, part_w))
    block = WIDTH // nr
    CORE, PLANE, PIECE, BACK, WIDE, LAST = range(6)

    def sems(n, stage):
        return sum_send.at[n, stage], sum_recv.at[n, stage]

    def core_copy(n):
        return copy(sums[n][1], sums[n][2], *sems(n, CORE), sibling)

    def core_start(n, part):
        sums[n][1][...] = part.astype(jnp.bfloat16)
        core_copy(n).start()

    def plane_rows(k):
        return pl.ds(pl.multiple_of((rep + k) % nr * block, block), block)

    def core_end(n):
        mine, _, core_got, half, plane_got = sums[n][:5]
        core_copy(n).wait()
        half[...] = (mine[...] + core_got[...].astype(jnp.float32)).astype(jnp.bfloat16)
        for k in range(1, nr):
            copy(half.at[plane_rows(k)], plane_got.at[rep], *sems(n, PLANE), plane_id(k)).start()
        plane_got[rep] = half[plane_rows(0), :]

    def plane_all(n):
        return copy(sums[n][3].at[pl.ds(0, block * (nr - 1))], sums[n][4].at[pl.ds(0, nr - 1)], *sems(n, PLANE), sibling)

    def piece_spot(n, zz):
        across = places[n][2] // LANES
        tall = block * across // nz
        return (
            pl.ds(pl.multiple_of(zz // across * tall, tall), tall),
            pl.ds(pl.multiple_of(zz % across * LANES, LANES), LANES),
        )

    def plane_end(n):
        plane_got, row_sum, piece_got = sums[n][4:7]
        plane_all(n).wait_recv()
        total = plane_got[0].astype(jnp.float32)
        for k in range(1, nr):
            total += plane_got[k].astype(jnp.float32)
        row_sum[...] = total
        for k in range(1, nz):
            copy(row_sum.at[piece_spot(n, (z + k) % nz)], piece_got.at[z], *sems(n, PIECE), z_id(k)).start()
        piece_got[z] = row_sum[piece_spot(n, z)]

    def piece_all(n):
        spot = sums[n][6].at[pl.ds(0, nz - 1)]
        return copy(spot, spot, *sems(n, PIECE), sibling)

    def piece_end(n):
        piece_got, final = sums[n][6:8]
        piece_all(n).wait_recv()
        total = piece_got[0]
        for k in range(1, nz):
            total += piece_got[k]
        spot = final.at[piece_spot(n, z)]
        spot[...] = total
        for k in range(1, nz):
            copy(spot, spot, *sems(n, BACK), z_id(k)).start()

    def back_all(n):
        spot = sums[n][6].at[pl.ds(0, nz - 1)]
        return copy(spot, spot, *sems(n, BACK), sibling)

    def wide_spot(n, core, k):
        ref, first, size = places[n]
        return ref.at[plane_rows(k), columns(core, first, size)]

    def back_end(n):
        back_all(n).wait_recv()
        spot = wide_spot(n, c, 0)
        spot[...] = sums[n][7][...].astype(jnp.bfloat16)
        for k in range(1, nr):
            copy(spot, spot, *sems(n, WIDE), plane_id(k)).start()

    def wide_all(n):
        ref, first, size = places[n]
        spot = ref.at[pl.ds(0, block * (nr - 1)), columns(c, first, size)]
        return copy(spot, spot, *sems(n, WIDE), sibling)

    def last_copy(n, core):
        ref, first, size = places[n]
        spot = ref.at[:, columns(core, first, size)]
        return copy(spot, spot, *sems(n, LAST), sibling)

    def wide_end(n):
        wide_all(n).wait_recv()
        last_copy(n, c).start()

    core_start(0, dot(chosen, items[:, columns(other)]))
    sums[0][0][...] = dot(chosen, items[:, columns(c)])
    core_end(0)

    pool_spot = pool_got.at[pl.ds(0, nz - 1)]
    pool_all = copy(pool_spot, pool_spot, pool_sem.at[2], pool_sem.at[3], sibling)
    pool_all.wait_recv()
    total = pool_got[0].astype(jnp.float32)
    for k in range(1, nz):
        total += pool_got[k].astype(jnp.float32)
    pool_t = total.astype(jnp.bfloat16).astype(jnp.float32).T.astype(jnp.bfloat16)
    tokens = slots * HIST
    slot = lax.broadcasted_iota(jnp.int32, (slots, tokens), 0)
    event = lax.broadcasted_iota(jnp.int32, (slots, tokens), 1)
    holds = (event // HIST == slot).astype(jnp.bfloat16)
    pre[...] = (dot(pool_t, holds) * slope[...].astype(jnp.float32)).astype(jnp.bfloat16)
    gate_part = dot(pre[...], x[:, columns(other)])
    core_start(1, gate_part[:, 0:part_w])
    core_start(2, gate_part[:, part_w:half_w])
    plane_end(0)
    gate_part = dot(pre[...], x[:, columns(c)])
    sums[1][0][...] = gate_part[:, 0:part_w]
    core_end(1)
    sums[2][0][...] = gate_part[:, part_w:half_w]
    core_end(2)
    piece_end(0)
    plane_end(1)
    back_end(0)
    plane_end(2)
    piece_end(1)
    piece_end(2)
    back_end(1)
    wide_end(0)
    back_end(2)
    wide_end(1)
    wide_end(2)

    def strips(n):
        ref, first, size = places[n]
        target = gate_hbm if n else out_hbm
        return [
            pltpu.make_async_copy(
                ref.at[:, core * half_w + first : core * half_w + first + size],
                target.at[:, core * half_w + first : core * half_w + first + size],
                out_sem.at[1 + n * CORES + core],
            )
            for core in range(CORES)
        ]

    for n in range(3):
        last_copy(n, other).wait()
        for strip in strips(n):
            strip.start()
    spot = users.at[pl.ds(0, nz - 1)]
    copy(spot, spot, user_send, user_recv.at[0], sibling).wait_send()
    all_relays.wait_send()
    py_relay.wait_send()
    pool_all.wait_send()
    for n in range(3):
        plane_all(n).wait_send()
        piece_all(n).wait_send()
        back_all(n).wait_send()
        wide_all(n).wait_send()
    logit_out.wait()
    for n in range(3):
        for strip in strips(n):
            strip.wait()


def train_step(histories, lengths, counts, imp_user, items, labels, w_uvqk, w_out):
    nz = lax.axis_size("own") // CORES
    nr = lax.axis_size("rep")
    slots = histories.shape[0]
    tokens = slots * HIST
    blocks = tokens // STEP
    imps = imp_user.shape[0]
    half_w = D // CORES
    bf16, f32 = jnp.bfloat16, jnp.float32
    hbm = pl.BlockSpec(memory_space=pltpu.HBM)
    dma = pltpu.SemaphoreType.DMA
    sums = []
    for size in (half_w, half_w // 2, half_w // 2):
        block = WIDTH // nr
        sums += [
            pltpu.VMEM((WIDTH, size), f32),
            pltpu.VMEM((WIDTH, size), bf16),
            pltpu.VMEM((WIDTH, size), bf16),
            pltpu.VMEM((WIDTH, size), bf16),
            pltpu.VMEM((nr, block, size), bf16),
            pltpu.VMEM((block, size), f32),
            pltpu.VMEM((nz, block * size // nz // LANES, LANES), f32),
            pltpu.VMEM((block, size), f32),
        ]
    return pl.pallas_call(
        functools.partial(step_kernel, nz, nr),
        in_specs=[hbm] * 8,
        out_specs=[hbm] * 3,
        out_shape=[
            jax.ShapeDtypeStruct((1, imps), f32),
            jax.ShapeDtypeStruct((WIDTH, D), bf16),
            jax.ShapeDtypeStruct((WIDTH, D), bf16),
        ],
        scratch_shapes=[
            pltpu.VMEM((1, imps), jnp.int32),
            pltpu.VMEM((1, imps), jnp.int32),
            pltpu.VMEM(items.shape, bf16),
            pltpu.VMEM(w_out.shape, bf16),
            pltpu.VMEM(w_uvqk.shape, bf16),
            pltpu.VMEM((tokens, D), bf16),
            pltpu.VMEM((WIDTH, tokens), bf16),
            pltpu.VMEM((STEP, 4 * WIDTH), f32),
            pltpu.VMEM((STEP, 4 * WIDTH), f32),
            pltpu.VMEM((slots, WIDTH), f32),
            pltpu.VMEM((1, imps), f32),
            pltpu.VMEM((WIDTH, D), bf16),
            pltpu.VMEM((WIDTH, D), bf16),
            pltpu.VMEM((CORES * nz, slots, D + WIDTH), bf16),
            pltpu.VMEM((nz, slots, WIDTH), bf16),
            pltpu.VMEM((nz, slots, WIDTH), bf16),
            pltpu.VMEM((nz, slots, WIDTH), f32),
            pltpu.VMEM((nz, slots, WIDTH), bf16),
            pltpu.VMEM((nz, slots, WIDTH), bf16),
            pltpu.VMEM((WIDTH, tokens), bf16),
            *sums,
            pltpu.SMEM(lengths.shape, jnp.int32),
            pltpu.SMEM(counts.shape, jnp.int32),
            dma((6,)), dma((blocks,)), dma((4,)), dma((1 + 3 * CORES,)),
            dma(()), dma((nz * PARTS,)), dma((4,)), dma((4,)),
            dma((3, 6)), dma((3, 6)),
        ],
        compiler_params=pltpu.CompilerParams(
            collective_id=0, has_side_effects=True, vmem_limit_bytes=58 * 1024 * 1024
        ),
        name="train_step",
    )(
        imp_user[None], labels[None], lengths, counts, items, w_out, w_uvqk, histories.reshape(tokens, D)
    )


def finish_kernel(logit_in, out_in, gate_in, logit_out, out_out, gate_out, turned, rows, flat, logit, sem):
    pieces = gate_in.shape[0] // LANES

    def moves(source, between, target, k):
        return (
            pltpu.make_async_copy(source, between, sem.at[0, k]),
            pltpu.make_async_copy(between, target, sem.at[1, k]),
        )

    def part(k):
        return pl.ds(k * LANES, LANES)

    gate_in_moves = [
        pltpu.make_async_copy(gate_in.at[part(k)], rows.at[part(k)], sem.at[0, k]) for k in range(pieces)
    ]
    out_moves = [
        moves(out_in.at[part(k)], flat.at[part(k)], out_out.at[part(k)], pieces + k) for k in range(pieces)
    ]
    logit_moves = moves(logit_in, logit, logit_out, 2 * pieces)
    for load in gate_in_moves:
        load.start()
    for load, _ in out_moves:
        load.start()
    logit_moves[0].start()
    for k in range(pieces):
        gate_in_moves[k].wait()
        turned[:, k * LANES : (k + 1) * LANES] = rows[part(k), :].astype(jnp.float32).T.astype(jnp.bfloat16)
        out_moves[k][0].wait()
        out_moves[k][1].start()
    last = pltpu.make_async_copy(turned, gate_out, sem.at[1, 0])
    last.start()
    logit_moves[0].wait()
    logit_moves[1].start()
    for _, store in out_moves:
        store.wait()
    logit_moves[1].wait()
    last.wait()


def finish(logits, grad_out, gate_t):
    hbm = pl.BlockSpec(memory_space=pltpu.HBM)
    across, deep = gate_t.shape
    return pl.pallas_call(
        finish_kernel,
        in_specs=[hbm] * 3,
        out_specs=[hbm] * 3,
        out_shape=[
            jax.ShapeDtypeStruct(logits.shape, logits.dtype),
            jax.ShapeDtypeStruct(grad_out.shape, grad_out.dtype),
            jax.ShapeDtypeStruct((deep, across), gate_t.dtype),
        ],
        scratch_shapes=[
            pltpu.VMEM((deep, across), gate_t.dtype),
            pltpu.VMEM((across, deep), gate_t.dtype),
            pltpu.VMEM(grad_out.shape, grad_out.dtype),
            pltpu.VMEM(logits.shape, logits.dtype),
            pltpu.SemaphoreType.DMA((2, 1 + 2 * across // LANES)),
        ],
        compiler_params=pltpu.CompilerParams(vmem_limit_bytes=58 * 1024 * 1024),
        name="finish",
    )(logits, grad_out, gate_t)


def body(histories, lengths, counts, imp_user, items, labels, w_uvqk, w_out):
    logits, grad_out, grad_gate = finish(
        *train_step(histories, lengths, counts, imp_user, items, labels, w_uvqk, w_out)
    )
    return (logits[0], grad_out, grad_gate)


def solution(mesh):
    return jax.shard_map(
        body,
        mesh=mesh,
        in_specs=(
            P(("own", "rep"), None, None),
            P(("own", "rep")),
            P(("own", "rep")),
            P(("own", "rep")),
            P(("own", "rep"), None),
            P(("own", "rep")),
            P(),
            P(),
        ),
        out_specs=(P(("own", "rep")), P(), P()),
        check_vma=False,
    )
```

time: 95.9 us -> 99.3 us (1.035)
  Pallas kernels: 92.3 us -> 98.4 us
  local copies, waits for them, and re-layouts: 2.87 us -> 0 us
    pallas_call x2, Pallas kernels: 92.3 us -> 98.4 us  [the longest x1 95.5 us: train_step(): pl.pallas_call(functools.partial(step_kernel, nz, nr), in_specs=[hbm] * 8...]
    unnamed x11 -> x0, local copies, waits for them, and re-layouts: 2.87 us -> none
where the time goes in v6:
time: 99.3 us; the launch traced here: 99.2 us
  Pallas kernels  98.4 us (99%)
    pallas_call x1, Pallas kernels, train_step(): pl.pallas_call(functools.partial(step_kernel, nz, nr), in_specs=[hbm] * 8...  95.5 us
    pallas_call x1, Pallas kernels, finish(): pl.pallas_call(finish_kernel, in_specs=[hbm] * 3, out_specs=[hbm] * 3, ou...  2.91 us

profile of v6, /device:TPU:1, one launch (start us, length us, event | category | flops | bytes accessed | tf_op | source)
XLA Modules:
  0.0 99.2 jit_solution(15907475108616013219)
XLA Ops:
  0.6 95.5 %train_step.1 = (f32[1,256]{1,0:T(1,128)}, bf16[512,1024]{1,0:T(8,128)(2,1)}, bf16[512,1024]{1,0:T(8,128)(2,1)}) custom-call(s32[1,256]{1,0:T(1,128)} %bitcast.5, s32[1,256]{1,0:T(1,128)} %bitcast.6, s32[32]{0:T(128)} %lengths_hbm.1, s32[16]{0:T(128)} %counts_hbm.1, bf16[256,1024]{1,0:T(8,128)(2,1)} %items_hbm.1, bf16[512,1024]{1,0:T(8,128)(2,1)} %w_out_hbm.1, ...), custom_call_target="tpu_custom_call" | custom-call | tf_op jit(solution)/shard_map/train_step/pallas_call | solution.py:492
  96.1 2.9 %finish.1 = (f32[1,256]{1,0:T(1,128)}, bf16[512,1024]{1,0:T(8,128)(2,1)}, bf16[1024,512]{1,0:T(8,128)(2,1)}) custom-call(f32[1,256]{1,0:T(1,128)} %get-tuple-element.9.logit_in, bf16[512,1024]{1,0:T(8,128)(2,1)} %get-tuple-element.10.out_in, bf16[512,1024]{1,0:T(8,128)(2,1)} %get-tuple-element.11.gate_in), custom_call_target="tpu_custom_call" | custom-call | tf_op jit(solution)/shard_map/finish/pallas_call | solution.py:580

commit v7 on v5

--- a/solution.py
+++ b/solution.py
@@ -37,46 +37,50 @@
 
 def forward_kernel(
     lengths_hbm, counts_hbm, h_hbm, w_hbm, both_hbm,
-    x, w, user_ref, slope_ref, even, odd, sum_y, lengths, counts, load_sem, h_sem, w_sem, out_sem,
+    x, w, user_ref, slope_ref, upper, lower, sum_x, sum_y, tile_y, lengths, counts, load_sem, h_sem, w_sem, out_sem,
 ):
     slots = user_ref.shape[0]
     blocks = slots * HIST // STEP
+    half_rows = STEP // 2
+    half_bins = half_rows // BIN
     step_bins = STEP // BIN
     step_slots = STEP // HIST
-    linear = (even, odd)
+    linear = (upper, lower)
 
     def block_rows(i):
-        return slice(i * STEP, (i + 1) * STEP)
+        return pl.ds(pl.multiple_of(i * STEP, STEP), STEP)
 
     def part(n):
         return slice(n * WIDTH, (n + 1) * WIDTH)
 
-    h_loads = [
-        pltpu.make_async_copy(h_hbm.at[block_rows(i)], x.at[block_rows(i)], h_sem.at[i]) for i in range(blocks)
-    ]
+    def h_load(i):
+        return pltpu.make_async_copy(h_hbm.at[block_rows(i)], x.at[block_rows(i)], h_sem.at[i])
+
     w_loads = [pltpu.make_async_copy(w_hbm.at[:, part(n)], w.at[:, part(n)], w_sem.at[n]) for n in range(4)]
     small = [
         pltpu.make_async_copy(lengths_hbm, lengths, load_sem.at[0]),
         pltpu.make_async_copy(counts_hbm, counts, load_sem.at[1]),
     ]
-    h_loads[0].start()
-    for load in w_loads:
+    h_load(0).start()
+    for load in w_loads + small:
         load.start()
-    for load in small + h_loads[1:]:
-        load.start()
-
-    def project(i, n):
-        linear[i % 2][:, part(n)] = dot(x[block_rows(i), :], w[:, part(n)])
+    for i in range(1, blocks):
+        h_load(i).start()
+
+    def project(i, half, n):
+        rows = pl.ds(pl.multiple_of(i * STEP + half * half_rows, half_rows), half_rows)
+        linear[half][:, part(n)] = dot(x[rows, :], w[:, part(n)])
 
     def span_of(s):
         return jnp.where(s % 2 < counts[s // 2], lengths[s], 0)
 
     def one_bin(i, k):
         b = i * step_bins + k
-        source = linear[i % 2]
-        rows = slice(k * BIN, (k + 1) * BIN)
+        source = linear[k // half_bins]
+        rows = slice(k % half_bins * BIN, (k % half_bins + 1) * BIN)
+        place = pl.ds(pl.multiple_of(b * BIN, BIN), BIN)
         first, second = span_of(2 * b), span_of(2 * b + 1)
-        feats = x[b * BIN : (b + 1) * BIN, :].astype(jnp.float32)
+        feats = x[place, :].astype(jnp.float32)
         half_scale = 0.5 * lax.rsqrt(jnp.mean(feats * feats, -1, keepdims=True) + EPS_NORM)
         row = lax.broadcasted_iota(jnp.int32, (BIN, BIN), 0)
         col = lax.broadcasted_iota(jnp.int32, (BIN, BIN), 1)
@@ -110,10 +114,10 @@
             normal = moved[h] * norm
             mixed = share * normal * (half * t + half)
             for j in range(2):
-                s = 2 * b + j
-                sum_y[s : s + 1, cols] = jnp.sum(mixed[j * HIST : (j + 1) * HIST], 0, keepdims=True)
+                s = 2 * k + j
+                tile_y[s : s + 1, cols] = jnp.sum(mixed[j * HIST : (j + 1) * HIST], 0, keepdims=True)
             slope = back * normal * ((1.0 + t) * (1.0 + half * (1.0 - t)))
-            slope_ref[cols, b * BIN : (b + 1) * BIN] = slope.T.astype(jnp.bfloat16)
+            slope_ref[cols, place] = slope.T.astype(jnp.bfloat16)
 
     def pool_x(i):
         slot = lax.broadcasted_iota(jnp.int32, (step_slots, STEP), 0)
@@ -130,23 +134,36 @@
         cols = block_rows(i)
         return pltpu.make_async_copy(slope_ref.at[:, cols], both_hbm.at[0:WIDTH, cols], out_sem.at[i])
 
-    h_loads[0].wait()
+    h_load(0).wait()
     for n in range(4):
         w_loads[n].wait()
-        project(0, n)
+        project(0, 0, n)
     for load in small:
         load.wait()
-    pooled = []
-    for i in range(blocks):
-        if i + 1 < blocks:
-            h_loads[i + 1].wait()
-        for k in range(step_bins):
-            if i + 1 < blocks:
-                project(i + 1, k)
-            one_bin(i, k)
-        pooled.append(pool_x(i))
+
+    def block(i, carry):
+        for n in range(4):
+            project(i, 1, n)
+            if n % 2 == 1:
+                one_bin(i, n // 2)
+        later = jnp.minimum(i + 1, blocks - 1)
+
+        @pl.when(i + 1 < blocks)
+        def _():
+            h_load(later).wait()
+
+        for n in range(4):
+            project(later, 0, n)
+            if n % 2 == 1:
+                one_bin(i, half_bins + n // 2)
+        group = pl.ds(pl.multiple_of(i * step_slots, step_slots), step_slots)
+        sum_x[group, :] = pool_x(i)
+        sum_y[group, :] = tile_y[...]
         slope_out(i).start()
-    user_ref[:, 0:D] = jnp.concatenate(pooled, 0).astype(jnp.bfloat16)
+        return carry
+
+    lax.fori_loop(0, blocks, block, 0)
+    user_ref[:, 0:D] = sum_x[...].astype(jnp.bfloat16)
     user_ref[:, D : D + WIDTH] = sum_y[...].astype(jnp.bfloat16)
     user_out = pltpu.make_async_copy(
         user_ref, both_hbm.at[WIDTH : WIDTH + slots, 0 : D + WIDTH], out_sem.at[blocks]
@@ -174,9 +191,11 @@
             pltpu.VMEM(w_uvqk.shape, bf16),
             pltpu.VMEM((slots, D + WIDTH), bf16),
             pltpu.VMEM((WIDTH, tokens), bf16),
-            pltpu.VMEM((STEP, 4 * WIDTH), f32),
-            pltpu.VMEM((STEP, 4 * WIDTH), f32),
+            pltpu.VMEM((STEP // 2, 4 * WIDTH), f32),
+            pltpu.VMEM((STEP // 2, 4 * WIDTH), f32),
+            pltpu.VMEM((slots, D), f32),
             pltpu.VMEM((slots, WIDTH), f32),
+            pltpu.VMEM((STEP // HIST, WIDTH), f32),
             pltpu.SMEM(lengths.shape, jnp.int32),
             pltpu.SMEM(counts.shape, jnp.int32),
             dma((2,)), dma((blocks,)), dma((4,)), dma((blocks + 1,)),
@@ -244,14 +263,18 @@
             device_id=device, device_id_type=MESH,
         )
 
+    def each(count, step):
+        def run(k, carry):
+            step(k)
+            return carry
+        lax.fori_loop(1, count, run, 0)
+
     def signal(device):
         pl.semaphore_signal(barrier, inc=1, device_id=device, device_id_type=MESH)
 
     barrier = pltpu.get_barrier_semaphore()
-    for k in range(1, nz):
-        signal(z_id(k))
-    for k in range(1, nr):
-        signal(plane_id(k))
+    each(nz, lambda k: signal(z_id(k)))
+    each(nr, lambda k: signal(plane_id(k)))
     signal(sibling)
     pl.semaphore_wait(barrier, nz - 1 + nr - 1 + 1)
 
@@ -327,8 +350,7 @@
     turned = users[:, :, D : D + WIDTH].reshape(2 * side, WIDTH).astype(jnp.float32).T.astype(jnp.bfloat16)
     pool_copy.wait()
     pool_z[...] = (pool_mine[...] + pool_core[...].astype(jnp.float32)).astype(jnp.bfloat16)
-    for k in range(1, nz):
-        copy(pool_z.at[(z + k) % nz], pool_got.at[z], pool_sem.at[2], pool_sem.at[3], z_id(k)).start()
+    each(nz, lambda k: copy(pool_z.at[(z + k) % nz], pool_got.at[z], pool_sem.at[2], pool_sem.at[3], z_id(k)).start())
     pool_got[z] = pool_z[z]
 
     chosen = dot(turned, picked.astype(jnp.bfloat16))
@@ -359,8 +381,7 @@
         mine, _, core_got, half, plane_got = sums[n][:5]
         core_copy(n).wait()
         half[...] = (mine[...] + core_got[...].astype(jnp.float32)).astype(jnp.bfloat16)
-        for k in range(1, nr):
-            copy(half.at[plane_rows(k)], plane_got.at[rep], *sems(n, PLANE), plane_id(k)).start()
+        each(nr, lambda k: copy(half.at[plane_rows(k)], plane_got.at[rep], *sems(n, PLANE), plane_id(k)).start())
         plane_got[rep] = half[plane_rows(0), :]
 
     def plane_all(n):
@@ -381,8 +402,7 @@
         for k in range(1, nr):
             total += plane_got[k].astype(jnp.float32)
         row_sum[...] = total
-        for k in range(1, nz):
-            copy(row_sum.at[piece_spot(n, (z + k) % nz)], piece_got.at[z], *sems(n, PIECE), z_id(k)).start()
+        each(nz, lambda k: copy(row_sum.at[piece_spot(n, (z + k) % nz)], piece_got.at[z], *sems(n, PIECE), z_id(k)).start())
         piece_got[z] = row_sum[piece_spot(n, z)]
 
     def piece_all(n):
@@ -397,8 +417,7 @@
             total += piece_got[k]
         spot = final.at[piece_spot(n, z)]
         spot[...] = total
-        for k in range(1, nz):
-            copy(spot, spot, *sems(n, BACK), z_id(k)).start()
+        each(nz, lambda k: copy(spot, spot, *sems(n, BACK), z_id(k)).start())
 
     def back_all(n):
         spot = sums[n][6].at[pl.ds(0, nz - 1)]
@@ -412,8 +431,7 @@
         back_all(n).wait_recv()
         spot = wide_spot(n, c, 0)
         spot[...] = sums[n][7][...].astype(jnp.bfloat16)
-        for k in range(1, nr):
-            copy(spot, spot, *sems(n, WIDE), plane_id(k)).start()
+        each(nr, lambda k: copy(spot, spot, *sems(n, WIDE), plane_id(k)).start())
 
     def wide_all(n):
         ref, first, size = places[n]
@@ -451,10 +469,9 @@
     core_start(1, gate_part[:, 0:part_w])
     core_start(2, gate_part[:, part_w:half_w])
     plane_end(0)
-    gate_part = dot(pre[...], hist[:, columns(c)])
-    sums[1][0][...] = gate_part[:, 0:part_w]
+    sums[1][0][...] = dot(pre[...], hist[:, columns(c, 0, part_w)])
     core_end(1)
-    sums[2][0][...] = gate_part[:, part_w:half_w]
+    sums[2][0][...] = dot(pre[...], hist[:, columns(c, part_w, part_w)])
     core_end(2)
     piece_end(0)
     plane_end(1)

time: 95.9 us -> 98.8 us (1.030)
  Pallas kernels: 92.3 us -> 95.2 us
    pallas_call x1, Pallas kernels: 23.3 us -> 25.6 us  [forward(): pl.pallas_call(forward_kernel, in_specs=[hbm] * 4, out_specs=hbm, out_sha...]
where the time goes in v7:
time: 98.8 us
  Pallas kernels  95.2 us (96%)
  local copies, waits for them, and re-layouts  2.87 us (3%)
    pallas_call x1, Pallas kernels, exchange(): pl.pallas_call(functools.partial(exchange_kernel, nz, nr), in_specs=[pl.B...  69.6 us
    pallas_call x1, Pallas kernels, forward(): pl.pallas_call(forward_kernel, in_specs=[hbm] * 4, out_specs=hbm, out_sha...  25.6 us
    unnamed x11, local copies, waits for them, and re-layouts  2.87 us

profile of v7, /device:TPU:1, one launch (start us, length us, event | category | flops | bytes accessed | tf_op | source)
XLA Modules:
  0.0 98.8 jit_solution(15021203692264678697)
XLA Ops:
  0.6 0.0 copy-start
  0.6 0.0 copy-start.1
  0.7 0.0 copy-start.2
  0.7 0.0 copy-start.3
  0.7 25.6 %forward.1.args_2_ = bf16[544,2048]{1,0:T(8,128)(2,1)} custom-call(s32[32]{0:T(128)} %lengths_hbm.1, s32[16]{0:T(128)} %counts_hbm.1, bf16[2048,1024]{1,0:T(8,128)(2,1)} %bitcast.9, bf16[1024,2048]{1,0:T(8,128)(2,1)} %w_hbm.1), custom_call_target="tpu_custom_call" | custom-call | tf_op jit(solution)/shard_map/forward/pallas_call | solution.py:184
  26.3 0.0 copy-done
  26.3 0.0 copy-done.1
  26.3 0.0 copy-done.2
  26.3 0.0 copy-done.3
  26.3 69.6 %exchange.1 = (f32[1,256]{1,0:T(1,128)S(1)}, bf16[512,1024]{1,0:T(8,128)(2,1)S(1)}, bf16[512,1024]{1,0:T(8,128)(2,1)S(1)}) custom-call(s32[1,256]{1,0:T(1,128)S(1)} %bitcast.6, s32[1,256]{1,0:T(1,128)S(1)} %bitcast.7, bf16[544,2048]{1,0:T(8,128)(2,1)} %forward.1.args_2_, bf16[256,1024]{1,0:T(8,128)(2,1)S(1)} %copy-done.1, bf16[512,1024]{1,0:T(8,128)(2,1)S(1)} %copy-done, ...), custom_call_target="tpu_custom_call" | custom-call | tf_op jit(solution)/shard_map/exchange/pallas_call | solution.py:524
  95.9 1.3 %copy.11 = bf16[1024,512]{1,0:T(8,128)(2,1)} copy(bf16[1024,512]{0,1:T(8,128)(2,1)S(1)} %bitcast.5) | data formatting | bytes 2097152
  97.2 0.6 copy.14
  97.8 1.0 copy.15
Async XLA Ops:
  0.6 25.7 %copy-start = (bf16[512,1024]{1,0:T(8,128)(2,1)S(1)}, bf16[512,1024]{1,0:T(8,128)(2,1)}, u32[]{:S(2)}) copy-start(bf16[512,1024]{1,0:T(8,128)(2,1)} %args_4_.4) | copy-start | bytes 3145732
  0.6 25.7 %copy-start.1 = (bf16[256,1024]{1,0:T(8,128)(2,1)S(1)}, bf16[256,1024]{1,0:T(8,128)(2,1)}, u32[]{:S(2)}) copy-start(bf16[256,1024]{1,0:T(8,128)(2,1)} %args_3_.4) | copy-start | bytes 1572868
  0.7 25.7 %copy-start.2 = (s32[256]{0:T(256)S(1)}, s32[256]{0:T(256)}, u32[]{:S(2)}) copy-start(s32[256]{0:T(256)} %param.11) | copy-start | bytes 3076
  0.7 25.7 %copy-start.3 = (s32[256]{0:T(256)S(1)}, s32[256]{0:T(256)}, u32[]{:S(2)}) copy-start(s32[256]{0:T(256)} %param.13) | copy-start | bytes 3076

commit v8 on v5

--- a/solution.py
+++ b/solution.py
@@ -36,8 +36,8 @@
 
 
 def forward_kernel(
-    lengths_hbm, counts_hbm, h_hbm, w_hbm, both_hbm,
-    x, w, user_ref, slope_ref, even, odd, sum_y, lengths, counts, load_sem, h_sem, w_sem, out_sem,
+    lengths_hbm, counts_hbm, h_hbm, w_hbm, w_out_hbm, both_hbm,
+    x, w, w_out, user_ref, slope_ref, even, odd, sum_y, lengths, counts, load_sem, h_sem, w_sem, out_sem,
 ):
     slots = user_ref.shape[0]
     blocks = slots * HIST // STEP
@@ -58,15 +58,17 @@
     small = [
         pltpu.make_async_copy(lengths_hbm, lengths, load_sem.at[0]),
         pltpu.make_async_copy(counts_hbm, counts, load_sem.at[1]),
+        pltpu.make_async_copy(w_out_hbm, w_out, load_sem.at[2]),
     ]
     h_loads[0].start()
     for load in w_loads:
         load.start()
-    for load in small + h_loads[1:]:
+    for load in small[:2] + h_loads[1:] + small[2:]:
         load.start()
 
     def project(i, n):
-        linear[i % 2][:, part(n)] = dot(x[block_rows(i), :], w[:, part(n)])
+        cols = slice(2 * n * WIDTH, 2 * (n + 1) * WIDTH)
+        linear[i % 2][:, cols] = dot(x[block_rows(i), :], w[:, cols])
 
     def span_of(s):
         return jnp.where(s % 2 < counts[s // 2], lengths[s], 0)
@@ -131,23 +133,26 @@
         return pltpu.make_async_copy(slope_ref.at[:, cols], both_hbm.at[0:WIDTH, cols], out_sem.at[i])
 
     h_loads[0].wait()
-    for n in range(4):
-        w_loads[n].wait()
+    for n in range(2):
+        w_loads[2 * n].wait()
+        w_loads[2 * n + 1].wait()
         project(0, n)
-    for load in small:
+    for load in small[:2]:
         load.wait()
     pooled = []
     for i in range(blocks):
         if i + 1 < blocks:
             h_loads[i + 1].wait()
         for k in range(step_bins):
-            if i + 1 < blocks:
-                project(i + 1, k)
+            if i + 1 < blocks and k % 2 == 0:
+                project(i + 1, k // 2)
             one_bin(i, k)
         pooled.append(pool_x(i))
         slope_out(i).start()
-    user_ref[:, 0:D] = jnp.concatenate(pooled, 0).astype(jnp.bfloat16)
-    user_ref[:, D : D + WIDTH] = sum_y[...].astype(jnp.bfloat16)
+    small[2].wait()
+    py = sum_y[...].astype(jnp.bfloat16)
+    user_ref[:, 0:D] = (jnp.concatenate(pooled, 0) + dot(py, w_out[...])).astype(jnp.bfloat16)
+    user_ref[:, D : D + WIDTH] = py
     user_out = pltpu.make_async_copy(
         user_ref, both_hbm.at[WIDTH : WIDTH + slots, 0 : D + WIDTH], out_sem.at[blocks]
     )
@@ -157,7 +162,7 @@
     user_out.wait()
 
 
-def forward(histories, lengths, counts, w_uvqk):
+def forward(histories, lengths, counts, w_uvqk, w_out):
     slots = histories.shape[0]
     tokens = slots * HIST
     blocks = tokens // STEP
@@ -166,12 +171,13 @@
     dma = pltpu.SemaphoreType.DMA
     return pl.pallas_call(
         forward_kernel,
-        in_specs=[hbm] * 4,
+        in_specs=[hbm] * 5,
         out_specs=hbm,
         out_shape=jax.ShapeDtypeStruct((WIDTH + slots, tokens), bf16),
         scratch_shapes=[
             pltpu.VMEM((tokens, D), bf16),
             pltpu.VMEM(w_uvqk.shape, bf16),
+            pltpu.VMEM(w_out.shape, bf16),
             pltpu.VMEM((slots, D + WIDTH), bf16),
             pltpu.VMEM((WIDTH, tokens), bf16),
             pltpu.VMEM((STEP, 4 * WIDTH), f32),
@@ -179,11 +185,11 @@
             pltpu.VMEM((slots, WIDTH), f32),
             pltpu.SMEM(lengths.shape, jnp.int32),
             pltpu.SMEM(counts.shape, jnp.int32),
-            dma((2,)), dma((blocks,)), dma((4,)), dma((blocks + 1,)),
+            dma((3,)), dma((blocks,)), dma((4,)), dma((blocks + 1,)),
         ],
         compiler_params=pltpu.CompilerParams(vmem_limit_bytes=58 * 1024 * 1024),
         name="forward",
-    )(lengths, counts, histories.reshape(tokens, D), w_uvqk)
+    )(lengths, counts, histories.reshape(tokens, D), w_uvqk, w_out)
 
 
 def exchange_kernel(
@@ -244,74 +250,93 @@
             device_id=device, device_id_type=MESH,
         )
 
+    def each(count, step):
+        def run(k, carry):
+            step(k)
+            return carry
+        lax.fori_loop(1, count, run, 0)
+
     def signal(device):
         pl.semaphore_signal(barrier, inc=1, device_id=device, device_id_type=MESH)
 
     barrier = pltpu.get_barrier_semaphore()
-    for k in range(1, nz):
-        signal(z_id(k))
-    for k in range(1, nr):
-        signal(plane_id(k))
+    each(nz, lambda k: signal(z_id(k)))
+    each(nr, lambda k: signal(plane_id(k)))
     signal(sibling)
     pl.semaphore_wait(barrier, nz - 1 + nr - 1 + 1)
 
     loads[2].wait()
+    at = c * nz + z
     reach = nz // 2
-    width = (D + WIDTH) // PARTS
+    some = slots // 2
     ends = (z_id(1), z_id(nz - 1))
 
     def origin(way, step):
         return (z + nz - step if way == 0 else z + step) % nz
 
-    def hop(way, step, part):
-        spot = users.at[c * nz + origin(way, step), :, part * width : (part + 1) * width]
-        return copy(spot, spot, user_send, user_recv.at[(way * reach + step) * PARTS + part], ends[way])
-
-    def landed(way, step, part):
-        spot = users.at[c * nz + origin(way, step + 1), :, part * width : (part + 1) * width]
-        copy(spot, spot, user_send, user_recv.at[(way * reach + step) * PARTS + part], ends[way]).wait_recv()
-
-    def goes(way, step, part):
-        return step < reach - 1 or part % 2 == way
+    def piece_of(block, piece):
+        rows = pl.ds(piece % 2 * some, some)
+        return users.at[block, rows, 0:D] if piece < 2 else users.at[block, rows, D : D + WIDTH]
+
+    def hop(way, step, piece):
+        spot = piece_of(c * nz + origin(way, step), piece)
+        return copy(spot, spot, user_send, user_recv.at[(way * reach + step) * PARTS + piece], ends[way])
+
+    def landed(way, step, piece):
+        spot = piece_of(c * nz + origin(way, step + 1), piece)
+        copy(spot, spot, user_send, user_recv.at[(way * reach + step) * PARTS + piece], ends[way]).wait_recv()
+
+    def goes(way, step, piece):
+        return step < reach - 1 or piece % 2 == way
+
+    def pass_on(step, pieces):
+        for piece in pieces:
+            for way in range(2):
+                if goes(way, step, piece):
+                    landed(way, step, piece)
+                if step + 1 < reach and goes(way, step + 1, piece):
+                    hop(way, step + 1, piece).start()
 
     def user_relay(zz):
-        spot = users.at[c * nz + zz]
+        spot = users.at[c * nz + zz, :, 0:D]
         return copy(spot, spot, relay_sem.at[0], relay_sem.at[1], sibling)
 
-    for part in range(PARTS):
+    for piece in range(PARTS):
         for way in range(2):
-            hop(way, 0, part).start()
+            hop(way, 0, piece).start()
     user_relay(z).start()
     loads[3].wait()
     loads[4].wait()
     item_w = dot_t(items[...], w_out[...]).astype(jnp.bfloat16)
     for step in range(reach):
-        for part in range(PARTS):
-            for way in range(2):
-                if goes(way, step, part):
-                    landed(way, step, part)
-                if step + 1 < reach and goes(way, step + 1, part):
-                    hop(way, step + 1, part).start()
+        pass_on(step, (0, 1))
         user_relay(origin(0, step + 1)).start()
         if step + 1 < reach:
             user_relay(origin(1, step + 1)).start()
-    all_relays = copy(
-        users.at[pl.ds(c * nz, nz)], users.at[pl.ds(other * nz, nz)], relay_sem.at[0], relay_sem.at[1], sibling
-    )
+    pass_on(0, (2, 3))
+
+    def line_of(core, first, size):
+        return users.at[pl.ds(core * nz, nz), :, first : first + size]
+
+    def line_relay(first, size, k):
+        return copy(
+            line_of(c, first, size), line_of(other, first, size), relay_sem.at[k], relay_sem.at[k + 1], sibling
+        )
+
     loads[0].wait()
     loads[1].wait()
-    all_relays.wait_recv()
+    line_relay(0, D, 0).wait_recv()
+    pass_on(1, (2, 3))
 
     index = user_ref[...]
     source = (index % slots) // 2
     place = (source % CORES) * side + (source // CORES) * slots + index // slots * 2 + index % 2
-    table = dot_t(users[:, :, 0:D].reshape(2 * side, D), items[...]) + dot_t(
-        users[:, :, D : D + WIDTH].reshape(2 * side, WIDTH), item_w
-    )
+    table = dot_t(users[:, :, 0:D].reshape(2 * side, D), items[...])
     imps = index.shape[1]
     picked = lax.broadcasted_iota(jnp.int32, (2 * side, imps), 0) == place
     logits = jnp.sum(jnp.where(picked, table, 0.0), 0, keepdims=True)
     logit_ref[...] = logits
+    pass_on(2, (2, 3))
     error = sigmoid(logits) - label_ref[...].astype(jnp.float32)
 
     line = lax.broadcasted_iota(jnp.int32, (side, imps), 0)
@@ -324,13 +349,17 @@
     pool_copy = copy(pool_send, pool_core, pool_sem.at[0], pool_sem.at[1], sibling)
     pool_copy.start()
     pool_mine[...] = pool_side(c)
-    turned = users[:, :, D : D + WIDTH].reshape(2 * side, WIDTH).astype(jnp.float32).T.astype(jnp.bfloat16)
     pool_copy.wait()
     pool_z[...] = (pool_mine[...] + pool_core[...].astype(jnp.float32)).astype(jnp.bfloat16)
-    for k in range(1, nz):
-        copy(pool_z.at[(z + k) % nz], pool_got.at[z], pool_sem.at[2], pool_sem.at[3], z_id(k)).start()
+    each(nz, lambda k: copy(pool_z.at[(z + k) % nz], pool_got.at[z], pool_sem.at[2], pool_sem.at[3], z_id(k)).start())
     pool_got[z] = pool_z[z]
 
+    pass_on(reach - 1, (2, 3))
+    spot = line_of(c, D, WIDTH)
+    py_relay = copy(spot, spot, relay_sem.at[2], relay_sem.at[3], sibling)
+    py_relay.start()
+    line_relay(D, WIDTH, 2).wait_recv()
+    turned = users[:, :, D : D + WIDTH].reshape(2 * side, WIDTH).astype(jnp.float32).T.astype(jnp.bfloat16)
     chosen = dot(turned, picked.astype(jnp.bfloat16))
     chosen = (chosen * error).astype(jnp.bfloat16)
 
@@ -359,8 +388,7 @@
         mine, _, core_got, half, plane_got = sums[n][:5]
         core_copy(n).wait()
         half[...] = (mine[...] + core_got[...].astype(jnp.float32)).astype(jnp.bfloat16)
-        for k in range(1, nr):
-            copy(half.at[plane_rows(k)], plane_got.at[rep], *sems(n, PLANE), plane_id(k)).start()
+        each(nr, lambda k: copy(half.at[plane_rows(k)], plane_got.at[rep], *sems(n, PLANE), plane_id(k)).start())
         plane_got[rep] = half[plane_rows(0), :]
 
     def plane_all(n):
@@ -381,8 +409,7 @@
         for k in range(1, nr):
             total += plane_got[k].astype(jnp.float32)
         row_sum[...] = total
-        for k in range(1, nz):
-            copy(row_sum.at[piece_spot(n, (z + k) % nz)], piece_got.at[z], *sems(n, PIECE), z_id(k)).start()
+        each(nz, lambda k: copy(row_sum.at[piece_spot(n, (z + k) % nz)], piece_got.at[z], *sems(n, PIECE), z_id(k)).start())
         piece_got[z] = row_sum[piece_spot(n, z)]
 
     def piece_all(n):
@@ -397,8 +424,7 @@
             total += piece_got[k]
         spot = final.at[piece_spot(n, z)]
         spot[...] = total
-        for k in range(1, nz):
-            copy(spot, spot, *sems(n, BACK), z_id(k)).start()
+        each(nz, lambda k: copy(spot, spot, *sems(n, BACK), z_id(k)).start())
 
     def back_all(n):
         spot = sums[n][6].at[pl.ds(0, nz - 1)]
@@ -412,8 +438,7 @@
         back_all(n).wait_recv()
         spot = wide_spot(n, c, 0)
         spot[...] = sums[n][7][...].astype(jnp.bfloat16)
-        for k in range(1, nr):
-            copy(spot, spot, *sems(n, WIDE), plane_id(k)).start()
+        each(nr, lambda k: copy(spot, spot, *sems(n, WIDE), plane_id(k)).start())
 
     def wide_all(n):
         ref, first, size = places[n]
@@ -470,7 +495,8 @@
 
     spot = users.at[pl.ds(0, nz - 1)]
     copy(spot, spot, user_send, user_recv.at[0], sibling).wait_send()
-    all_relays.wait_send()
+    line_relay(0, D, 0).wait_send()
+    py_relay.wait_send()
     pool_all.wait_send()
     for n in range(3):
         plane_all(n).wait_send()
@@ -525,7 +551,7 @@
             pltpu.VMEM((nz, slots, WIDTH), bf16),
             pltpu.VMEM((WIDTH, tokens), bf16),
             *sums,
-            dma((7,)), dma(()), dma((nz * PARTS,)), dma((2,)),
+            dma((7,)), dma(()), dma((nz * PARTS,)), dma((4,)),
             dma((4,)),
             dma((3, 6)), dma((3, 6)),
         ],
@@ -537,7 +563,7 @@
 
 
 def body(histories, lengths, counts, imp_user, items, labels, w_uvqk, w_out):
-    both = forward(histories, lengths, counts, w_uvqk)
+    both = forward(histories, lengths, counts, w_uvqk, w_out)
     logits, grad_out, grad_gate = exchange(
         imp_user, labels, both, items, w_out, histories.reshape(-1, D)
     )

time: 95.9 us -> 103 us (1.074)
  Pallas kernels: 92.3 us -> 99.7 us
    pallas_call x1, Pallas kernels: 69 us -> 75.5 us  [exchange(): pl.pallas_call(functools.partial(exchange_kernel, nz, nr), in_specs=[pl.B...]
where the time goes in v8:
time: 103 us
  Pallas kernels  99.7 us (97%)
  local copies, waits for them, and re-layouts  2.87 us (3%)
    pallas_call x1, Pallas kernels, exchange(): pl.pallas_call(functools.partial(exchange_kernel, nz, nr), in_specs=[pl.B...  75.5 us
    pallas_call x1, Pallas kernels, forward(): pl.pallas_call(forward_kernel, in_specs=[hbm] * 5, out_specs=hbm, out_sha...  24.2 us
    unnamed x11, local copies, waits for them, and re-layouts  2.87 us

profile of v8, /device:TPU:1, one launch (start us, length us, event | category | flops | bytes accessed | tf_op | source)
XLA Modules:
  0.0 103.3 jit_solution(17036104240164000362)
XLA Ops:
  0.6 0.0 copy-start
  0.6 0.0 copy-start.1
  0.7 0.0 copy-start.2
  0.7 0.0 copy-start.3
  0.7 24.2 %forward.1.args_2_ = bf16[544,2048]{1,0:T(8,128)(2,1)} custom-call(s32[32]{0:T(128)} %lengths_hbm.1, s32[16]{0:T(128)} %counts_hbm.1, bf16[2048,1024]{1,0:T(8,128)(2,1)} %bitcast.9, bf16[1024,2048]{1,0:T(8,128)(2,1)} %w_hbm.1, bf16[512,1024]{1,0:T(8,128)(2,1)} %args_4_.4), custom_call_target="tpu_custom_call" | custom-call | tf_op jit(solution)/shard_map/forward/pallas_call | solution.py:172
  24.9 0.0 copy-done
  24.9 0.0 copy-done.1
  24.9 0.0 copy-done.2
  24.9 0.0 copy-done.3
  24.9 75.5 %exchange.1 = (f32[1,256]{1,0:T(1,128)S(1)}, bf16[512,1024]{1,0:T(8,128)(2,1)S(1)}, bf16[512,1024]{1,0:T(8,128)(2,1)S(1)}) custom-call(s32[1,256]{1,0:T(1,128)S(1)} %bitcast.6, s32[1,256]{1,0:T(1,128)S(1)} %bitcast.7, bf16[544,2048]{1,0:T(8,128)(2,1)} %forward.1.args_2_, bf16[256,1024]{1,0:T(8,128)(2,1)S(1)} %copy-done.1, bf16[512,1024]{1,0:T(8,128)(2,1)S(1)} %copy-done, ...), custom_call_target="tpu_custom_call" | custom-call | tf_op jit(solution)/shard_map/exchange/pallas_call | solution.py:533
  100.5 1.3 %copy.11 = bf16[1024,512]{1,0:T(8,128)(2,1)} copy(bf16[1024,512]{0,1:T(8,128)(2,1)S(1)} %bitcast.5) | data formatting | bytes 2097152
  101.8 0.6 copy.14
  102.3 1.0 copy.15
Async XLA Ops:
  0.6 24.3 %copy-start = (bf16[512,1024]{1,0:T(8,128)(2,1)S(1)}, bf16[512,1024]{1,0:T(8,128)(2,1)}, u32[]{:S(2)}) copy-start(bf16[512,1024]{1,0:T(8,128)(2,1)} %args_4_.4) | copy-start | bytes 3145732
  0.6 24.3 %copy-start.1 = (bf16[256,1024]{1,0:T(8,128)(2,1)S(1)}, bf16[256,1024]{1,0:T(8,128)(2,1)}, u32[]{:S(2)}) copy-start(bf16[256,1024]{1,0:T(8,128)(2,1)} %args_3_.4) | copy-start | bytes 1572868
  0.7 24.3 %copy-start.2 = (s32[256]{0:T(256)S(1)}, s32[256]{0:T(256)}, u32[]{:S(2)}) copy-start(s32[256]{0:T(256)} %param.11) | copy-start | bytes 3076
  0.7 24.3 %copy-start.3 = (s32[256]{0:T(256)S(1)}, s32[256]{0:T(256)}, u32[]{:S(2)}) copy-start(s32[256]{0:T(256)} %param.13) | copy-start | bytes 3076

commit v9 on v6

--- a/solution.py
+++ b/solution.py
@@ -111,36 +111,25 @@
 
     at = c * nz + z
     reach = nz // 2
-    some = slots // 2
+    width = (D + WIDTH) // PARTS
     ends = (z_id(1), z_id(nz - 1))
 
     def origin(way, step):
         return (z + nz - step if way == 0 else z + step) % nz
 
-    def piece_of(block, piece):
-        rows = pl.ds(piece % 2 * some, some)
-        return users.at[block, rows, 0:D] if piece < 2 else users.at[block, rows, D : D + WIDTH]
-
-    def hop(way, step, piece):
-        spot = piece_of(c * nz + origin(way, step), piece)
-        return copy(spot, spot, user_send, user_recv.at[(way * reach + step) * PARTS + piece], ends[way])
-
-    def landed(way, step, piece):
-        spot = piece_of(c * nz + origin(way, step + 1), piece)
-        copy(spot, spot, user_send, user_recv.at[(way * reach + step) * PARTS + piece], ends[way]).wait_recv()
-
-    def goes(way, step, piece):
-        return step < reach - 1 or piece % 2 == way
-
-    def forward_hop(step, piece):
-        for way in range(2):
-            if goes(way, step, piece):
-                landed(way, step, piece)
-            if step + 1 < reach and goes(way, step + 1, piece):
-                hop(way, step + 1, piece).start()
+    def hop(way, step, part):
+        spot = users.at[c * nz + origin(way, step), :, part * width : (part + 1) * width]
+        return copy(spot, spot, user_send, user_recv.at[(way * reach + step) * PARTS + part], ends[way])
+
+    def landed(way, step, part):
+        spot = users.at[c * nz + origin(way, step + 1), :, part * width : (part + 1) * width]
+        copy(spot, spot, user_send, user_recv.at[(way * reach + step) * PARTS + part], ends[way]).wait_recv()
+
+    def goes(way, step, part):
+        return step < reach - 1 or part % 2 == way
 
     def user_relay(zz):
-        spot = users.at[c * nz + zz, :, 0:D]
+        spot = users.at[c * nz + zz]
         return copy(spot, spot, relay_sem.at[0], relay_sem.at[1], sibling)
 
     def project(i, n):
@@ -204,16 +193,6 @@
         inverse = 1.0 / jnp.maximum(span, 1).astype(jnp.float32)
         return dot(live, x[block_rows(i), :]) * inverse
 
-    def embed(g):
-        rows = slice(g * some, (g + 1) * some)
-        py = sum_y[rows, :].astype(jnp.bfloat16)
-        users[at, rows, D : D + WIDTH] = py
-        px = jnp.concatenate(pooled[g * blocks // 2 : (g + 1) * blocks // 2], 0)
-        users[at, rows, 0:D] = (px + dot(py, w_out[...])).astype(jnp.bfloat16)
-        for piece in (g, g + 2):
-            for way in range(2):
-                hop(way, 0, piece).start()
-
     h_loads[0].wait()
     for n in range(4):
         w_loads[n].wait()
@@ -228,51 +207,44 @@
             if i + 1 < blocks:
                 project(i + 1, k)
             one_bin(i, k)
-            if i == blocks - 1 and k == step_bins // 2 - 1:
-                for piece in (0, 2):
-                    forward_hop(1, piece)
         pooled.append(pool_x(i))
-        if i == blocks // 2 - 1:
-            pl.semaphore_wait(barrier, nz - 1 + nr - 1 + 1)
-            embed(0)
-        elif i == blocks - 2:
-            for piece in (0, 2):
-                forward_hop(0, piece)
-    embed(1)
+    users[at, :, 0:D] = jnp.concatenate(pooled, 0).astype(jnp.bfloat16)
+    users[at, :, D : D + WIDTH] = sum_y[...].astype(jnp.bfloat16)
+    pl.semaphore_wait(barrier, nz - 1 + nr - 1 + 1)
+    for piece in range(PARTS):
+        for way in range(2):
+            hop(way, 0, piece).start()
     user_relay(z).start()
-    for piece in (0, 2):
-        forward_hop(2, piece)
     for load in loads[3:]:
         load.wait()
     item_w = dot_t(items[...], w_out[...]).astype(jnp.bfloat16)
     for step in range(reach):
-        forward_hop(step, 1)
-        if step == reach - 1:
-            forward_hop(step, 0)
+        for piece in range(PARTS):
+            for way in range(2):
+                if goes(way, step, piece):
+                    landed(way, step, piece)
+                if step + 1 < reach and goes(way, step + 1, piece):
+                    hop(way, step + 1, piece).start()
         user_relay(origin(0, step + 1)).start()
         if step + 1 < reach:
             user_relay(origin(1, step + 1)).start()
-    forward_hop(reach - 1, 2)
-    forward_hop(0, 3)
-
-    def line_of(core, first, size):
-        return users.at[pl.ds(core * nz, nz), :, first : first + size]
-
-    all_relays = copy(line_of(c, 0, D), line_of(other, 0, D), relay_sem.at[0], relay_sem.at[1], sibling)
+    all_relays = copy(
+        users.at[pl.ds(c * nz, nz)], users.at[pl.ds(other * nz, nz)], relay_sem.at[0], relay_sem.at[1], sibling
+    )
     all_relays.wait_recv()
-    forward_hop(1, 3)
 
     index = user_ref[...]
     source = (index % slots) // 2
     place = (source % CORES) * side + (source // CORES) * slots + index // slots * 2 + index % 2
-    table = dot_t(users[:, :, 0:D].reshape(2 * side, D), items[...])
+    table = dot_t(users[:, :, 0:D].reshape(2 * side, D), items[...]) + dot_t(
+        users[:, :, D : D + WIDTH].reshape(2 * side, WIDTH), item_w
+    )
     imps = index.shape[1]
     picked = lax.broadcasted_iota(jnp.int32, (2 * side, imps), 0) == place
     logits = jnp.sum(jnp.where(picked, table, 0.0), 0, keepdims=True)
     logit_ref[...] = logits
     logit_out = pltpu.make_async_copy(logit_ref, logit_hbm, out_sem.at[0])
     logit_out.start()
-    forward_hop(2, 3)
     error = sigmoid(logits) - label_ref[...].astype(jnp.float32)
 
     line = lax.broadcasted_iota(jnp.int32, (side, imps), 0)
@@ -285,19 +257,13 @@
     pool_copy = copy(pool_send, pool_core, pool_sem.at[0], pool_sem.at[1], sibling)
     pool_copy.start()
     pool_mine[...] = pool_side(c)
-    forward_hop(reach - 1, 3)
-    py_relay = copy(
-        line_of(c, D, WIDTH), line_of(c, D, WIDTH), relay_sem.at[2], relay_sem.at[3], sibling
-    )
-    py_relay.start()
+    turned = users[:, :, D : D + WIDTH].reshape(2 * side, WIDTH).astype(jnp.float32).T.astype(jnp.bfloat16)
     pool_copy.wait()
     pool_z[...] = (pool_mine[...] + pool_core[...].astype(jnp.float32)).astype(jnp.bfloat16)
     for k in range(1, nz):
         copy(pool_z.at[(z + k) % nz], pool_got.at[z], pool_sem.at[2], pool_sem.at[3], z_id(k)).start()
     pool_got[z] = pool_z[z]
 
-    copy(line_of(c, D, WIDTH), line_of(other, D, WIDTH), relay_sem.at[2], relay_sem.at[3], sibling).wait_recv()
-    turned = users[:, :, D : D + WIDTH].reshape(2 * side, WIDTH).astype(jnp.float32).T.astype(jnp.bfloat16)
     chosen = dot(turned, picked.astype(jnp.bfloat16))
     chosen = (chosen * error).astype(jnp.bfloat16)
 
@@ -452,7 +418,6 @@
     spot = users.at[pl.ds(0, nz - 1)]
     copy(spot, spot, user_send, user_recv.at[0], sibling).wait_send()
     all_relays.wait_send()
-    py_relay.wait_send()
     pool_all.wait_send()
     for n in range(3):
         plane_all(n).wait_send()

time: 99.3 us -> 91.8 us (0.924)
  Pallas kernels: 98.4 us -> 90.9 us
    pallas_call x1, Pallas kernels: 95.5 us -> 87.9 us  [train_step(): pl.pallas_call(functools.partial(step_kernel, nz, nr), in_specs=[hbm] * 8...]
where the time goes in v9:
time: 91.8 us; the launch traced here: 91.7 us
  Pallas kernels  90.9 us (99%)
    pallas_call x1, Pallas kernels, train_step(): pl.pallas_call(functools.partial(step_kernel, nz, nr), in_specs=[hbm] * 8...  87.9 us
    pallas_call x1, Pallas kernels, finish(): pl.pallas_call(finish_kernel, in_specs=[hbm] * 3, out_specs=[hbm] * 3, ou...  2.91 us

profile of v9, /device:TPU:1, one launch (start us, length us, event | category | flops | bytes accessed | tf_op | source)
XLA Modules:
  0.0 91.7 jit_solution(18037865557264893590)
XLA Ops:
  0.6 87.9 %train_step.1 = (f32[1,256]{1,0:T(1,128)}, bf16[512,1024]{1,0:T(8,128)(2,1)}, bf16[512,1024]{1,0:T(8,128)(2,1)}) custom-call(s32[1,256]{1,0:T(1,128)} %bitcast.5, s32[1,256]{1,0:T(1,128)} %bitcast.6, s32[32]{0:T(128)} %lengths_hbm.1, s32[16]{0:T(128)} %counts_hbm.1, bf16[256,1024]{1,0:T(8,128)(2,1)} %items_hbm.1, bf16[512,1024]{1,0:T(8,128)(2,1)} %w_out_hbm.1, ...), custom_call_target="tpu_custom_call" | custom-call | tf_op jit(solution)/shard_map/train_step/pallas_call | solution.py:457
  88.6 2.9 %finish.1 = (f32[1,256]{1,0:T(1,128)}, bf16[512,1024]{1,0:T(8,128)(2,1)}, bf16[1024,512]{1,0:T(8,128)(2,1)}) custom-call(f32[1,256]{1,0:T(1,128)} %get-tuple-element.9.logit_in, bf16[512,1024]{1,0:T(8,128)(2,1)} %get-tuple-element.10.out_in, bf16[512,1024]{1,0:T(8,128)(2,1)} %get-tuple-element.11.gate_in), custom_call_target="tpu_custom_call" | custom-call | tf_op jit(solution)/shard_map/finish/pallas_call | solution.py:545

commit v10 on v9

--- a/solution.py
+++ b/solution.py
@@ -16,7 +16,7 @@
 STEP = 512
 CORES = 2
 LANES = 128
-PARTS = 4
+PARTS = 2
 MESH = pl.DeviceIdType.MESH
 
 EPS_NORM = 1e-06
@@ -45,7 +45,7 @@
     sums = [rest[n * per_sum : (n + 1) * per_sum] for n in range(3)]
     (
         lengths, counts, load_sem, h_sem, w_sem, out_sem,
-        user_send, user_recv, relay_sem, pool_sem, sum_send, sum_recv,
+        user_send, user_recv, py_send, py_recv, relay_sem, pool_sem, sum_send, sum_recv,
     ) = rest[3 * per_sum :]
     own = lax.axis_index("own")
     rep = lax.axis_index("rep")
@@ -111,7 +111,7 @@
 
     at = c * nz + z
     reach = nz // 2
-    width = (D + WIDTH) // PARTS
+    width = D // PARTS
     ends = (z_id(1), z_id(nz - 1))
 
     def origin(way, step):
@@ -128,9 +128,35 @@
     def goes(way, step, part):
         return step < reach - 1 or part % 2 == way
 
-    def user_relay(zz):
-        spot = users.at[c * nz + zz]
-        return copy(spot, spot, relay_sem.at[0], relay_sem.at[1], sibling)
+    def pass_on(step):
+        for piece in range(PARTS):
+            for way in range(2):
+                if goes(way, step, piece):
+                    landed(way, step, piece)
+                if step + 1 < reach and goes(way, step + 1, piece):
+                    hop(way, step + 1, piece).start()
+        user_relay(origin(0, step + 1), 0).start()
+        if step + 1 < reach:
+            user_relay(origin(1, step + 1), 0).start()
+
+    def user_relay(zz, k):
+        spot = users.at[c * nz + zz, :, D * k : D + WIDTH * k]
+        return copy(spot, spot, relay_sem.at[2 * k], relay_sem.at[2 * k + 1], sibling)
+
+    def all_relays(k):
+        cols = slice(D * k, D + WIDTH * k)
+        return copy(
+            users.at[pl.ds(c * nz, nz), :, cols], users.at[pl.ds(other * nz, nz), :, cols],
+            relay_sem.at[2 * k], relay_sem.at[2 * k + 1], sibling,
+        )
+
+    def direct(k):
+        spot = users.at[at, :, D : D + WIDTH]
+        return copy(spot, spot, py_send, py_recv.at[z], z_id(k))
+
+    def direct_landed(zz):
+        spot = users.at[c * nz + zz, :, D : D + WIDTH]
+        copy(spot, spot, py_send, py_recv.at[zz], sibling).wait_recv()
 
     def project(i, n):
         linear[i % 2][:, part(n)] = dot(x[block_rows(i), :], w[:, part(n)])
@@ -199,46 +225,46 @@
         project(0, n)
     for load in loads[:3]:
         load.wait()
-    pooled = []
     for i in range(blocks):
-        if i + 1 < blocks:
-            h_loads[i + 1].wait()
+        if i == 0:
+            for load in h_loads[1:]:
+                load.wait()
         for k in range(step_bins):
             if i + 1 < blocks:
                 project(i + 1, k)
             one_bin(i, k)
-        pooled.append(pool_x(i))
-    users[at, :, 0:D] = jnp.concatenate(pooled, 0).astype(jnp.bfloat16)
+            if k == step_bins // 2 - 1 and i >= 2:
+                pass_on(2 * i - 3)
+        if i == 0:
+            px = jnp.concatenate([pool_x(j) for j in range(blocks)], 0)
+            users[at, :, 0:D] = px.astype(jnp.bfloat16)
+            pl.semaphore_wait(barrier, nz - 1 + nr - 1 + 1)
+            for piece in range(PARTS):
+                for way in range(2):
+                    hop(way, 0, piece).start()
+            user_relay(z, 0).start()
+        elif i < blocks - 1:
+            pass_on(2 * i - 2)
     users[at, :, D : D + WIDTH] = sum_y[...].astype(jnp.bfloat16)
-    pl.semaphore_wait(barrier, nz - 1 + nr - 1 + 1)
-    for piece in range(PARTS):
-        for way in range(2):
-            hop(way, 0, piece).start()
-    user_relay(z).start()
+    order = [k for near in range(1, reach) for k in (near, nz - near)] + [reach]
+    for k in order:
+        direct(k).start()
+    user_relay(z, 1).start()
     for load in loads[3:]:
         load.wait()
     item_w = dot_t(items[...], w_out[...]).astype(jnp.bfloat16)
-    for step in range(reach):
-        for piece in range(PARTS):
-            for way in range(2):
-                if goes(way, step, piece):
-                    landed(way, step, piece)
-                if step + 1 < reach and goes(way, step + 1, piece):
-                    hop(way, step + 1, piece).start()
-        user_relay(origin(0, step + 1)).start()
-        if step + 1 < reach:
-            user_relay(origin(1, step + 1)).start()
-    all_relays = copy(
-        users.at[pl.ds(c * nz, nz)], users.at[pl.ds(other * nz, nz)], relay_sem.at[0], relay_sem.at[1], sibling
-    )
-    all_relays.wait_recv()
+    all_relays(0).wait_recv()
+    table_x = dot_t(users[:, :, 0:D].reshape(2 * side, D), items[...])
+    for k in order:
+        zz = (z + k) % nz
+        direct_landed(zz)
+        user_relay(zz, 1).start()
+    all_relays(1).wait_recv()
 
     index = user_ref[...]
     source = (index % slots) // 2
     place = (source % CORES) * side + (source // CORES) * slots + index // slots * 2 + index % 2
-    table = dot_t(users[:, :, 0:D].reshape(2 * side, D), items[...]) + dot_t(
-        users[:, :, D : D + WIDTH].reshape(2 * side, WIDTH), item_w
-    )
+    table = table_x + dot_t(users[:, :, D : D + WIDTH].reshape(2 * side, WIDTH), item_w)
     imps = index.shape[1]
     picked = lax.broadcasted_iota(jnp.int32, (2 * side, imps), 0) == place
     logits = jnp.sum(jnp.where(picked, table, 0.0), 0, keepdims=True)
@@ -415,9 +441,12 @@
         last_copy(n, other).wait()
         for strip in strips(n):
             strip.start()
-    spot = users.at[pl.ds(0, nz - 1)]
+    spot = users.at[pl.ds(0, nz - 1), :, 0:D]
     copy(spot, spot, user_send, user_recv.at[0], sibling).wait_send()
-    all_relays.wait_send()
+    spot = users.at[pl.ds(0, nz - 1), :, D : D + WIDTH]
+    copy(spot, spot, py_send, py_recv.at[0], sibling).wait_send()
+    for k in range(2):
+        all_relays(k).wait_send()
     pool_all.wait_send()
     for n in range(3):
         plane_all(n).wait_send()
@@ -488,7 +517,7 @@
             pltpu.SMEM(lengths.shape, jnp.int32),
             pltpu.SMEM(counts.shape, jnp.int32),
             dma((6,)), dma((blocks,)), dma((4,)), dma((1 + 3 * CORES,)),
-            dma(()), dma((nz * PARTS,)), dma((4,)), dma((4,)),
+            dma(()), dma((nz * PARTS,)), dma(()), dma((nz,)), dma((4,)), dma((4,)),
             dma((3, 6)), dma((3, 6)),
         ],
         compiler_params=pltpu.CompilerParams(

time: 91.8 us -> 88.9 us (0.968)
  Pallas kernels: 90.9 us -> 88 us
    pallas_call x1, Pallas kernels: 87.9 us -> 85.1 us  [train_step(): pl.pallas_call(functools.partial(step_kernel, nz, nr), in_specs=[hbm] * 8...]
where the time goes in v10:
time: 88.9 us; the launch traced here: 88.8 us
  Pallas kernels  88 us (99%)
    pallas_call x1, Pallas kernels, train_step(): pl.pallas_call(functools.partial(step_kernel, nz, nr), in_specs=[hbm] * 8...  85.1 us
    pallas_call x1, Pallas kernels, finish(): pl.pallas_call(finish_kernel, in_specs=[hbm] * 3, out_specs=[hbm] * 3, ou...  2.91 us

profile of v10, /device:TPU:1, one launch (start us, length us, event | category | flops | bytes accessed | tf_op | source)
XLA Modules:
  0.0 88.8 jit_solution(2617524882016754402)
XLA Ops:
  0.6 85.1 %train_step.1 = (f32[1,256]{1,0:T(1,128)}, bf16[512,1024]{1,0:T(8,128)(2,1)}, bf16[512,1024]{1,0:T(8,128)(2,1)}) custom-call(s32[1,256]{1,0:T(1,128)} %bitcast.5, s32[1,256]{1,0:T(1,128)} %bitcast.6, s32[32]{0:T(128)} %lengths_hbm.1, s32[16]{0:T(128)} %counts_hbm.1, bf16[256,1024]{1,0:T(8,128)(2,1)} %items_hbm.1, bf16[512,1024]{1,0:T(8,128)(2,1)} %w_out_hbm.1, ...), custom_call_target="tpu_custom_call" | custom-call | tf_op jit(solution)/shard_map/train_step/pallas_call | solution.py:486
  85.7 2.9 %finish.1 = (f32[1,256]{1,0:T(1,128)}, bf16[512,1024]{1,0:T(8,128)(2,1)}, bf16[1024,512]{1,0:T(8,128)(2,1)}) custom-call(f32[1,256]{1,0:T(1,128)} %get-tuple-element.9.logit_in, bf16[512,1024]{1,0:T(8,128)(2,1)} %get-tuple-element.10.out_in, bf16[512,1024]{1,0:T(8,128)(2,1)} %get-tuple-element.11.gate_in), custom_call_target="tpu_custom_call" | custom-call | tf_op jit(solution)/shard_map/finish/pallas_call | solution.py:574

commit v11 on v10

--- a/solution.py
+++ b/solution.py
@@ -150,13 +150,20 @@
             relay_sem.at[2 * k], relay_sem.at[2 * k + 1], sibling,
         )
 
-    def direct(k):
-        spot = users.at[at, :, D : D + WIDTH]
-        return copy(spot, spot, py_send, py_recv.at[z], z_id(k))
+    order = [k for near in range(1, reach) for k in (near, nz - near)] + [reach]
+    some = slots // 2
+
+    def direct(g):
+        rows = slice(g * some, (g + 1) * some)
+        users[at, rows, D : D + WIDTH] = sum_y[rows, :].astype(jnp.bfloat16)
+        spot = users.at[at, rows, D : D + WIDTH]
+        for k in order:
+            copy(spot, spot, py_send, py_recv.at[g * nz + z], z_id(k)).start()
 
     def direct_landed(zz):
-        spot = users.at[c * nz + zz, :, D : D + WIDTH]
-        copy(spot, spot, py_send, py_recv.at[zz], sibling).wait_recv()
+        for g in range(2):
+            spot = users.at[c * nz + zz, g * some : (g + 1) * some, D : D + WIDTH]
+            copy(spot, spot, py_send, py_recv.at[g * nz + zz], sibling).wait_recv()
 
     def project(i, n):
         linear[i % 2][:, part(n)] = dot(x[block_rows(i), :], w[:, part(n)])
@@ -245,10 +252,9 @@
             user_relay(z, 0).start()
         elif i < blocks - 1:
             pass_on(2 * i - 2)
-    users[at, :, D : D + WIDTH] = sum_y[...].astype(jnp.bfloat16)
-    order = [k for near in range(1, reach) for k in (near, nz - near)] + [reach]
-    for k in order:
-        direct(k).start()
+        if i == blocks // 2 - 1:
+            direct(0)
+    direct(1)
     user_relay(z, 1).start()
     for load in loads[3:]:
         load.wait()
@@ -517,7 +523,7 @@
             pltpu.SMEM(lengths.shape, jnp.int32),
             pltpu.SMEM(counts.shape, jnp.int32),
             dma((6,)), dma((blocks,)), dma((4,)), dma((1 + 3 * CORES,)),
-            dma(()), dma((nz * PARTS,)), dma(()), dma((nz,)), dma((4,)), dma((4,)),
+            dma(()), dma((nz * PARTS,)), dma(()), dma((2 * nz,)), dma((4,)), dma((4,)),
             dma((3, 6)), dma((3, 6)),
         ],
         compiler_params=pltpu.CompilerParams(

time: 88.9 us -> 87.9 us (0.989)
  Pallas kernels: 88 us -> 87 us
    pallas_call x1, Pallas kernels: 85.1 us -> 84.1 us  [train_step(): pl.pallas_call(functools.partial(step_kernel, nz, nr), in_specs=[hbm] * 8...]
where the time goes in v11:
time: 87.9 us; the launch traced here: 87.8 us
  Pallas kernels  87 us (99%)
    pallas_call x1, Pallas kernels, train_step(): pl.pallas_call(functools.partial(step_kernel, nz, nr), in_specs=[hbm] * 8...  84.1 us
    pallas_call x1, Pallas kernels, finish(): pl.pallas_call(finish_kernel, in_specs=[hbm] * 3, out_specs=[hbm] * 3, ou...  2.91 us

profile of v11, /device:TPU:1, one launch (start us, length us, event | category | flops | bytes accessed | tf_op | source)
XLA Modules:
  0.0 87.8 jit_solution(18188997498608801314)
XLA Ops:
  0.6 84.1 %train_step.1 = (f32[1,256]{1,0:T(1,128)}, bf16[512,1024]{1,0:T(8,128)(2,1)}, bf16[512,1024]{1,0:T(8,128)(2,1)}) custom-call(s32[1,256]{1,0:T(1,128)} %bitcast.5, s32[1,256]{1,0:T(1,128)} %bitcast.6, s32[32]{0:T(128)} %lengths_hbm.1, s32[16]{0:T(128)} %counts_hbm.1, bf16[256,1024]{1,0:T(8,128)(2,1)} %items_hbm.1, bf16[512,1024]{1,0:T(8,128)(2,1)} %w_out_hbm.1, ...), custom_call_target="tpu_custom_call" | custom-call | tf_op jit(solution)/shard_map/train_step/pallas_call | solution.py:492
  84.7 2.9 %finish.1 = (f32[1,256]{1,0:T(1,128)}, bf16[512,1024]{1,0:T(8,128)(2,1)}, bf16[1024,512]{1,0:T(8,128)(2,1)}) custom-call(f32[1,256]{1,0:T(1,128)} %get-tuple-element.9.logit_in, bf16[512,1024]{1,0:T(8,128)(2,1)} %get-tuple-element.10.out_in, bf16[512,1024]{1,0:T(8,128)(2,1)} %get-tuple-element.11.gate_in), custom_call_target="tpu_custom_call" | custom-call | tf_op jit(solution)/shard_map/finish/pallas_call | solution.py:580

commit v12 on v11

--- a/solution.py
+++ b/solution.py
@@ -421,8 +421,8 @@
     core_end(2)
     piece_end(0)
     plane_end(1)
+    plane_end(2)
     back_end(0)
-    plane_end(2)
     piece_end(1)
     piece_end(2)
     back_end(1)

time: 87.9 us -> 87.8 us (level)
  no operation moved by 1% of the time
where the time goes in v12:
time: 87.8 us; the launch traced here: 87.7 us
  Pallas kernels  86.9 us (99%)
    pallas_call x1, Pallas kernels, train_step(): pl.pallas_call(functools.partial(step_kernel, nz, nr), in_specs=[hbm] * 8...  84 us
    pallas_call x1, Pallas kernels, finish(): pl.pallas_call(finish_kernel, in_specs=[hbm] * 3, out_specs=[hbm] * 3, ou...  2.91 us

profile of v12, /device:TPU:1, one launch (start us, length us, event | category | flops | bytes accessed | tf_op | source)
XLA Modules:
  0.0 87.7 jit_solution(10735640295577423139)
XLA Ops:
  0.6 84.0 %train_step.1 = (f32[1,256]{1,0:T(1,128)}, bf16[512,1024]{1,0:T(8,128)(2,1)}, bf16[512,1024]{1,0:T(8,128)(2,1)}) custom-call(s32[1,256]{1,0:T(1,128)} %bitcast.5, s32[1,256]{1,0:T(1,128)} %bitcast.6, s32[32]{0:T(128)} %lengths_hbm.1, s32[16]{0:T(128)} %counts_hbm.1, bf16[256,1024]{1,0:T(8,128)(2,1)} %items_hbm.1, bf16[512,1024]{1,0:T(8,128)(2,1)} %w_out_hbm.1, ...), custom_call_target="tpu_custom_call" | custom-call | tf_op jit(solution)/shard_map/train_step/pallas_call | solution.py:492
  84.6 2.9 %finish.1 = (f32[1,256]{1,0:T(1,128)}, bf16[512,1024]{1,0:T(8,128)(2,1)}, bf16[1024,512]{1,0:T(8,128)(2,1)}) custom-call(f32[1,256]{1,0:T(1,128)} %get-tuple-element.9.logit_in, bf16[512,1024]{1,0:T(8,128)(2,1)} %get-tuple-element.10.out_in, bf16[512,1024]{1,0:T(8,128)(2,1)} %get-tuple-element.11.gate_in), custom_call_target="tpu_custom_call" | custom-call | tf_op jit(solution)/shard_map/finish/pallas_call | solution.py:580
